TPU v7x, 256 devices: a whole 4x4x8 slice. The times are simulated.
256 devices in a mesh: grp: 8 (over x, core), seq: 32 (over y, z).
Axes of the slice: x: 4, y: 4, z: 8, core: 2. Of those that a mesh axis runs over, the one named last changes fastest.
Arguments:
- features: bfloat16 [65536, 2048], P(('grp', 'seq')), may hold values from -6 to 6
- gate_input: bfloat16 [65536, 2048], P(('grp', 'seq')), may hold values from -6 to 6
- b_forward: bfloat16 [65536, 128], P(('grp', 'seq')), may hold values from -6 to 6
- c_forward: bfloat16 [65536, 128], P(('grp', 'seq')), may hold values from -6 to 6
- b_backward: bfloat16 [65536, 128], P(('grp', 'seq')), may hold values from -6 to 6
- c_backward: bfloat16 [65536, 128], P(('grp', 'seq')), may hold values from -6 to 6
- rate_forward: float32 [32, 65536], P(None, ('grp', 'seq')), may hold values from 3.0517578e-07 to 0.8, as said below
- rate_backward: float32 [32, 65536], P(None, ('grp', 'seq')), may hold values from 3.0517578e-07 to 0.8, as said below
- norm_gain: float32 [2048], replicated, may hold values from 0.5 to 1.5
- out_weight: bfloat16 [2048, 1024], replicated, may hold values from -0.125 to 0.125
Outputs:
- mixed: bfloat16 [65536, 1024], P(('grp', 'seq'))
Inputs may be any that keep to these rules, and one draw needn't show every extreme that they name: `rate_forward`: positive decay rates; one token keeps exp(-rate) of a head's state. `rate_backward`: positive decay rates; one token keeps exp(-rate) of a head's state.
All inputs are finite; a program needn't handle non-finite values.
Results may differ from a plain program's by a relative error of at most 0.019.
Values may be sent and summed in bfloat16 or wider, within the bound.
No kernel may reach another device: no remote copies, remote signals or barrier semaphores. Data moves between devices by JAX's collectives and lax.ppermute only.
A program may use at most 64 MiB of HBM per device.

v0:
```python
import functools
import jax
import jax.numpy as jnp
from jax import lax
from jax.experimental import pallas as pl
from jax.experimental.pallas import tpu as pltpu
from jax.sharding import PartitionSpec as P

Q = 256
H = 32
HEAD = 64
N = 128
E = 2048
D = 1024
BLK = 256
STEPS = E // BLK
HPB = BLK // HEAD
ROWS = N + 16
LOG2E = 1.4426950408889634
F32 = jnp.float32
BF16 = jnp.bfloat16


def lane_sums(r):
    width = r.shape[1]
    lane = lax.broadcasted_iota(jnp.int32, r.shape, 1)
    shift = 1
    while shift < width:
        r = r + jnp.where(lane >= shift, pltpu.roll(r, shift, 1), 0.0)
        shift *= 2
    return r


def lane_sums_back(r):
    width = r.shape[1]
    lane = lax.broadcasted_iota(jnp.int32, r.shape, 1)
    shift = 1
    while shift < width:
        r = r + jnp.where(lane < width - shift, pltpu.roll(r, width - shift, 1), 0.0)
        shift *= 2
    return r


def step_of(r):
    y = 2.0 * r
    s = jnp.full_like(y, 1.0)
    for k in range(9, 1, -1):
        s = 1.0 - y * (1.0 / k) * s
    return jnp.sqrt(jnp.where(y < 0.5, y * s, 1.0 - jnp.exp(-y)))


def two_parts(a):
    high = a.astype(BF16).astype(F32)
    return high, a - high


def head_select(block, rows, width, first, pairs):
    row = lax.broadcasted_iota(jnp.int32, (rows, width), 0)
    column = lax.broadcasted_iota(jnp.int32, (rows, width), 1)
    head = block * HPB + column // HEAD
    hit = (row % H == head) & (row >= first) & (row < first + pairs * H)
    return jnp.where(hit, 1.0, 0.0).astype(BF16)


def dot(a, b):
    return jnp.dot(a, b, preferred_element_type=F32)


def state_kernel(x_ref, rf_ref, rb_ref, bf_ref, bb_ref, out_ref, scale_ref, bt_ref, keep_ref):
    j = pl.program_id(0)

    @pl.when(j == 0)
    def _():
        parts = []
        for d, (r_ref, sums) in enumerate(((rf_ref, lane_sums), (rb_ref, lane_sums_back))):
            r = r_ref[...]
            c = sums(r)
            total = c[:, Q - 1 : Q] if d == 0 else c[:, 0:1]
            parts += two_parts(step_of(r) * jnp.exp(c - total))
            keep_ref[d] = jnp.broadcast_to(jnp.exp(-total), (H, 128))
        scale_ref[...] = jnp.concatenate(parts, axis=0).T.astype(BF16)
        bt_ref[0] = bf_ref[...].astype(F32).T.astype(BF16)
        bt_ref[1] = bb_ref[...].astype(F32).T.astype(BF16)

    x = x_ref[...].astype(F32)
    for d in range(2):
        factor = dot(scale_ref[...], head_select(j, 4 * H, BLK, 2 * H * d, 2))
        v = (x * factor).astype(BF16)
        s = dot(bt_ref[d], v).astype(BF16)
        head = lax.broadcasted_iota(jnp.int32, (H, BLK), 0)
        column = lax.broadcasted_iota(jnp.int32, (H, BLK), 1)
        keep = jnp.concatenate([keep_ref[d]] * (BLK // 128), axis=1)
        keep = jnp.sum(
            jnp.where(head == j * HPB + column // HEAD, keep, 0.0), axis=0, keepdims=True
        )
        high, rest = two_parts(keep)
        middle, low = two_parts(rest)
        row = lax.broadcasted_iota(jnp.int32, (16, BLK), 0)
        tail = jnp.where(row == 0, high, jnp.where(row == 1, middle, jnp.where(row == 2, low, 0.0)))
        tail = tail.astype(BF16)
        for k in range(BLK // 128):
            out_ref[d, k, 0:N, :] = s[:, 128 * k : 128 * (k + 1)]
            out_ref[d, k, N:ROWS, :] = tail[:, 128 * k : 128 * (k + 1)]


def state_call(x, rate_f, rate_b, b_f, b_b):
    whole = lambda shape: pl.BlockSpec(shape, lambda j: (0,) * len(shape))
    return pl.pallas_call(
        state_kernel,
        grid=(STEPS,),
        in_specs=[
            pl.BlockSpec((Q, BLK), lambda j: (0, j)),
            whole((H, Q)),
            whole((H, Q)),
            whole((Q, N)),
            whole((Q, N)),
        ],
        out_specs=pl.BlockSpec((2, BLK // 128, ROWS, 128), lambda j: (0, j, 0, 0)),
        out_shape=jax.ShapeDtypeStruct((2, E // 128, ROWS, 128), BF16),
        scratch_shapes=[
            pltpu.VMEM((Q, 4 * H), BF16),
            pltpu.VMEM((2, N, Q), BF16),
            pltpu.VMEM((2, H, 128), F32),
        ],
        name="span_states",
    )(x, rate_f, rate_b, b_f, b_b)


def inside_kernel(
    x_ref, gate_ref, rf_ref, rb_ref, bf_ref, cf_ref, bb_ref, cb_ref,
    out_ref, silu_ref, score_ref, rows_ref, cols_ref,
):
    j = pl.program_id(0)
    t = lax.broadcasted_iota(jnp.int32, (Q, Q), 0)
    s = lax.broadcasted_iota(jnp.int32, (Q, Q), 1)

    @pl.when(j == 0)
    def _():
        contract = (((1,), (1,)), ((), ()))
        forward = lax.dot_general(cf_ref[...], bf_ref[...], contract, preferred_element_type=F32)
        backward = lax.dot_general(cb_ref[...], bb_ref[...], contract, preferred_element_type=F32)
        score_ref[...] = jnp.where(s <= t, forward, backward)
        own = jnp.sum(jnp.where(s == t, backward, 0.0), axis=0, keepdims=True)
        c_f = lane_sums(rf_ref[...]) * LOG2E
        c_b = lane_sums_back(rb_ref[...]) * LOG2E
        step_f = step_of(rf_ref[...])
        step_b = step_of(rb_ref[...])
        rows_ref[0] = c_f + jnp.log(step_f) * LOG2E
        rows_ref[1] = c_b + jnp.log(step_b) * LOG2E
        high, low = two_parts(own * step_b)
        cols_ref[...] = jnp.concatenate([c_f, c_b, high, low], axis=0).T

    gate = gate_ref[...].astype(F32)
    silu_ref[...] = (gate * jax.nn.sigmoid(gate)).astype(BF16)
    cols = cols_ref[...]
    own = dot(cols.astype(BF16), head_select(j, 4 * H, BLK, 2 * H, 2))
    cols = pltpu.roll(cols, lax.rem(4 * H - HPB * j, 4 * H), 1)
    lane = lax.broadcasted_iota(jnp.int32, (Q, 128), 1)
    for p in range(HPB // 2):
        x = x_ref[:, 128 * p : 128 * (p + 1)]
        halves = []
        for i in (2 * p, 2 * p + 1):
            forward = rows_ref[0, pl.ds(HPB * j + i, 1), :] - cols[:, i : i + 1]
            backward = rows_ref[1, pl.ds(HPB * j + i, 1), :] - cols[:, H + i : H + i + 1]
            w = score_ref[...] * jnp.exp2(jnp.where(s <= t, forward, backward))
            halves.append(dot(w.astype(BF16), x))
        y = jnp.where(lane < HEAD, halves[0], halves[1])
        y = y + own[:, 128 * p : 128 * (p + 1)] * x.astype(F32)
        out_ref[:, 128 * p : 128 * (p + 1)] = y.astype(BF16)


def inside_call(x, gate, rate_f, rate_b, b_f, c_f, b_b, c_b):
    whole = lambda shape: pl.BlockSpec(shape, lambda j: (0,) * len(shape))
    columns = pl.BlockSpec((Q, BLK), lambda j: (0, j))
    return pl.pallas_call(
        inside_kernel,
        grid=(STEPS,),
        in_specs=[columns, columns, whole((H, Q)), whole((H, Q))] + [whole((Q, N))] * 4,
        out_specs=[columns, columns],
        out_shape=[jax.ShapeDtypeStruct((Q, E), BF16)] * 2,
        scratch_shapes=[
            pltpu.VMEM((Q, Q), F32),
            pltpu.VMEM((2, H, Q), F32),
            pltpu.VMEM((Q, 4 * H), F32),
        ],
        cost_estimate=pl.CostEstimate(
            flops=2 * H * Q * Q * 128, bytes_accessed=4 * Q * E * 2, transcendentals=H * Q * Q
        ),
        name="inside_spans",
    )(x, gate, rate_f, rate_b, b_f, c_f, b_b, c_b)


def read_part(ref, index):
    state = ref[index, 0:N, :].astype(F32)
    tail = ref[index, N:ROWS, :].astype(F32)
    return state, tail[0:1] + tail[1:2] + tail[2:3]


def total_kernel(count, copies, place_ref, parts_ref, out_ref):
    backward = place_ref[0]

    def step(i, carried):
        state, kept = carried
        index = jnp.where(backward == 1, count - 1 - i, i)
        own, keep = read_part(parts_ref, index)
        return keep * state + own, keep * kept

    state, kept = lax.fori_loop(
        0, count, step, (jnp.zeros((N, 128), F32), jnp.ones((1, 128), F32)), unroll=4
    )
    high, rest = two_parts(kept)
    middle, low = two_parts(rest)
    row = lax.broadcasted_iota(jnp.int32, (16, 128), 0)
    tail = jnp.where(row == 0, high, jnp.where(row == 1, middle, jnp.where(row == 2, low, 0.0)))
    for g in range(copies):
        out_ref[g, 0:N, :] = state.astype(BF16)
        out_ref[g, N:ROWS, :] = tail.astype(BF16)


def entry_kernel(count, groups, place_ref, totals_ref, parts_ref, out_ref):
    backward, mine = place_ref[0], place_ref[1]

    def outer(i, state):
        index = jnp.where(backward == 1, groups - 1 - i, i)
        own, keep = read_part(totals_ref, index)
        return keep * state + own

    state = lax.fori_loop(0, mine, outer, jnp.zeros((N, 128), F32))

    def step(i, state):
        index = jnp.where(backward == 1, count - 1 - i, i)
        out_ref[index] = state.astype(BF16)
        own, keep = read_part(parts_ref, index)
        return keep * state + own

    lax.fori_loop(0, count, step, state, unroll=4)


def vmem_specs(n):
    return [pl.BlockSpec(memory_space=pltpu.SMEM)] + [pl.BlockSpec(memory_space=pltpu.VMEM)] * n


def final_kernel(
    in_ref, silu_ref, m_ref, rf_ref, rb_ref, cf_ref, cb_ref, gain_ref, w_ref,
    out_ref, scale_ref, acc_ref, square_ref,
):
    j = pl.program_id(0)

    @pl.when(j == 0)
    def _():
        parts = two_parts(jnp.exp(-lane_sums(rf_ref[...])))
        parts += two_parts(jnp.exp(-lane_sums_back(rb_ref[...])))
        scale_ref[...] = jnp.concatenate(parts, axis=0).T.astype(BF16)
        acc_ref[...] = jnp.zeros_like(acc_ref)
        square_ref[...] = jnp.zeros_like(square_ref)

    y = in_ref[...].astype(F32)
    for d, c_ref in enumerate((cf_ref, cb_ref)):
        factor = dot(scale_ref[...], head_select(j, 4 * H, BLK, 2 * H * d, 2))
        m = jnp.concatenate([m_ref[d, k] for k in range(BLK // 128)], axis=1)
        y = y + factor * dot(c_ref[...], m)
    gated = y * silu_ref[...].astype(F32)
    square = gated * gated
    square_ref[...] += square[:, :128] + square[:, 128:]
    acc_ref[...] += dot((gated * gain_ref[...]).astype(BF16), w_ref[...])

    @pl.when(j == STEPS - 1)
    def _():
        mean = jnp.sum(square_ref[...], axis=1, keepdims=True) * (1.0 / E)
        out_ref[...] = (acc_ref[...] * lax.rsqrt(mean + 1e-05)).astype(BF16)


def final_call(inside, silu, m, rate_f, rate_b, c_f, c_b, gain, weight):
    whole = lambda shape: pl.BlockSpec(shape, lambda j: (0,) * len(shape))
    columns = pl.BlockSpec((Q, BLK), lambda j: (0, j))
    return pl.pallas_call(
        final_kernel,
        grid=(STEPS,),
        in_specs=[
            columns,
            columns,
            pl.BlockSpec((2, BLK // 128, N, 128), lambda j: (0, j, 0, 0)),
            whole((H, Q)),
            whole((H, Q)),
            whole((Q, N)),
            whole((Q, N)),
            pl.BlockSpec((1, BLK), lambda j: (0, j)),
            pl.BlockSpec((BLK, D), lambda j: (j, 0)),
        ],
        out_specs=whole((Q, D)),
        out_shape=jax.ShapeDtypeStruct((Q, D), BF16),
        scratch_shapes=[
            pltpu.VMEM((Q, 4 * H), BF16),
            pltpu.VMEM((Q, D), F32),
            pltpu.VMEM((Q, 128), F32),
        ],
        name="gate_norm_project",
    )(inside, silu, m, rate_f, rate_b, c_f, c_b, gain, weight)


def per_device(
    features, gate_input, b_forward, c_forward, b_backward, c_backward,
    rate_forward, rate_backward, norm_gain, out_weight,
):
    count, groups = lax.axis_size("seq"), lax.axis_size("grp")
    states = state_call(features, rate_forward, rate_backward, b_forward, b_backward)
    states = states.reshape(count, ROWS, 128)
    backward = (lax.axis_index("seq") >= count // 2).astype(jnp.int32)
    group = lax.axis_index("grp")
    mine = jnp.where(backward == 1, groups - 1 - group, group)
    place = jnp.stack([backward, mine]).astype(jnp.int32)
    parts = lax.all_to_all(states, "seq", 0, 0, tiled=True)
    totals = pl.pallas_call(
        functools.partial(total_kernel, count, groups),
        in_specs=vmem_specs(1),
        out_specs=pl.BlockSpec(memory_space=pltpu.VMEM),
        out_shape=jax.ShapeDtypeStruct((groups, ROWS, 128), BF16),
        name="group_totals",
    )(place, parts)
    totals = lax.all_to_all(totals, "grp", 0, 0, tiled=True)
    entries = pl.pallas_call(
        functools.partial(entry_kernel, count, groups),
        in_specs=vmem_specs(2),
        out_specs=pl.BlockSpec(memory_space=pltpu.VMEM),
        out_shape=jax.ShapeDtypeStruct((count, N, 128), BF16),
        name="entry_states",
    )(place, totals, parts)
    m = lax.all_to_all(entries, "seq", 0, 0, tiled=True).reshape(2, E // 128, N, 128)
    inside, silu = inside_call(
        features, gate_input, rate_forward, rate_backward,
        b_forward, c_forward, b_backward, c_backward,
    )
    return final_call(
        inside, silu, m, rate_forward, rate_backward, c_forward, c_backward,
        norm_gain.reshape(1, E), out_weight,
    )


def solution(mesh):
    rows = P(("grp", "seq"), None)
    heads = P(None, ("grp", "seq"))
    placed = (rows,) * 6 + (heads, heads, P(), P())
    return jax.shard_map(per_device, mesh=mesh, in_specs=placed, out_specs=rows, check_vma=False)
```

profile of v0, /device:TPU:32, one launch (start us, length us, event | category | flops | bytes accessed | tf_op | source)
XLA Modules:
  0.0 113.5 jit_solution(13074563300855412485)
XLA Ops:
  0.0 8.2 %span_states.1 = bf16[2,16,144,128]{3,2,1,0:T(8,128)(2,1)} custom-call(bf16[256,2048]{1,0:T(8,128)(2,1)} %x_ref.3, f32[32,256]{1,0:T(8,128)} %rf_ref.5, f32[32,256]{1,0:T(8,128)} %rb_ref.5, bf16[256,128]{1,0:T(8,128)(2,1)} %bf_ref.3, bf16[256,128]{1,0:T(8,128)(2,1)} %bb_ref.3), custom_call_target="tpu_custom_call" | custom-call | tf_op jit(solution)/shard_map/span_states/pallas_call | solution.py:108
  8.2 11.4 %all-to-all-start = ((bf16[32,144,128]{2,1,0:T(8,128)(2,1)}), bf16[32,144,128]{2,1,0:T(8,128)(2,1)S(1)}, u32[]{:S(2)}, u32[]{:S(2)}) async-start(bf16[32,144,128]{2,1,0:T(8,128)(2,1)} %bitcast.5), calls=%async_computation | async-start | bytes 2359296 | tf_op jit(solution)/shard_map/all_to_all | solution.py:312
  19.6 0.6 pad_add_fusion.place_ref
  20.2 30.6 %all-to-all-done.parts_ref = bf16[32,144,128]{2,1,0:T(8,128)(2,1)S(1)} async-done(((bf16[32,144,128]{2,1,0:T(8,128)(2,1)}), bf16[32,144,128]{2,1,0:T(8,128)(2,1)S(1)}, u32[]{:S(2)}, u32[]{:S(2)}) %all-to-all-start) | async-done | bytes 1179680 | tf_op jit(solution)/shard_map/all_to_all | solution.py:312
  50.8 0.0 copy-start
  50.8 1.0 copy-done
  51.8 2.3 %group_totals.1 = bf16[8,144,128]{2,1,0:T(8,128)(2,1)} custom-call(s32[2]{0:T(128)} %pad_add_fusion.place_ref, bf16[32,144,128]{2,1,0:T(8,128)(2,1)} %copy-done), custom_call_target="tpu_custom_call" | custom-call | tf_op jit(solution)/shard_map/group_totals/pallas_call | solution.py:313
  54.2 12.3 %all_to_all.15.totals_ref = bf16[8,144,128]{2,1,0:T(8,128)(2,1)} all-to-all(bf16[8,144,128]{2,1,0:T(8,128)(2,1)} %group_totals.1), channel_id=1, replica_groups=mesh['grp'=8,'seq'=32] {'grp'}, dimensions={0} | all-to-all | bytes 589824 | tf_op jit(solution)/shard_map/all_to_all | solution.py:320
  66.5 2.7 %entry_states.1 = bf16[32,128,128]{2,1,0:T(8,128)(2,1)} custom-call(s32[2]{0:T(128)} %pad_add_fusion.place_ref, bf16[8,144,128]{2,1,0:T(8,128)(2,1)} %all_to_all.15.totals_ref, bf16[32,144,128]{2,1,0:T(8,128)(2,1)} %copy-done), custom_call_target="tpu_custom_call" | custom-call | tf_op jit(solution)/shard_map/entry_states/pallas_call | solution.py:321
  69.1 5.4 %all-to-all-start.2 = ((bf16[32,128,128]{2,1,0:T(8,128)(2,1)}), bf16[32,128,128]{2,1,0:T(8,128)(2,1)S(1)}, u32[]{:S(2)}, u32[]{:S(2)}) async-start(bf16[32,128,128]{2,1,0:T(8,128)(2,1)} %entry_states.1), calls=%async_computation.2 | async-start | bytes 2097152 | tf_op jit(solution)/shard_map/all_to_all | solution.py:328
  74.6 9.0 %inside_spans.1 = (bf16[256,2048]{1,0:T(8,128)(2,1)}, bf16[256,2048]{1,0:T(8,128)(2,1)}) custom-call(bf16[256,2048]{1,0:T(8,128)(2,1)} %x_ref.3, bf16[256,2048]{1,0:T(8,128)(2,1)} %gate_ref.1, f32[32,256]{1,0:T(8,128)} %rf_ref.5, f32[32,256]{1,0:T(8,128)} %rb_ref.5, bf16[256,128]{1,0:T(8,128)(2,1)} %bf_ref.3, bf16[256,128]{1,0:T(8,128)(2,1)} %cf_ref.3, ...), custom_call_target="tpu_custom_call" | custom-call | flops 536870912 | bytes 4194304 | tf_op jit(solution)/shard_map/inside_spans/pallas_call | solution.py:175
  83.6 19.6 %all-to-all-done.2 = bf16[32,128,128]{2,1,0:T(8,128)(2,1)S(1)} async-done(((bf16[32,128,128]{2,1,0:T(8,128)(2,1)}), bf16[32,128,128]{2,1,0:T(8,128)(2,1)S(1)}, u32[]{:S(2)}, u32[]{:S(2)}) %all-to-all-start.2) | async-done | bytes 1048608 | tf_op jit(solution)/shard_map/all_to_all | solution.py:328
  103.2 0.0 copy-start.1
  103.2 1.0 copy-done.1
  104.2 9.3 %gate_norm_project.1 = bf16[256,1024]{1,0:T(8,128)(2,1)} custom-call(bf16[256,2048]{1,0:T(8,128)(2,1)} %get-tuple-element.7.in_ref, bf16[256,2048]{1,0:T(8,128)(2,1)} %get-tuple-element.8.silu_ref, bf16[2,16,128,128]{3,2,1,0:T(8,128)(2,1)} %bitcast.6, f32[32,256]{1,0:T(8,128)} %rf_ref.5, f32[32,256]{1,0:T(8,128)} %rb_ref.5, bf16[256,128]{1,0:T(8,128)(2,1)} %cf_ref.3, ...), custom_call_target="tpu_custom_call" | custom-call | tf_op jit(solution)/shard_map/gate_norm_project/pallas_call | solution.py:276
Async XLA Ops:
  8.2 42.6 %all-to-all-start = ((bf16[32,144,128]{2,1,0:T(8,128)(2,1)}), bf16[32,144,128]{2,1,0:T(8,128)(2,1)S(1)}, u32[]{:S(2)}, u32[]{:S(2)}) async-start(bf16[32,144,128]{2,1,0:T(8,128)(2,1)} %bitcast.5), calls=%async_computation | async-start | bytes 2359296 | tf_op jit(solution)/shard_map/all_to_all | solution.py:312
  50.8 1.1 copy-start
  69.1 34.0 %all-to-all-start.2 = ((bf16[32,128,128]{2,1,0:T(8,128)(2,1)}), bf16[32,128,128]{2,1,0:T(8,128)(2,1)S(1)}, u32[]{:S(2)}, u32[]{:S(2)}) async-start(bf16[32,128,128]{2,1,0:T(8,128)(2,1)} %entry_states.1), calls=%async_computation.2 | async-start | bytes 2097152 | tf_op jit(solution)/shard_map/all_to_all | solution.py:328
  103.2 1.0 copy-start.1
where the time goes:
time: 114 us; the launch traced here: 113 us
  waiting for transfers between devices  50.2 us (44%)
  Pallas kernels  31.5 us (28%)
  starting transfers between devices  16.8 us (15%)
  blocking collectives  12.3 us (11%)
  local copies, waits for them, and re-layouts  2.02 us (2%)
    all_to_all x1, waiting for transfers between devices, per_device(): parts = lax.all_to_all(states, 'seq', 0, 0, tiled=True)  30.6 us
    all_to_all x1, waiting for transfers between devices, per_device(): lax.all_to_all(entries, 'seq', 0, 0, tiled=True)  19.6 us
    all_to_all x1, blocking collectives, per_device(): totals = lax.all_to_all(totals, 'grp', 0, 0, tiled=True)  12.3 us
    all_to_all x1, starting transfers between devices, per_device(): parts = lax.all_to_all(states, 'seq', 0, 0, tiled=True)  11.4 us
    pallas_call x1, Pallas kernels, final_call(): pl.pallas_call(final_kernel, grid=(STEPS,), in_specs=[columns, columns, p...  9.3 us
    pallas_call x1, Pallas kernels, inside_call(): pl.pallas_call(inside_kernel, grid=(STEPS,), in_specs=[columns, columns,...  9.02 us
    pallas_call x1, Pallas kernels, state_call(): pl.pallas_call(state_kernel, grid=(STEPS,), in_specs=[pl.BlockSpec((Q, BL...  8.23 us
    all_to_all x1, starting transfers between devices, per_device(): lax.all_to_all(entries, 'seq', 0, 0, tiled=True)  5.42 us
  transfers between devices with their start and end apart: 2, of which 2 were waited for; matrix products, arithmetic and copies ran while one was open for 1% of the time, Pallas kernels for 8%

commit v1 on v0

--- a/solution.py
+++ b/solution.py
@@ -14,11 +14,13 @@
 D = 1024
 BLK = 256
 STEPS = E // BLK
+FW = 256
 HPB = BLK // HEAD
 ROWS = N + 16
 LOG2E = 1.4426950408889634
 F32 = jnp.float32
 BF16 = jnp.bfloat16
+LIMIT = pltpu.CompilerParams(vmem_limit_bytes=24 * 1024 * 1024)
 
 
 def lane_sums(r):
@@ -57,7 +59,7 @@
 def head_select(block, rows, width, first, pairs):
     row = lax.broadcasted_iota(jnp.int32, (rows, width), 0)
     column = lax.broadcasted_iota(jnp.int32, (rows, width), 1)
-    head = block * HPB + column // HEAD
+    head = block * (width // HEAD) + column // HEAD
     hit = (row % H == head) & (row >= first) & (row < first + pairs * H)
     return jnp.where(hit, 1.0, 0.0).astype(BF16)
 
@@ -66,69 +68,75 @@
     return jnp.dot(a, b, preferred_element_type=F32)
 
 
-def state_kernel(x_ref, rf_ref, rb_ref, bf_ref, bb_ref, out_ref, scale_ref, bt_ref, keep_ref):
-    j = pl.program_id(0)
-
-    @pl.when(j == 0)
-    def _():
-        parts = []
-        for d, (r_ref, sums) in enumerate(((rf_ref, lane_sums), (rb_ref, lane_sums_back))):
-            r = r_ref[...]
-            c = sums(r)
-            total = c[:, Q - 1 : Q] if d == 0 else c[:, 0:1]
-            parts += two_parts(step_of(r) * jnp.exp(c - total))
-            keep_ref[d] = jnp.broadcast_to(jnp.exp(-total), (H, 128))
-        scale_ref[...] = jnp.concatenate(parts, axis=0).T.astype(BF16)
-        bt_ref[0] = bf_ref[...].astype(F32).T.astype(BF16)
-        bt_ref[1] = bb_ref[...].astype(F32).T.astype(BF16)
-
+def three_rows(value, width):
+    high, rest = two_parts(value)
+    middle, low = two_parts(rest)
+    row = lax.broadcasted_iota(jnp.int32, (16, width), 0)
+    tail = jnp.where(row == 0, high, jnp.where(row == 1, middle, jnp.where(row == 2, low, 0.0)))
+    return tail.astype(BF16)
+
+
+def state_kernel(
+    x_hbm, rf_hbm, rb_hbm, bf_hbm, bb_hbm, out_ref,
+    x_ref, r_ref, b_ref, scale_ref, sems,
+):
+    copies = [
+        pltpu.make_async_copy(rf_hbm, r_ref.at[0], sems.at[0]),
+        pltpu.make_async_copy(rb_hbm, r_ref.at[1], sems.at[1]),
+        pltpu.make_async_copy(bf_hbm, b_ref.at[0], sems.at[2]),
+        pltpu.make_async_copy(bb_hbm, b_ref.at[1], sems.at[3]),
+        pltpu.make_async_copy(x_hbm, x_ref, sems.at[4]),
+    ]
+    for copy in copies:
+        copy.start()
+    copies[0].wait()
+    copies[1].wait()
+    parts, keeps = [], []
+    for d, sums in enumerate((lane_sums, lane_sums_back)):
+        r = r_ref[d]
+        c = sums(r)
+        total = c[:, Q - 1 : Q] if d == 0 else c[:, 0:1]
+        parts += two_parts(step_of(r) * jnp.exp(c - total))
+        keeps.append(jnp.broadcast_to(jnp.exp(-total), (H, E)))
+    scale_ref[...] = jnp.concatenate(parts, axis=0).T.astype(BF16)
+    copies[2].wait()
+    copies[3].wait()
+    turned = [b_ref[d].astype(F32).T.astype(BF16) for d in range(2)]
+    copies[4].wait()
     x = x_ref[...].astype(F32)
+    head = lax.broadcasted_iota(jnp.int32, (H, E), 0)
+    column = lax.broadcasted_iota(jnp.int32, (H, E), 1)
     for d in range(2):
-        factor = dot(scale_ref[...], head_select(j, 4 * H, BLK, 2 * H * d, 2))
-        v = (x * factor).astype(BF16)
-        s = dot(bt_ref[d], v).astype(BF16)
-        head = lax.broadcasted_iota(jnp.int32, (H, BLK), 0)
-        column = lax.broadcasted_iota(jnp.int32, (H, BLK), 1)
-        keep = jnp.concatenate([keep_ref[d]] * (BLK // 128), axis=1)
-        keep = jnp.sum(
-            jnp.where(head == j * HPB + column // HEAD, keep, 0.0), axis=0, keepdims=True
-        )
-        high, rest = two_parts(keep)
-        middle, low = two_parts(rest)
-        row = lax.broadcasted_iota(jnp.int32, (16, BLK), 0)
-        tail = jnp.where(row == 0, high, jnp.where(row == 1, middle, jnp.where(row == 2, low, 0.0)))
-        tail = tail.astype(BF16)
-        for k in range(BLK // 128):
+        factor = dot(scale_ref[...], head_select(0, 4 * H, E, 2 * H * d, 2))
+        s = dot(turned[d], (x * factor).astype(BF16)).astype(BF16)
+        keep = jnp.where(head == column // HEAD, keeps[d], 0.0)
+        tail = three_rows(jnp.sum(keep, axis=0, keepdims=True), E)
+        for k in range(E // 128):
             out_ref[d, k, 0:N, :] = s[:, 128 * k : 128 * (k + 1)]
             out_ref[d, k, N:ROWS, :] = tail[:, 128 * k : 128 * (k + 1)]
 
 
 def state_call(x, rate_f, rate_b, b_f, b_b):
-    whole = lambda shape: pl.BlockSpec(shape, lambda j: (0,) * len(shape))
     return pl.pallas_call(
         state_kernel,
-        grid=(STEPS,),
-        in_specs=[
-            pl.BlockSpec((Q, BLK), lambda j: (0, j)),
-            whole((H, Q)),
-            whole((H, Q)),
-            whole((Q, N)),
-            whole((Q, N)),
-        ],
-        out_specs=pl.BlockSpec((2, BLK // 128, ROWS, 128), lambda j: (0, j, 0, 0)),
+        in_specs=[pl.BlockSpec(memory_space=pltpu.HBM)] * 5,
+        out_specs=pl.BlockSpec(memory_space=pltpu.VMEM),
         out_shape=jax.ShapeDtypeStruct((2, E // 128, ROWS, 128), BF16),
         scratch_shapes=[
+            pltpu.VMEM((Q, E), BF16),
+            pltpu.VMEM((2, H, Q), F32),
+            pltpu.VMEM((2, Q, N), BF16),
             pltpu.VMEM((Q, 4 * H), BF16),
-            pltpu.VMEM((2, N, Q), BF16),
-            pltpu.VMEM((2, H, 128), F32),
+            pltpu.SemaphoreType.DMA((5,)),
         ],
+        compiler_params=LIMIT,
         name="span_states",
     )(x, rate_f, rate_b, b_f, b_b)
 
 
 def inside_kernel(
     x_ref, gate_ref, rf_ref, rb_ref, bf_ref, cf_ref, bb_ref, cb_ref,
-    out_ref, silu_ref, score_ref, rows_ref, cols_ref,
+    out_ref, silu_ref, scale_ref, score_ref, rows_ref, cols_ref,
 ):
     j = pl.program_id(0)
     t = lax.broadcasted_iota(jnp.int32, (Q, Q), 0)
@@ -149,6 +157,8 @@
         rows_ref[1] = c_b + jnp.log(step_b) * LOG2E
         high, low = two_parts(own * step_b)
         cols_ref[...] = jnp.concatenate([c_f, c_b, high, low], axis=0).T
+        parts = two_parts(jnp.exp2(-c_f)) + two_parts(jnp.exp2(-c_b))
+        scale_ref[...] = jnp.concatenate(parts, axis=0).T.astype(BF16)
 
     gate = gate_ref[...].astype(F32)
     silu_ref[...] = (gate * jax.nn.sigmoid(gate)).astype(BF16)
@@ -176,8 +186,10 @@
         inside_kernel,
         grid=(STEPS,),
         in_specs=[columns, columns, whole((H, Q)), whole((H, Q))] + [whole((Q, N))] * 4,
-        out_specs=[columns, columns],
-        out_shape=[jax.ShapeDtypeStruct((Q, E), BF16)] * 2,
+        out_specs=[columns, columns, whole((Q, 4 * H))],
+        out_shape=[jax.ShapeDtypeStruct((Q, E), BF16)] * 2
+        + [jax.ShapeDtypeStruct((Q, 4 * H), BF16)],
+        compiler_params=LIMIT,
         scratch_shapes=[
             pltpu.VMEM((Q, Q), F32),
             pltpu.VMEM((2, H, Q), F32),
@@ -208,13 +220,10 @@
     state, kept = lax.fori_loop(
         0, count, step, (jnp.zeros((N, 128), F32), jnp.ones((1, 128), F32)), unroll=4
     )
-    high, rest = two_parts(kept)
-    middle, low = two_parts(rest)
-    row = lax.broadcasted_iota(jnp.int32, (16, 128), 0)
-    tail = jnp.where(row == 0, high, jnp.where(row == 1, middle, jnp.where(row == 2, low, 0.0)))
+    tail = three_rows(kept, 128)
     for g in range(copies):
         out_ref[g, 0:N, :] = state.astype(BF16)
-        out_ref[g, N:ROWS, :] = tail.astype(BF16)
+        out_ref[g, N:ROWS, :] = tail
 
 
 def entry_kernel(count, groups, place_ref, totals_ref, parts_ref, out_ref):
@@ -241,61 +250,38 @@
 
 
 def final_kernel(
-    in_ref, silu_ref, m_ref, rf_ref, rb_ref, cf_ref, cb_ref, gain_ref, w_ref,
-    out_ref, scale_ref, acc_ref, square_ref,
+    in_ref, silu_ref, scale_ref, m_ref, cf_ref, cb_ref, gain_ref, w_ref, out_ref, normed_ref
 ):
-    j = pl.program_id(0)
-
-    @pl.when(j == 0)
-    def _():
-        parts = two_parts(jnp.exp(-lane_sums(rf_ref[...])))
-        parts += two_parts(jnp.exp(-lane_sums_back(rb_ref[...])))
-        scale_ref[...] = jnp.concatenate(parts, axis=0).T.astype(BF16)
-        acc_ref[...] = jnp.zeros_like(acc_ref)
-        square_ref[...] = jnp.zeros_like(square_ref)
-
-    y = in_ref[...].astype(F32)
-    for d, c_ref in enumerate((cf_ref, cb_ref)):
-        factor = dot(scale_ref[...], head_select(j, 4 * H, BLK, 2 * H * d, 2))
-        m = jnp.concatenate([m_ref[d, k] for k in range(BLK // 128)], axis=1)
-        y = y + factor * dot(c_ref[...], m)
-    gated = y * silu_ref[...].astype(F32)
-    square = gated * gated
-    square_ref[...] += square[:, :128] + square[:, 128:]
-    acc_ref[...] += dot((gated * gain_ref[...]).astype(BF16), w_ref[...])
-
-    @pl.when(j == STEPS - 1)
-    def _():
-        mean = jnp.sum(square_ref[...], axis=1, keepdims=True) * (1.0 / E)
-        out_ref[...] = (acc_ref[...] * lax.rsqrt(mean + 1e-05)).astype(BF16)
-
-
-def final_call(inside, silu, m, rate_f, rate_b, c_f, c_b, gain, weight):
-    whole = lambda shape: pl.BlockSpec(shape, lambda j: (0,) * len(shape))
-    columns = pl.BlockSpec((Q, BLK), lambda j: (0, j))
+    square = jnp.zeros((Q, 128), F32)
+    for j in range(E // FW):
+        at = pl.ds(FW * j, FW)
+        y = in_ref[:, at].astype(F32)
+        for d, c_ref in enumerate((cf_ref, cb_ref)):
+            factor = dot(scale_ref[...], head_select(j, 4 * H, FW, 2 * H * d, 2))
+            m = jnp.concatenate([m_ref[d, FW // 128 * j + k] for k in range(FW // 128)], axis=1)
+            y = y + factor * dot(c_ref[...], m)
+        gated = y * silu_ref[:, at].astype(F32)
+        for k in range(FW // 128):
+            part = gated[:, 128 * k : 128 * (k + 1)]
+            square = square + part * part
+        normed_ref[:, at] = (gated * gain_ref[:, at]).astype(BF16)
+    mean = jnp.sum(square, axis=1, keepdims=True) * (1.0 / E)
+    scale = lax.rsqrt(mean + 1e-05)
+    for n in range(D // 256):
+        at = pl.ds(256 * n, 256)
+        out_ref[:, at] = (dot(normed_ref[...], w_ref[:, at]) * scale).astype(BF16)
+
+
+def final_call(inside, silu, scale, m, c_f, c_b, gain, weight):
     return pl.pallas_call(
         final_kernel,
-        grid=(STEPS,),
-        in_specs=[
-            columns,
-            columns,
-            pl.BlockSpec((2, BLK // 128, N, 128), lambda j: (0, j, 0, 0)),
-            whole((H, Q)),
-            whole((H, Q)),
-            whole((Q, N)),
-            whole((Q, N)),
-            pl.BlockSpec((1, BLK), lambda j: (0, j)),
-            pl.BlockSpec((BLK, D), lambda j: (j, 0)),
-        ],
-        out_specs=whole((Q, D)),
+        in_specs=[pl.BlockSpec(memory_space=pltpu.VMEM)] * 8,
+        out_specs=pl.BlockSpec(memory_space=pltpu.VMEM),
         out_shape=jax.ShapeDtypeStruct((Q, D), BF16),
-        scratch_shapes=[
-            pltpu.VMEM((Q, 4 * H), BF16),
-            pltpu.VMEM((Q, D), F32),
-            pltpu.VMEM((Q, 128), F32),
-        ],
+        scratch_shapes=[pltpu.VMEM((Q, E), BF16)],
+        compiler_params=LIMIT,
         name="gate_norm_project",
-    )(inside, silu, m, rate_f, rate_b, c_f, c_b, gain, weight)
+    )(inside, silu, scale, m, c_f, c_b, gain, weight)
 
 
 def per_device(
@@ -315,6 +301,7 @@
         in_specs=vmem_specs(1),
         out_specs=pl.BlockSpec(memory_space=pltpu.VMEM),
         out_shape=jax.ShapeDtypeStruct((groups, ROWS, 128), BF16),
+        compiler_params=LIMIT,
         name="group_totals",
     )(place, parts)
     totals = lax.all_to_all(totals, "grp", 0, 0, tiled=True)
@@ -323,16 +310,16 @@
         in_specs=vmem_specs(2),
         out_specs=pl.BlockSpec(memory_space=pltpu.VMEM),
         out_shape=jax.ShapeDtypeStruct((count, N, 128), BF16),
+        compiler_params=LIMIT,
         name="entry_states",
     )(place, totals, parts)
     m = lax.all_to_all(entries, "seq", 0, 0, tiled=True).reshape(2, E // 128, N, 128)
-    inside, silu = inside_call(
+    inside, silu, scale = inside_call(
         features, gate_input, rate_forward, rate_backward,
         b_forward, c_forward, b_backward, c_backward,
     )
     return final_call(
-        inside, silu, m, rate_forward, rate_backward, c_forward, c_backward,
-        norm_gain.reshape(1, E), out_weight,
+        inside, silu, scale, m, c_forward, c_backward, norm_gain.reshape(1, E), out_weight
     )
 
 

time: 114 us -> 105 us (0.921)
  Pallas kernels: 31.5 us -> 15.7 us
  local copies, waits for them, and re-layouts: 2.02 us -> 9.08 us
    pallas_call x2, Pallas kernels: 17.5 us -> 6.51 us  [the longest x1 3.28 us: final_call(): pl.pallas_call(final_kernel, in_specs=[pl.BlockSpec(memory_space=pltpu.VM...]
    unnamed x4 -> x30, local copies, waits for them, and re-layouts: 2.02 us -> 9.08 us
    pallas_call x1, Pallas kernels: 9.02 us -> 6.45 us  [inside_call(): pl.pallas_call(inside_kernel, grid=(STEPS,), in_specs=[columns, columns,...]
    pallas_call x1, Pallas kernels: 2.32 us -> 0.86 us  [per_device(): pl.pallas_call(functools.partial(total_kernel, count, groups), in_specs=v...]
  transfers between devices with their start and end apart: 2 -> 2, of which waited for: 2 -> 2; matrix products, arithmetic and copies ran while one was open for 1% -> 0% of each run, Pallas kernels for 8% -> 6%
where the time goes in v1:
time: 105 us
  waiting for transfers between devices  50.8 us (48%)
  starting transfers between devices  16.9 us (16%)
  Pallas kernels  15.7 us (15%)
  blocking collectives  12 us (11%)
  local copies, waits for them, and re-layouts  9.08 us (9%)
    all_to_all x1, waiting for transfers between devices, per_device(): parts = lax.all_to_all(states, 'seq', 0, 0, tiled=True)  31.1 us
    all_to_all x1, waiting for transfers between devices, per_device(): lax.all_to_all(entries, 'seq', 0, 0, tiled=True)  19.6 us
    all_to_all x1, blocking collectives, per_device(): totals = lax.all_to_all(totals, 'grp', 0, 0, tiled=True)  12 us
    all_to_all x1, starting transfers between devices, per_device(): parts = lax.all_to_all(states, 'seq', 0, 0, tiled=True)  11.4 us
    unnamed x30, local copies, waits for them, and re-layouts  9.08 us
    pallas_call x1, Pallas kernels, inside_call(): pl.pallas_call(inside_kernel, grid=(STEPS,), in_specs=[columns, columns,...  6.45 us
    all_to_all x1, starting transfers between devices, per_device(): lax.all_to_all(entries, 'seq', 0, 0, tiled=True)  5.56 us
    pallas_call x1, Pallas kernels, final_call(): pl.pallas_call(final_kernel, in_specs=[pl.BlockSpec(memory_space=pltpu.VM...  3.28 us
  transfers between devices with their start and end apart: 2, of which 2 were waited for; matrix products, arithmetic and copies ran while one was open for 0% of the time, Pallas kernels for 6%

profile of v1, /device:TPU:32, one launch (start us, length us, event | category | flops | bytes accessed | tf_op | source)
XLA Modules:
  0.0 104.6 jit_solution(17033191990882835985)
XLA Ops:
  0.0 0.0 copy-start.1
  0.0 1.2 %copy-done.1 = bf16[256,2048]{1,0:T(8,128)(2,1)S(1)} copy-done((bf16[256,2048]{1,0:T(8,128)(2,1)S(1)}, bf16[256,2048]{1,0:T(8,128)(2,1)}, u32[]{:S(2)}) %copy-start.1) | copy-done | bytes 1048600
  1.2 0.0 copy-start.5
  1.2 0.8 copy-done.5
  2.1 0.0 copy-start.7
  2.1 0.8 copy-done.7
  2.9 0.0 copy-start.9
  2.9 0.8 copy-done.9
  3.7 0.0 copy-start.11
  3.7 0.8 copy-done.11
  4.4 3.2 %span_states.1 = bf16[2,16,144,128]{3,2,1,0:T(8,128)(2,1)} custom-call(bf16[256,2048]{1,0:T(8,128)(2,1)S(1)} %copy-done.1, f32[32,256]{1,0:T(8,128)S(1)} %copy-done.9, f32[32,256]{1,0:T(8,128)S(1)} %copy-done.11, bf16[256,128]{1,0:T(8,128)(2,1)S(1)} %copy-done.5, bf16[256,128]{1,0:T(8,128)(2,1)S(1)} %copy-done.7), custom_call_target="tpu_custom_call" | custom-call | tf_op jit(solution)/shard_map/span_states/pallas_call | solution.py:120
  7.7 11.4 %all-to-all-start = ((bf16[32,144,128]{2,1,0:T(8,128)(2,1)}), bf16[32,144,128]{2,1,0:T(8,128)(2,1)S(1)}, u32[]{:S(2)}, u32[]{:S(2)}) async-start(bf16[32,144,128]{2,1,0:T(8,128)(2,1)} %bitcast.2), calls=%async_computation | async-start | bytes 2359296 | tf_op jit(solution)/shard_map/all_to_all | solution.py:298
  19.0 0.1 pad_add_fusion.place_ref
  19.1 31.1 %all-to-all-done.parts_ref = bf16[32,144,128]{2,1,0:T(8,128)(2,1)S(1)} async-done(((bf16[32,144,128]{2,1,0:T(8,128)(2,1)}), bf16[32,144,128]{2,1,0:T(8,128)(2,1)S(1)}, u32[]{:S(2)}, u32[]{:S(2)}) %all-to-all-start) | async-done | bytes 1179680 | tf_op jit(solution)/shard_map/all_to_all | solution.py:298
  50.2 0.9 group_totals.1
  51.1 12.0 %all_to_all.15.totals_ref = bf16[8,144,128]{2,1,0:T(8,128)(2,1)S(1)} all-to-all(bf16[8,144,128]{2,1,0:T(8,128)(2,1)S(1)} %group_totals.1), channel_id=1, replica_groups=mesh['grp'=8,'seq'=32] {'grp'}, dimensions={0} | all-to-all | bytes 589824 | tf_op jit(solution)/shard_map/all_to_all | solution.py:307
  63.1 1.8 %entry_states.1 = bf16[32,128,128]{2,1,0:T(8,128)(2,1)} custom-call(s32[2]{0:T(128)S(1)} %pad_add_fusion.place_ref, bf16[8,144,128]{2,1,0:T(8,128)(2,1)S(1)} %all_to_all.15.totals_ref, bf16[32,144,128]{2,1,0:T(8,128)(2,1)S(1)} %all-to-all-done.parts_ref), custom_call_target="tpu_custom_call" | custom-call | tf_op jit(solution)/shard_map/entry_states/pallas_call | solution.py:308
  64.9 0.0 copy-start.3
  64.9 0.0 copy-start.4
  64.9 0.0 copy-start.6
  64.9 0.0 copy-start.8
  64.9 0.0 copy-start.10
  65.0 0.0 copy-start.12
  65.0 5.6 %all-to-all-start.2 = ((bf16[32,128,128]{2,1,0:T(8,128)(2,1)}), bf16[32,128,128]{2,1,0:T(8,128)(2,1)S(1)}, u32[]{:S(2)}, u32[]{:S(2)}) async-start(bf16[32,128,128]{2,1,0:T(8,128)(2,1)} %entry_states.1), calls=%async_computation.2 | async-start | bytes 2097152 | tf_op jit(solution)/shard_map/all_to_all | solution.py:316
  70.5 0.0 copy-done.3
  70.6 0.0 copy-done.4
  70.6 0.0 copy-done.6
  70.6 0.0 copy-done.8
  70.6 0.0 copy-done.10
  70.6 0.0 copy-done.12
  70.6 0.0 copy-start.2
  70.6 1.2 %copy-done.2 = bf16[256,2048]{1,0:T(8,128)(2,1)S(1)} copy-done((bf16[256,2048]{1,0:T(8,128)(2,1)S(1)}, bf16[256,2048]{1,0:T(8,128)(2,1)}, u32[]{:S(2)}) %copy-start.2) | copy-done | bytes 1048600
  71.8 0.0 copy-start.14
  71.8 1.2 %copy-done.14 = bf16[256,2048]{1,0:T(8,128)(2,1)S(1)} copy-done((bf16[256,2048]{1,0:T(8,128)(2,1)S(1)}, bf16[256,2048]{1,0:T(8,128)(2,1)}, u32[]{:S(2)}) %copy-start.14) | copy-done | bytes 1048600
  73.1 0.0 copy-start.13
  73.1 6.4 %inside_spans.1 = (bf16[256,2048]{1,0:T(8,128)(2,1)S(1)}, bf16[256,2048]{1,0:T(8,128)(2,1)S(1)}, bf16[256,128]{1,0:T(8,128)(2,1)S(1)}) custom-call(bf16[256,2048]{1,0:T(8,128)(2,1)S(1)} %copy-done.2, bf16[256,2048]{1,0:T(8,128)(2,1)S(1)} %copy-done.14, f32[32,256]{1,0:T(8,128)S(1)} %copy-done.10, f32[32,256]{1,0:T(8,128)S(1)} %copy-done.12, ...), custom_call_target="tpu_custom_call" | custom-call | flops 536870912 | bytes 4194304 | tf_op jit(solution)/shard_map/inside_spans/pallas_call | solution.py:185
  79.5 19.6 %all-to-all-done.2 = bf16[32,128,128]{2,1,0:T(8,128)(2,1)S(1)} async-done(((bf16[32,128,128]{2,1,0:T(8,128)(2,1)}), bf16[32,128,128]{2,1,0:T(8,128)(2,1)S(1)}, u32[]{:S(2)}, u32[]{:S(2)}) %all-to-all-start.2) | async-done | bytes 1048608 | tf_op jit(solution)/shard_map/all_to_all | solution.py:316
  99.2 0.0 copy-done.13
  99.2 0.0 copy-start
  99.2 2.2 %copy-done = bf16[2048,1024]{1,0:T(8,128)(2,1)S(1)} copy-done((bf16[2048,1024]{1,0:T(8,128)(2,1)S(1)}, bf16[2048,1024]{1,0:T(8,128)(2,1)}, u32[]{:S(2)}) %copy-start) | copy-done | bytes 4194328
  101.4 3.3 %gate_norm_project.1 = bf16[256,1024]{1,0:T(8,128)(2,1)} custom-call(bf16[256,2048]{1,0:T(8,128)(2,1)S(1)} %get-tuple-element.8.in_ref, bf16[256,2048]{1,0:T(8,128)(2,1)S(1)} %get-tuple-element.9.silu_ref, bf16[256,128]{1,0:T(8,128)(2,1)S(1)} %get-tuple-element.10.scale_ref, bf16[2,16,128,128]{3,2,1,0:T(8,128)(2,1)S(1)} %bitcast.5, ...), custom_call_target="tpu_custom_call" | custom-call | tf_op jit(solution)/shard_map/gate_norm_project/pallas_call | solution.py:276
Async XLA Ops:
  0.0 1.2 %copy-start.1 = (bf16[256,2048]{1,0:T(8,128)(2,1)S(1)}, bf16[256,2048]{1,0:T(8,128)(2,1)}, u32[]{:S(2)}) copy-start(bf16[256,2048]{1,0:T(8,128)(2,1)} %x_hbm.1) | copy-start | bytes 3145732
  1.2 0.8 copy-start.5
  2.1 0.8 copy-start.7
  2.9 0.8 copy-start.9
  3.7 0.8 copy-start.11
  7.7 42.6 %all-to-all-start = ((bf16[32,144,128]{2,1,0:T(8,128)(2,1)}), bf16[32,144,128]{2,1,0:T(8,128)(2,1)S(1)}, u32[]{:S(2)}, u32[]{:S(2)}) async-start(bf16[32,144,128]{2,1,0:T(8,128)(2,1)} %bitcast.2), calls=%async_computation | async-start | bytes 2359296 | tf_op jit(solution)/shard_map/all_to_all | solution.py:298
  64.9 5.6 %copy-start.3 = (bf16[256,128]{1,0:T(8,128)(2,1)S(1)}, bf16[256,128]{1,0:T(8,128)(2,1)}, u32[]{:S(2)}) copy-start(bf16[256,128]{1,0:T(8,128)(2,1)} %cf_ref.3) | copy-start | bytes 196612
  64.9 5.6 %copy-start.4 = (bf16[256,128]{1,0:T(8,128)(2,1)S(1)}, bf16[256,128]{1,0:T(8,128)(2,1)}, u32[]{:S(2)}) copy-start(bf16[256,128]{1,0:T(8,128)(2,1)} %cb_ref.3) | copy-start | bytes 196612
  64.9 5.6 %copy-start.6 = (bf16[256,128]{1,0:T(8,128)(2,1)S(1)}, bf16[256,128]{1,0:T(8,128)(2,1)}, u32[]{:S(2)}) copy-start(bf16[256,128]{1,0:T(8,128)(2,1)} %bf_hbm.1) | copy-start | bytes 196612
  64.9 5.6 %copy-start.8 = (bf16[256,128]{1,0:T(8,128)(2,1)S(1)}, bf16[256,128]{1,0:T(8,128)(2,1)}, u32[]{:S(2)}) copy-start(bf16[256,128]{1,0:T(8,128)(2,1)} %bb_hbm.1) | copy-start | bytes 196612
  64.9 5.6 %copy-start.10 = (f32[32,256]{1,0:T(8,128)S(1)}, f32[32,256]{1,0:T(8,128)}, u32[]{:S(2)}) copy-start(f32[32,256]{1,0:T(8,128)} %rf_hbm.1) | copy-start | bytes 98308
  65.0 5.6 %copy-start.12 = (f32[32,256]{1,0:T(8,128)S(1)}, f32[32,256]{1,0:T(8,128)}, u32[]{:S(2)}) copy-start(f32[32,256]{1,0:T(8,128)} %rb_hbm.1) | copy-start | bytes 98308
  65.0 34.2 %all-to-all-start.2 = ((bf16[32,128,128]{2,1,0:T(8,128)(2,1)}), bf16[32,128,128]{2,1,0:T(8,128)(2,1)S(1)}, u32[]{:S(2)}, u32[]{:S(2)}) async-start(bf16[32,128,128]{2,1,0:T(8,128)(2,1)} %entry_states.1), calls=%async_computation.2 | async-start | bytes 2097152 | tf_op jit(solution)/shard_map/all_to_all | solution.py:316
  70.6 1.2 %copy-start.2 = (bf16[256,2048]{1,0:T(8,128)(2,1)S(1)}, bf16[256,2048]{1,0:T(8,128)(2,1)}, u32[]{:S(2)}) copy-start(bf16[256,2048]{1,0:T(8,128)(2,1)} %x_hbm.1) | copy-start | bytes 3145732
  71.8 1.2 %copy-start.14 = (bf16[256,2048]{1,0:T(8,128)(2,1)S(1)}, bf16[256,2048]{1,0:T(8,128)(2,1)}, u32[]{:S(2)}) copy-start(bf16[256,2048]{1,0:T(8,128)(2,1)} %gate_ref.1) | copy-start | bytes 3145732
  73.1 26.1 %copy-start.13 = (f32[2048]{0:T(1024)S(1)}, f32[2048]{0:T(1024)}, u32[]{:S(2)}) copy-start(f32[2048]{0:T(1024)} %param.18) | copy-start | bytes 24580
  99.2 2.2 %copy-start = (bf16[2048,1024]{1,0:T(8,128)(2,1)S(1)}, bf16[2048,1024]{1,0:T(8,128)(2,1)}, u32[]{:S(2)}) copy-start(bf16[2048,1024]{1,0:T(8,128)(2,1)} %w_ref.1) | copy-start | bytes 12582916

commit v2 on v1

--- a/solution.py
+++ b/solution.py
@@ -17,6 +17,9 @@
 FW = 256
 HPB = BLK // HEAD
 ROWS = N + 16
+HALF = E // 2
+SHARE = N // 2
+PART = SHARE + 16
 LOG2E = 1.4426950408889634
 F32 = jnp.float32
 BF16 = jnp.bfloat16
@@ -77,8 +80,8 @@
 
 
 def state_kernel(
-    x_hbm, rf_hbm, rb_hbm, bf_hbm, bb_hbm, out_ref,
-    x_ref, r_ref, b_ref, scale_ref, sems,
+    place_ref, x_hbm, rf_hbm, rb_hbm, bf_hbm, bb_hbm, own_ref, next_ref, last_ref,
+    x_ref, r_ref, b_ref, scale_ref, keep_ref, sems,
 ):
     copies = [
         pltpu.make_async_copy(rf_hbm, r_ref.at[0], sems.at[0]),
@@ -89,53 +92,84 @@
     ]
     for copy in copies:
         copy.start()
+    odd = place_ref[0]
     copies[0].wait()
     copies[1].wait()
-    parts, keeps = [], []
+    parts = []
     for d, sums in enumerate((lane_sums, lane_sums_back)):
         r = r_ref[d]
         c = sums(r)
         total = c[:, Q - 1 : Q] if d == 0 else c[:, 0:1]
         parts += two_parts(step_of(r) * jnp.exp(c - total))
-        keeps.append(jnp.broadcast_to(jnp.exp(-total), (H, E)))
+        keep_ref[d] = jnp.broadcast_to(jnp.exp(-total), (H, HALF))
     scale_ref[...] = jnp.concatenate(parts, axis=0).T.astype(BF16)
     copies[2].wait()
     copies[3].wait()
     turned = [b_ref[d].astype(F32).T.astype(BF16) for d in range(2)]
     copies[4].wait()
-    x = x_ref[...].astype(F32)
-    head = lax.broadcasted_iota(jnp.int32, (H, E), 0)
-    column = lax.broadcasted_iota(jnp.int32, (H, E), 1)
-    for d in range(2):
-        factor = dot(scale_ref[...], head_select(0, 4 * H, E, 2 * H * d, 2))
+    head = lax.broadcasted_iota(jnp.int32, (H, HALF), 0)
+    column = lax.broadcasted_iota(jnp.int32, (H, HALF), 1)
+
+    work = ((0, odd, next_ref), (1, 1 - odd, last_ref), (0, 1 - odd, own_ref.at[0]), (1, odd, own_ref.at[1]))
+    for d, half, ref in work:
+        at = pl.multiple_of(half * HALF, HALF)
+        x = x_ref[:, pl.ds(at, HALF)].astype(F32)
+        factor = dot(scale_ref[...], head_select(half, 4 * H, HALF, 2 * H * d, 2))
         s = dot(turned[d], (x * factor).astype(BF16)).astype(BF16)
-        keep = jnp.where(head == column // HEAD, keeps[d], 0.0)
-        tail = three_rows(jnp.sum(keep, axis=0, keepdims=True), E)
-        for k in range(E // 128):
-            out_ref[d, k, 0:N, :] = s[:, 128 * k : 128 * (k + 1)]
-            out_ref[d, k, N:ROWS, :] = tail[:, 128 * k : 128 * (k + 1)]
-
-
-def state_call(x, rate_f, rate_b, b_f, b_b):
+        keep = jnp.where(head == half * (H // 2) + column // HEAD, keep_ref[d], 0.0)
+        tail = three_rows(jnp.sum(keep, axis=0, keepdims=True), HALF)
+        for k in range(HALF // 128):
+            ref[k, 0:N, :] = s[:, 128 * k : 128 * (k + 1)]
+            ref[k, N:ROWS, :] = tail[:, 128 * k : 128 * (k + 1)]
+
+
+def state_call(place, x, rate_f, rate_b, b_f, b_b):
+    part = jax.ShapeDtypeStruct((HALF // 128, ROWS, 128), BF16)
     return pl.pallas_call(
         state_kernel,
-        in_specs=[pl.BlockSpec(memory_space=pltpu.HBM)] * 5,
-        out_specs=pl.BlockSpec(memory_space=pltpu.VMEM),
-        out_shape=jax.ShapeDtypeStruct((2, E // 128, ROWS, 128), BF16),
+        in_specs=[pl.BlockSpec(memory_space=pltpu.SMEM)]
+        + [pl.BlockSpec(memory_space=pltpu.HBM)] * 5,
+        out_specs=[pl.BlockSpec(memory_space=pltpu.VMEM)] * 3,
+        out_shape=[jax.ShapeDtypeStruct((2, HALF // 128, ROWS, 128), BF16), part, part],
         scratch_shapes=[
             pltpu.VMEM((Q, E), BF16),
             pltpu.VMEM((2, H, Q), F32),
             pltpu.VMEM((2, Q, N), BF16),
             pltpu.VMEM((Q, 4 * H), BF16),
+            pltpu.VMEM((2, H, HALF), F32),
             pltpu.SemaphoreType.DMA((5,)),
         ],
+        compiler_params=pltpu.CompilerParams(vmem_limit_bytes=60 * 1024 * 1024),
+        name="span_states",
+    )(place, x, rate_f, rate_b, b_f, b_b)
+
+
+def pair_kernel(own_ref, from_last_ref, from_next_ref, out_ref):
+    for d, first_ref in enumerate((from_last_ref, from_next_ref)):
+        for k in range(HALF // 128):
+            second, keep = read_part(own_ref.at[d], k, N)
+            first, first_keep = read_part(first_ref, k, N)
+            total = (keep * first + second).astype(BF16)
+            tail = three_rows(keep * first_keep, 128)
+            for n in range(2):
+                place = (d * (HALF // 128) + k) * 2 + n
+                out_ref[place, 0:SHARE, :] = total[SHARE * n : SHARE * (n + 1)]
+                out_ref[place, SHARE:PART, :] = tail
+
+
+def pair_call(own, from_last, from_next):
+    return pl.pallas_call(
+        pair_kernel,
+        in_specs=[pl.BlockSpec(memory_space=pltpu.VMEM)] * 3,
+        out_specs=pl.BlockSpec(memory_space=pltpu.VMEM),
+        out_shape=jax.ShapeDtypeStruct((2 * E // 128, PART, 128), BF16),
         compiler_params=LIMIT,
-        name="span_states",
-    )(x, rate_f, rate_b, b_f, b_b)
+        name="pair_totals",
+    )(own, from_last, from_next)
 
 
 def inside_kernel(
-    x_ref, gate_ref, rf_ref, rb_ref, bf_ref, cf_ref, bb_ref, cb_ref,
+    x_ref, gate_ref, rf_ref, rb_ref, bf_ref, cf_ref, bb_ref, cb_ref, w_ref,
     out_ref, silu_ref, scale_ref, score_ref, rows_ref, cols_ref,
 ):
     j = pl.program_id(0)
@@ -179,13 +213,14 @@
         out_ref[:, 128 * p : 128 * (p + 1)] = y.astype(BF16)
 
 
-def inside_call(x, gate, rate_f, rate_b, b_f, c_f, b_b, c_b):
+def inside_call(x, gate, rate_f, rate_b, b_f, c_f, b_b, c_b, weight):
     whole = lambda shape: pl.BlockSpec(shape, lambda j: (0,) * len(shape))
     columns = pl.BlockSpec((Q, BLK), lambda j: (0, j))
     return pl.pallas_call(
         inside_kernel,
         grid=(STEPS,),
-        in_specs=[columns, columns, whole((H, Q)), whole((H, Q))] + [whole((Q, N))] * 4,
+        in_specs=[columns, columns, whole((H, Q)), whole((H, Q))] + [whole((Q, N))] * 4
+        + [pl.BlockSpec(memory_space=pltpu.VMEM)],
         out_specs=[columns, columns, whole((Q, 4 * H))],
         out_shape=[jax.ShapeDtypeStruct((Q, E), BF16)] * 2
         + [jax.ShapeDtypeStruct((Q, 4 * H), BF16)],
@@ -199,50 +234,60 @@
             flops=2 * H * Q * Q * 128, bytes_accessed=4 * Q * E * 2, transcendentals=H * Q * Q
         ),
         name="inside_spans",
-    )(x, gate, rate_f, rate_b, b_f, c_f, b_b, c_b)
-
-
-def read_part(ref, index):
-    state = ref[index, 0:N, :].astype(F32)
-    tail = ref[index, N:ROWS, :].astype(F32)
+    )(x, gate, rate_f, rate_b, b_f, c_f, b_b, c_b, weight)
+
+
+def read_part(ref, index, rows):
+    state = ref[index, 0:rows, :].astype(F32)
+    tail = ref[index, rows : rows + 16, :].astype(F32)
     return state, tail[0:1] + tail[1:2] + tail[2:3]
 
 
 def total_kernel(count, copies, place_ref, parts_ref, out_ref):
-    backward = place_ref[0]
+    backward = place_ref[1]
 
     def step(i, carried):
-        state, kept = carried
-        index = jnp.where(backward == 1, count - 1 - i, i)
-        own, keep = read_part(parts_ref, index)
-        return keep * state + own, keep * kept
-
-    state, kept = lax.fori_loop(
-        0, count, step, (jnp.zeros((N, 128), F32), jnp.ones((1, 128), F32)), unroll=4
-    )
-    tail = three_rows(kept, 128)
-    for g in range(copies):
-        out_ref[g, 0:N, :] = state.astype(BF16)
-        out_ref[g, N:ROWS, :] = tail
+        pair = jnp.where(backward == 1, count // 2 - 1 - i, i)
+        result = []
+        for q in range(2):
+            own, keep = read_part(parts_ref, 2 * pair + q, SHARE)
+            result += [keep * carried[2 * q] + own, keep * carried[2 * q + 1]]
+        return tuple(result)
+
+    start = (jnp.zeros((SHARE, 128), F32), jnp.ones((1, 128), F32))
+    result = lax.fori_loop(0, count // 2, step, start + start, unroll=4)
+    for q in range(2):
+        state = result[2 * q].astype(BF16)
+        tail = three_rows(result[2 * q + 1], 128)
+        for g in range(copies):
+            out_ref[g, PART * q : PART * q + SHARE, :] = state
+            out_ref[g, PART * q + SHARE : PART * (q + 1), :] = tail
 
 
 def entry_kernel(count, groups, place_ref, totals_ref, parts_ref, out_ref):
-    backward, mine = place_ref[0], place_ref[1]
-
-    def outer(i, state):
-        index = jnp.where(backward == 1, groups - 1 - i, i)
-        own, keep = read_part(totals_ref, index)
-        return keep * state + own
-
-    state = lax.fori_loop(0, mine, outer, jnp.zeros((N, 128), F32))
-
-    def step(i, state):
-        index = jnp.where(backward == 1, count - 1 - i, i)
-        out_ref[index] = state.astype(BF16)
-        own, keep = read_part(parts_ref, index)
-        return keep * state + own
-
-    lax.fori_loop(0, count, step, state, unroll=4)
+    backward, mine = place_ref[1], place_ref[2]
+    states = []
+    for q in range(2):
+        def outer(i, state, q=q):
+            index = jnp.where(backward == 1, groups - 1 - i, i)
+            own = totals_ref[index, PART * q : PART * q + SHARE, :].astype(F32)
+            tail = totals_ref[index, PART * q + SHARE : PART * (q + 1), :].astype(F32)
+            return (tail[0:1] + tail[1:2] + tail[2:3]) * state + own
+
+        open_pair = (mine == 0) & (backward == q)
+        limit = jnp.where(open_pair, groups, mine)
+        states.append(lax.fori_loop(0, limit, outer, jnp.zeros((SHARE, 128), F32)))
+
+    def step(i, states):
+        pair = jnp.where(backward == 1, count // 2 - 1 - i, i)
+        result = []
+        for q in range(2):
+            out_ref[2 * pair + q] = states[q].astype(BF16)
+            own, keep = read_part(parts_ref, 2 * pair + q, SHARE)
+            result.append(keep * states[q] + own)
+        return tuple(result)
+
+    lax.fori_loop(0, count // 2, step, tuple(states), unroll=4)
 
 
 def vmem_specs(n):
@@ -250,8 +295,19 @@
 
 
 def final_kernel(
-    in_ref, silu_ref, scale_ref, m_ref, cf_ref, cb_ref, gain_ref, w_ref, out_ref, normed_ref
+    place_ref, in_ref, silu_ref, scale_ref, pair_ref, from_last_ref, from_next_ref,
+    other_f_ref, other_b_ref, cf_ref, cb_ref, gain_ref, w_ref, out_ref, normed_ref, m_ref,
 ):
+    odd = place_ref[0]
+    blocks = HALF // 128
+    others = (other_f_ref, other_b_ref)
+    for d, first_ref in enumerate((from_last_ref, from_next_ref)):
+        half = 1 - odd if d == 0 else odd
+        for k in range(blocks):
+            first, keep = read_part(first_ref, k, N)
+            entry = keep * pair_ref[d, k].astype(F32) + first
+            m_ref[d, half * blocks + k] = entry.astype(BF16)
+            m_ref[d, (1 - half) * blocks + k] = others[d][k]
     square = jnp.zeros((Q, 128), F32)
     for j in range(E // FW):
         at = pl.ds(FW * j, FW)
@@ -272,16 +328,19 @@
         out_ref[:, at] = (dot(normed_ref[...], w_ref[:, at]) * scale).astype(BF16)
 
 
-def final_call(inside, silu, scale, m, c_f, c_b, gain, weight):
+def final_call(place, inside, silu, scale, states, c_f, c_b, gain, weight):
     return pl.pallas_call(
         final_kernel,
-        in_specs=[pl.BlockSpec(memory_space=pltpu.VMEM)] * 8,
+        in_specs=vmem_specs(12),
         out_specs=pl.BlockSpec(memory_space=pltpu.VMEM),
         out_shape=jax.ShapeDtypeStruct((Q, D), BF16),
-        scratch_shapes=[pltpu.VMEM((Q, E), BF16)],
+        scratch_shapes=[
+            pltpu.VMEM((Q, E), BF16),
+            pltpu.VMEM((2, E // 128, N, 128), BF16),
+        ],
         compiler_params=LIMIT,
         name="gate_norm_project",
-    )(inside, silu, scale, m, c_f, c_b, gain, weight)
+    )(place, inside, silu, scale, *states, c_f, c_b, gain, weight)
 
 
 def per_device(
@@ -289,18 +348,26 @@
     rate_forward, rate_backward, norm_gain, out_weight,
 ):
     count, groups = lax.axis_size("seq"), lax.axis_size("grp")
-    states = state_call(features, rate_forward, rate_backward, b_forward, b_backward)
-    states = states.reshape(count, ROWS, 128)
-    backward = (lax.axis_index("seq") >= count // 2).astype(jnp.int32)
-    group = lax.axis_index("grp")
+    member, group = lax.axis_index("seq"), lax.axis_index("grp")
+    odd = member % 2
+    backward = (member >= count // 2).astype(jnp.int32)
     mine = jnp.where(backward == 1, groups - 1 - group, group)
-    place = jnp.stack([backward, mine]).astype(jnp.int32)
-    parts = lax.all_to_all(states, "seq", 0, 0, tiled=True)
+    place = jnp.stack([odd, backward, mine]).astype(jnp.int32)
+    spans = count * groups
+    up = [(k, k + 1) for k in range(spans)]
+    down = [(k, k - 1) for k in range(spans)]
+    own, to_next, to_last = state_call(
+        place, features, rate_forward, rate_backward, b_forward, b_backward
+    )
+    from_last = lax.ppermute(to_next, ("grp", "seq"), up[:-1])
+    from_next = lax.ppermute(to_last, ("grp", "seq"), down[1:])
+    parts = pair_call(own, from_last, from_next)
+    parts = lax.all_to_all(parts, "seq", 0, 0, tiled=True)
     totals = pl.pallas_call(
         functools.partial(total_kernel, count, groups),
         in_specs=vmem_specs(1),
         out_specs=pl.BlockSpec(memory_space=pltpu.VMEM),
-        out_shape=jax.ShapeDtypeStruct((groups, ROWS, 128), BF16),
+        out_shape=jax.ShapeDtypeStruct((groups, 2 * PART, 128), BF16),
         compiler_params=LIMIT,
         name="group_totals",
     )(place, parts)
@@ -309,17 +376,22 @@
         functools.partial(entry_kernel, count, groups),
         in_specs=vmem_specs(2),
         out_specs=pl.BlockSpec(memory_space=pltpu.VMEM),
-        out_shape=jax.ShapeDtypeStruct((count, N, 128), BF16),
+        out_shape=jax.ShapeDtypeStruct((count, SHARE, 128), BF16),
         compiler_params=LIMIT,
         name="entry_states",
     )(place, totals, parts)
-    m = lax.all_to_all(entries, "seq", 0, 0, tiled=True).reshape(2, E // 128, N, 128)
+    pair = lax.all_to_all(entries, "seq", 0, 0, tiled=True)
+    pair = pair.reshape(2, HALF // 128, N, 128)
+    other_f = lax.ppermute(pair[0], ("grp", "seq"), down[1:] + [(0, spans - 1)])
+    other_b = lax.ppermute(pair[1], ("grp", "seq"), up[:-1] + [(spans - 1, 0)])
     inside, silu, scale = inside_call(
         features, gate_input, rate_forward, rate_backward,
-        b_forward, c_forward, b_backward, c_backward,
+        b_forward, c_forward, b_backward, c_backward, out_weight,
     )
+    states = (pair, from_last, from_next, other_f, other_b)
     return final_call(
-        inside, silu, scale, m, c_forward, c_backward, norm_gain.reshape(1, E), out_weight
+        place, inside, silu, scale, states, c_forward, c_backward,
+        norm_gain.reshape(1, E), out_weight,
     )
 
 

time: 105 us -> 109 us (1.038)
  the two profiles are of different devices: /device:TPU:32 before, /device:TPU:1 now
where the time goes in v2:
time: 109 us
  blocking collectives  61.1 us (56%)
  starting transfers between devices  19.6 us (18%)
  Pallas kernels  16.9 us (16%)
  waiting for transfers between devices  9.69 us (9%)
  local copies, waits for them, and re-layouts  1.16 us (1%)
    all_to_all x1, blocking collectives, per_device(): parts = lax.all_to_all(parts, 'seq', 0, 0, tiled=True)  29.3 us
    all_to_all x1, blocking collectives, per_device(): pair = lax.all_to_all(entries, 'seq', 0, 0, tiled=True)  19.4 us
    all_to_all x1, blocking collectives, per_device(): totals = lax.all_to_all(totals, 'grp', 0, 0, tiled=True)  12.4 us
    ppermute x1, starting transfers between devices, per_device(): from_next = lax.ppermute(to_last, ('grp', 'seq'), down[1:])  8.87 us
    pallas_call x1, Pallas kernels, inside_call(): pl.pallas_call(inside_kernel, grid=(STEPS,), in_specs=[columns, columns,...  6.46 us
    ppermute x1, starting transfers between devices, per_device(): other_f = lax.ppermute(pair[0], ('grp', 'seq'), down[1:] + [(0, spans - 1)])  6.31 us
    ppermute x1, waiting for transfers between devices, per_device(): from_last = lax.ppermute(to_next, ('grp', 'seq'), up[:-1])  4.98 us
    pallas_call x1, Pallas kernels, state_call(): pl.pallas_call(state_kernel, in_specs=[pl.BlockSpec(memory_space=pltpu.SM...  4.72 us
  transfers between devices with their start and end apart: 4, of which 2 were waited for; matrix products, arithmetic and copies ran while one was open for 0% of the time, Pallas kernels for 6%

profile of v2, /device:TPU:1, one launch (start us, length us, event | category | flops | bytes accessed | tf_op | source)
XLA Modules:
  0.0 109.2 jit_solution(16322046641413085449)
XLA Ops:
  0.0 0.6 pad_add_fusion.place_ref
  0.6 0.0 copy-start.10
  0.6 4.7 %span_states.1 = (bf16[2,8,144,128]{3,2,1,0:T(8,128)(2,1)}, bf16[8,144,128]{2,1,0:T(8,128)(2,1)}, bf16[8,144,128]{2,1,0:T(8,128)(2,1)}) custom-call(s32[3]{0:T(128)} %pad_add_fusion.place_ref, bf16[256,2048]{1,0:T(8,128)(2,1)} %x_hbm.1, f32[32,256]{1,0:T(8,128)} %rf_hbm.1, f32[32,256]{1,0:T(8,128)} %rb_hbm.1, bf16[256,128]{1,0:T(8,128)(2,1)} %bf_hbm.1, ...), custom_call_target="tpu_custom_call" | custom-call | tf_op jit(solution)/shard_map/span_states/pallas_call | solution.py:128
  5.3 4.4 %collective-permute-start = (bf16[8,144,128]{2,1,0:T(8,128)(2,1)}, bf16[8,144,128]{2,1,0:T(8,128)(2,1)S(1)}, u32[]{:S(2)}, u32[]{:S(2)}) collective-permute-start(bf16[8,144,128]{2,1,0:T(8,128)(2,1)} %get-tuple-element.15), channel_id=1, source_target_pairs={{0,1},{1,2},{2,3},{3,4},{4,5},{5,6},{6,7},{7,8},{8,9},{9,10},{10,1... | collective-permute-start | bytes 884744 | tf_op jit(solution)/shard_map/ppermute | solution.py:362
  9.7 8.9 %collective-permute-start.1 = (bf16[8,144,128]{2,1,0:T(8,128)(2,1)}, bf16[8,144,128]{2,1,0:T(8,128)(2,1)S(1)}, u32[]{:S(2)}, u32[]{:S(2)}) collective-permute-start(bf16[8,144,128]{2,1,0:T(8,128)(2,1)} %get-tuple-element.16), channel_id=1, source_target_pairs={{1,0},{2,1},{3,2},{4,3},{5,4},{6,5},{7,6},{8,7},{9,8},{10,9},{11,1... | collective-permute-start | bytes 884744 | tf_op jit(solution)/shard_map/ppermute | solution.py:363
  18.6 5.0 %collective-permute-done.from_last_ref = bf16[8,144,128]{2,1,0:T(8,128)(2,1)S(1)} collective-permute-done((bf16[8,144,128]{2,1,0:T(8,128)(2,1)}, bf16[8,144,128]{2,1,0:T(8,128)(2,1)S(1)}, u32[]{:S(2)}, u32[]{:S(2)}) %collective-permute-start) | collective-permute-done | bytes 294944 | tf_op jit(solution)/shard_map/ppermute | solution.py:362
  23.6 0.0 collective-permute-done.1.from_next_ref
  23.6 0.0 copy-start.3
  23.6 1.1 copy-done.3
  24.6 0.0 copy-start
  24.6 0.0 copy-start.1
  24.6 0.0 copy-start.2
  24.7 0.0 copy-start.4
  24.7 0.0 copy-start.5
  24.7 0.0 copy-start.6
  24.7 0.0 copy-start.7
  24.7 0.0 copy-start.8
  24.7 0.0 copy-start.9
  24.7 0.2 pair_totals.1
  24.9 29.3 %all_to_all.15.parts_ref = bf16[32,80,128]{2,1,0:T(8,128)(2,1)S(1)} all-to-all(bf16[32,80,128]{2,1,0:T(8,128)(2,1)S(1)} %pair_totals.1), channel_id=1, replica_groups=mesh['grp'=8,'seq'=32] {'seq'}, dimensions={0} | all-to-all | bytes 1310720 | tf_op jit(solution)/shard_map/all_to_all | solution.py:365
  54.2 0.0 copy-done.10
  54.2 0.7 group_totals.1
  55.0 12.4 %all_to_all.16.totals_ref = bf16[8,160,128]{2,1,0:T(8,128)(2,1)S(1)} all-to-all(bf16[8,160,128]{2,1,0:T(8,128)(2,1)S(1)} %group_totals.1), channel_id=1, replica_groups=mesh['grp'=8,'seq'=32] {'grp'}, dimensions={0} | all-to-all | bytes 655360 | tf_op jit(solution)/shard_map/all_to_all | solution.py:374
  67.3 0.7 entry_states.1
  68.1 0.0 copy-start.11
  68.1 19.4 %all_to_all.17 = bf16[32,64,128]{2,1,0:T(8,128)(2,1)S(1)} all-to-all(bf16[32,64,128]{2,1,0:T(8,128)(2,1)S(1)} %entry_states.1), channel_id=1, replica_groups=mesh['grp'=8,'seq'=32] {'seq'}, dimensions={0} | all-to-all | bytes 1048576 | tf_op jit(solution)/shard_map/all_to_all | solution.py:383
  87.6 6.3 %collective-permute-start.2 = (bf16[8,128,128]{2,1,0:T(8,128)(2,1)S(1)}, bf16[8,128,128]{2,1,0:T(8,128)(2,1)S(1)}, u32[]{:S(2)}, u32[]{:S(2)}) collective-permute-start(bf16[8,128,128]{2,1,0:T(8,128)(2,1)S(1)} %bitcast.10), channel_id=1, source_target_pairs={{1,0},{2,1},{3,2},{4,3},{5,4},{6,5},{7,6},{8,7},{9,8},{10,9},{11,1... | collective-permute-start | bytes 786440 | tf_op jit(solution)/shard_map/ppermute | solution.py:385
  93.9 0.0 collective-permute-start.3
  93.9 0.0 copy-done
  93.9 0.0 copy-done.1
  93.9 0.0 copy-done.2
  93.9 0.0 copy-done.4
  93.9 0.0 copy-done.5
  93.9 0.0 copy-done.6
  93.9 0.0 copy-done.7
  94.0 0.0 copy-done.8
  94.0 0.0 copy-done.9
  94.0 6.5 %inside_spans.1 = (bf16[256,2048]{1,0:T(8,128)(2,1)S(1)}, bf16[256,2048]{1,0:T(8,128)(2,1)S(1)}, bf16[256,128]{1,0:T(8,128)(2,1)S(1)}) custom-call(bf16[256,2048]{1,0:T(8,128)(2,1)S(1)} %copy-done.1, bf16[256,2048]{1,0:T(8,128)(2,1)S(1)} %copy-done.2, f32[32,256]{1,0:T(8,128)S(1)} %copy-done.8, f32[32,256]{1,0:T(8,128)S(1)} %copy-done.9, ...), custom_call_target="tpu_custom_call" | custom-call | flops 536870912 | bytes 4194304 | tf_op jit(solution)/shard_map/inside_spans/pallas_call | solution.py:219
  100.4 0.0 collective-permute-done.2.other_f_ref
  100.4 4.7 %collective-permute-done.3.other_b_ref = bf16[8,128,128]{2,1,0:T(8,128)(2,1)S(1)} collective-permute-done((bf16[8,128,128]{2,1,0:T(8,128)(2,1)S(1)}, bf16[8,128,128]{2,1,0:T(8,128)(2,1)S(1)}, u32[]{:S(2)}, u32[]{:S(2)}) %collective-permute-start.3) | collective-permute-done | bytes 262176 | tf_op jit(solution)/shard_map/ppermute | solution.py:386
  105.2 0.0 copy-done.11
  105.2 4.0 %gate_norm_project.1 = bf16[256,1024]{1,0:T(8,128)(2,1)} custom-call(s32[3]{0:T(128)S(1)} %copy-done.10, bf16[256,2048]{1,0:T(8,128)(2,1)S(1)} %get-tuple-element.11.in_ref, bf16[256,2048]{1,0:T(8,128)(2,1)S(1)} %get-tuple-element.12.silu_ref, bf16[256,128]{1,0:T(8,128)(2,1)S(1)} %get-tuple-element.13.scale_ref, bf16[2,8,128,128]{3,2,1,0:T(8,128)(2,1)S(1)} %bitcast.7, ...), custom_call_target="tpu_custom_call" | custom-call | tf_op jit(solution)/shard_map/gate_norm_project/pallas_call | solution.py:332
  (1 shorter events, 0.0 us)
Async XLA Ops:
  0.6 53.6 %copy-start.10 = (s32[3]{0:T(128)S(1)}, s32[3]{0:T(128)}, u32[]{:S(2)}) copy-start(s32[3]{0:T(128)} %pad_add_fusion.place_ref) | copy-start | bytes 40
  5.3 18.2 %collective-permute-start = (bf16[8,144,128]{2,1,0:T(8,128)(2,1)}, bf16[8,144,128]{2,1,0:T(8,128)(2,1)S(1)}, u32[]{:S(2)}, u32[]{:S(2)}) collective-permute-start(bf16[8,144,128]{2,1,0:T(8,128)(2,1)} %get-tuple-element.15), channel_id=1, source_target_pairs={{0,1},{1,2},{2,3},{3,4},{4,5},{5,6},{6,7},{7,8},{8,9},{9,10},{10,1... | collective-permute-start | bytes 884744 | tf_op jit(solution)/shard_map/ppermute | solution.py:362
  9.7 13.9 %collective-permute-start.1 = (bf16[8,144,128]{2,1,0:T(8,128)(2,1)}, bf16[8,144,128]{2,1,0:T(8,128)(2,1)S(1)}, u32[]{:S(2)}, u32[]{:S(2)}) collective-permute-start(bf16[8,144,128]{2,1,0:T(8,128)(2,1)} %get-tuple-element.16), channel_id=1, source_target_pairs={{1,0},{2,1},{3,2},{4,3},{5,4},{6,5},{7,6},{8,7},{9,8},{10,9},{11,1... | collective-permute-start | bytes 884744 | tf_op jit(solution)/shard_map/ppermute | solution.py:363
  23.6 1.1 copy-start.3
  24.6 69.2 %copy-start = (bf16[2048,1024]{1,0:T(8,128)(2,1)S(1)}, bf16[2048,1024]{1,0:T(8,128)(2,1)}, u32[]{:S(2)}) copy-start(bf16[2048,1024]{1,0:T(8,128)(2,1)} %w_ref.3) | copy-start | bytes 12582916
  24.6 69.3 %copy-start.1 = (bf16[256,2048]{1,0:T(8,128)(2,1)S(1)}, bf16[256,2048]{1,0:T(8,128)(2,1)}, u32[]{:S(2)}) copy-start(bf16[256,2048]{1,0:T(8,128)(2,1)} %x_hbm.1) | copy-start | bytes 3145732
  24.6 69.3 %copy-start.2 = (bf16[256,2048]{1,0:T(8,128)(2,1)S(1)}, bf16[256,2048]{1,0:T(8,128)(2,1)}, u32[]{:S(2)}) copy-start(bf16[256,2048]{1,0:T(8,128)(2,1)} %gate_ref.1) | copy-start | bytes 3145732
  24.7 69.3 %copy-start.4 = (bf16[256,128]{1,0:T(8,128)(2,1)S(1)}, bf16[256,128]{1,0:T(8,128)(2,1)}, u32[]{:S(2)}) copy-start(bf16[256,128]{1,0:T(8,128)(2,1)} %cf_ref.3) | copy-start | bytes 196612
  24.7 69.3 %copy-start.5 = (bf16[256,128]{1,0:T(8,128)(2,1)S(1)}, bf16[256,128]{1,0:T(8,128)(2,1)}, u32[]{:S(2)}) copy-start(bf16[256,128]{1,0:T(8,128)(2,1)} %cb_ref.3) | copy-start | bytes 196612
  24.7 69.3 %copy-start.6 = (bf16[256,128]{1,0:T(8,128)(2,1)S(1)}, bf16[256,128]{1,0:T(8,128)(2,1)}, u32[]{:S(2)}) copy-start(bf16[256,128]{1,0:T(8,128)(2,1)} %bf_hbm.1) | copy-start | bytes 196612
  24.7 69.3 %copy-start.7 = (bf16[256,128]{1,0:T(8,128)(2,1)S(1)}, bf16[256,128]{1,0:T(8,128)(2,1)}, u32[]{:S(2)}) copy-start(bf16[256,128]{1,0:T(8,128)(2,1)} %bb_hbm.1) | copy-start | bytes 196612
  24.7 69.3 %copy-start.8 = (f32[32,256]{1,0:T(8,128)S(1)}, f32[32,256]{1,0:T(8,128)}, u32[]{:S(2)}) copy-start(f32[32,256]{1,0:T(8,128)} %rf_hbm.1) | copy-start | bytes 98308
  24.7 69.3 %copy-start.9 = (f32[32,256]{1,0:T(8,128)S(1)}, f32[32,256]{1,0:T(8,128)}, u32[]{:S(2)}) copy-start(f32[32,256]{1,0:T(8,128)} %rb_hbm.1) | copy-start | bytes 98308
  68.1 37.1 %copy-start.11 = (f32[2048]{0:T(1024)S(1)}, f32[2048]{0:T(1024)}, u32[]{:S(2)}) copy-start(f32[2048]{0:T(1024)} %param.18) | copy-start | bytes 24580
  87.6 12.9 %collective-permute-start.2 = (bf16[8,128,128]{2,1,0:T(8,128)(2,1)S(1)}, bf16[8,128,128]{2,1,0:T(8,128)(2,1)S(1)}, u32[]{:S(2)}, u32[]{:S(2)}) collective-permute-start(bf16[8,128,128]{2,1,0:T(8,128)(2,1)S(1)} %bitcast.10), channel_id=1, source_target_pairs={{1,0},{2,1},{3,2},{4,3},{5,4},{6,5},{7,6},{8,7},{9,8},{10,9},{11,1... | collective-permute-start | bytes 786440 | tf_op jit(solution)/shard_map/ppermute | solution.py:385
  93.9 11.3 %collective-permute-start.3 = (bf16[8,128,128]{2,1,0:T(8,128)(2,1)S(1)}, bf16[8,128,128]{2,1,0:T(8,128)(2,1)S(1)}, u32[]{:S(2)}, u32[]{:S(2)}) collective-permute-start(bf16[8,128,128]{2,1,0:T(8,128)(2,1)S(1)} %bitcast.9), channel_id=1, source_target_pairs={{0,1},{1,2},{2,3},{3,4},{4,5},{5,6},{6,7},{7,8},{8,9},{9,10},{10,1... | collective-permute-start | bytes 786440 | tf_op jit(solution)/shard_map/ppermute | solution.py:386

commit v3 on v1

--- a/solution.py
+++ b/solution.py
@@ -77,7 +77,7 @@
 
 
 def state_kernel(
-    x_hbm, rf_hbm, rb_hbm, bf_hbm, bb_hbm, out_ref,
+    x_hbm, rf_hbm, rb_hbm, bf_hbm, bb_hbm, out_ref, total_ref,
     x_ref, r_ref, b_ref, scale_ref, sems,
 ):
     copies = [
@@ -91,37 +91,38 @@
         copy.start()
     copies[0].wait()
     copies[1].wait()
-    parts, keeps = [], []
+    row = lax.broadcasted_iota(jnp.int32, (H, 128), 0)
+    lane = lax.broadcasted_iota(jnp.int32, (H, 128), 1)
+    parts, totals = [], 0.0
     for d, sums in enumerate((lane_sums, lane_sums_back)):
         r = r_ref[d]
         c = sums(r)
         total = c[:, Q - 1 : Q] if d == 0 else c[:, 0:1]
         parts += two_parts(step_of(r) * jnp.exp(c - total))
-        keeps.append(jnp.broadcast_to(jnp.exp(-total), (H, E)))
+        totals = totals + jnp.where(lane == row + H * d, total, 0.0)
+    total_ref[...] = jnp.sum(totals, axis=0, keepdims=True)
     scale_ref[...] = jnp.concatenate(parts, axis=0).T.astype(BF16)
     copies[2].wait()
     copies[3].wait()
     turned = [b_ref[d].astype(F32).T.astype(BF16) for d in range(2)]
     copies[4].wait()
     x = x_ref[...].astype(F32)
-    head = lax.broadcasted_iota(jnp.int32, (H, E), 0)
-    column = lax.broadcasted_iota(jnp.int32, (H, E), 1)
     for d in range(2):
         factor = dot(scale_ref[...], head_select(0, 4 * H, E, 2 * H * d, 2))
         s = dot(turned[d], (x * factor).astype(BF16)).astype(BF16)
-        keep = jnp.where(head == column // HEAD, keeps[d], 0.0)
-        tail = three_rows(jnp.sum(keep, axis=0, keepdims=True), E)
         for k in range(E // 128):
-            out_ref[d, k, 0:N, :] = s[:, 128 * k : 128 * (k + 1)]
-            out_ref[d, k, N:ROWS, :] = tail[:, 128 * k : 128 * (k + 1)]
+            out_ref[d, k] = s[:, 128 * k : 128 * (k + 1)]
 
 
 def state_call(x, rate_f, rate_b, b_f, b_b):
     return pl.pallas_call(
         state_kernel,
         in_specs=[pl.BlockSpec(memory_space=pltpu.HBM)] * 5,
-        out_specs=pl.BlockSpec(memory_space=pltpu.VMEM),
-        out_shape=jax.ShapeDtypeStruct((2, E // 128, ROWS, 128), BF16),
+        out_specs=[pl.BlockSpec(memory_space=pltpu.VMEM)] * 2,
+        out_shape=[
+            jax.ShapeDtypeStruct((2, E // 128, N, 128), BF16),
+            jax.ShapeDtypeStruct((1, 128), F32),
+        ],
         scratch_shapes=[
             pltpu.VMEM((Q, E), BF16),
             pltpu.VMEM((2, H, Q), F32),
@@ -129,13 +130,13 @@
             pltpu.VMEM((Q, 4 * H), BF16),
             pltpu.SemaphoreType.DMA((5,)),
         ],
-        compiler_params=LIMIT,
+        compiler_params=pltpu.CompilerParams(vmem_limit_bytes=60 * 1024 * 1024),
         name="span_states",
     )(x, rate_f, rate_b, b_f, b_b)
 
 
 def inside_kernel(
-    x_ref, gate_ref, rf_ref, rb_ref, bf_ref, cf_ref, bb_ref, cb_ref,
+    x_ref, gate_ref, rf_ref, rb_ref, bf_ref, cf_ref, bb_ref, cb_ref, w_ref,
     out_ref, silu_ref, scale_ref, score_ref, rows_ref, cols_ref,
 ):
     j = pl.program_id(0)
@@ -179,13 +180,14 @@
         out_ref[:, 128 * p : 128 * (p + 1)] = y.astype(BF16)
 
 
-def inside_call(x, gate, rate_f, rate_b, b_f, c_f, b_b, c_b):
+def inside_call(x, gate, rate_f, rate_b, b_f, c_f, b_b, c_b, weight):
     whole = lambda shape: pl.BlockSpec(shape, lambda j: (0,) * len(shape))
     columns = pl.BlockSpec((Q, BLK), lambda j: (0, j))
     return pl.pallas_call(
         inside_kernel,
         grid=(STEPS,),
-        in_specs=[columns, columns, whole((H, Q)), whole((H, Q))] + [whole((Q, N))] * 4,
+        in_specs=[columns, columns, whole((H, Q)), whole((H, Q))] + [whole((Q, N))] * 4
+        + [pl.BlockSpec(memory_space=pltpu.VMEM)],
         out_specs=[columns, columns, whole((Q, 4 * H))],
         out_shape=[jax.ShapeDtypeStruct((Q, E), BF16)] * 2
         + [jax.ShapeDtypeStruct((Q, 4 * H), BF16)],
@@ -199,7 +201,7 @@
             flops=2 * H * Q * Q * 128, bytes_accessed=4 * Q * E * 2, transcendentals=H * Q * Q
         ),
         name="inside_spans",
-    )(x, gate, rate_f, rate_b, b_f, c_f, b_b, c_b)
+    )(x, gate, rate_f, rate_b, b_f, c_f, b_b, c_b, weight)
 
 
 def read_part(ref, index):
@@ -208,14 +210,23 @@
     return state, tail[0:1] + tail[1:2] + tail[2:3]
 
 
-def total_kernel(count, copies, place_ref, parts_ref, out_ref):
+def owned_decays(first, logs_ref, keep_ref):
+    lane = lax.broadcasted_iota(jnp.int32, logs_ref.shape, 1)
+    logs = logs_ref[...]
+    low = jnp.sum(jnp.where(lane == first, logs, 0.0), axis=1, keepdims=True)
+    high = jnp.sum(jnp.where(lane == first + 1, logs, 0.0), axis=1, keepdims=True)
+    keep_ref[...] = jnp.exp(-jnp.where(lane < HEAD, low, high))
+
+
+def total_kernel(count, copies, place_ref, logs_ref, parts_ref, out_ref, keep_ref):
     backward = place_ref[0]
+    owned_decays(place_ref[2], logs_ref, keep_ref)
 
     def step(i, carried):
         state, kept = carried
         index = jnp.where(backward == 1, count - 1 - i, i)
-        own, keep = read_part(parts_ref, index)
-        return keep * state + own, keep * kept
+        keep = keep_ref[pl.ds(index, 1), :]
+        return keep * state + parts_ref[index].astype(F32), keep * kept
 
     state, kept = lax.fori_loop(
         0, count, step, (jnp.zeros((N, 128), F32), jnp.ones((1, 128), F32)), unroll=4
@@ -226,8 +237,9 @@
         out_ref[g, N:ROWS, :] = tail
 
 
-def entry_kernel(count, groups, place_ref, totals_ref, parts_ref, out_ref):
+def entry_kernel(count, groups, place_ref, totals_ref, logs_ref, parts_ref, out_ref, keep_ref):
     backward, mine = place_ref[0], place_ref[1]
+    owned_decays(place_ref[2], logs_ref, keep_ref)
 
     def outer(i, state):
         index = jnp.where(backward == 1, groups - 1 - i, i)
@@ -239,8 +251,7 @@
     def step(i, state):
         index = jnp.where(backward == 1, count - 1 - i, i)
         out_ref[index] = state.astype(BF16)
-        own, keep = read_part(parts_ref, index)
-        return keep * state + own
+        return keep_ref[pl.ds(index, 1), :] * state + parts_ref[index].astype(F32)
 
     lax.fori_loop(0, count, step, state, unroll=4)
 
@@ -289,34 +300,38 @@
     rate_forward, rate_backward, norm_gain, out_weight,
 ):
     count, groups = lax.axis_size("seq"), lax.axis_size("grp")
-    states = state_call(features, rate_forward, rate_backward, b_forward, b_backward)
-    states = states.reshape(count, ROWS, 128)
-    backward = (lax.axis_index("seq") >= count // 2).astype(jnp.int32)
-    group = lax.axis_index("grp")
+    states, logs = state_call(features, rate_forward, rate_backward, b_forward, b_backward)
+    states = states.reshape(count, N, 128)
+    member, group = lax.axis_index("seq"), lax.axis_index("grp")
+    backward = (member >= count // 2).astype(jnp.int32)
     mine = jnp.where(backward == 1, groups - 1 - group, group)
-    place = jnp.stack([backward, mine]).astype(jnp.int32)
+    place = jnp.stack([backward, mine, 2 * member]).astype(jnp.int32)
     parts = lax.all_to_all(states, "seq", 0, 0, tiled=True)
+    logs = lax.all_gather(logs, "seq", tiled=True)
+    keep = pltpu.VMEM((count, 128), F32)
     totals = pl.pallas_call(
         functools.partial(total_kernel, count, groups),
-        in_specs=vmem_specs(1),
+        in_specs=vmem_specs(2),
         out_specs=pl.BlockSpec(memory_space=pltpu.VMEM),
         out_shape=jax.ShapeDtypeStruct((groups, ROWS, 128), BF16),
+        scratch_shapes=[keep],
         compiler_params=LIMIT,
         name="group_totals",
-    )(place, parts)
+    )(place, logs, parts)
     totals = lax.all_to_all(totals, "grp", 0, 0, tiled=True)
     entries = pl.pallas_call(
         functools.partial(entry_kernel, count, groups),
-        in_specs=vmem_specs(2),
+        in_specs=vmem_specs(3),
         out_specs=pl.BlockSpec(memory_space=pltpu.VMEM),
         out_shape=jax.ShapeDtypeStruct((count, N, 128), BF16),
+        scratch_shapes=[keep],
         compiler_params=LIMIT,
         name="entry_states",
-    )(place, totals, parts)
+    )(place, totals, logs, parts)
     m = lax.all_to_all(entries, "seq", 0, 0, tiled=True).reshape(2, E // 128, N, 128)
     inside, silu, scale = inside_call(
         features, gate_input, rate_forward, rate_backward,
-        b_forward, c_forward, b_backward, c_backward,
+        b_forward, c_forward, b_backward, c_backward, out_weight,
     )
     return final_call(
         inside, silu, scale, m, c_forward, c_backward, norm_gain.reshape(1, E), out_weight

time: 105 us -> 130 us (1.24)
  blocking collectives: 12 us -> 67.7 us
  waiting for transfers between devices: 50.8 us -> 18 us
  starting transfers between devices: 16.9 us -> 18.4 us
    all_gather x0 -> x1, blocking collectives: none -> 55.7 us  [per_device(): logs = lax.all_gather(logs, 'seq', tiled=True)]
    all_to_all x1, waiting for transfers between devices: 31.1 us -> 0.01 us  [per_device(): parts = lax.all_to_all(states, 'seq', 0, 0, tiled=True)]
    all_to_all x1, waiting for transfers between devices: 19.6 us -> 18 us  [per_device(): lax.all_to_all(entries, 'seq', 0, 0, tiled=True)]
  transfers between devices with their start and end apart: 2 -> 2, of which waited for: 2 -> 1; matrix products, arithmetic and copies ran while one was open for 0% -> 0% of each run, Pallas kernels for 6% -> 5%
where the time goes in v3:
time: 130 us; the launch traced here: 129 us
  blocking collectives  67.7 us (52%)
  starting transfers between devices  18.4 us (14%)
  waiting for transfers between devices  18 us (14%)
  Pallas kernels  16.1 us (12%)
  local copies, waits for them, and re-layouts  8.84 us (7%)
    all_gather x1, blocking collectives, per_device(): logs = lax.all_gather(logs, 'seq', tiled=True)  55.7 us
    all_to_all x1, waiting for transfers between devices, per_device(): lax.all_to_all(entries, 'seq', 0, 0, tiled=True)  18 us
    all_to_all x1, blocking collectives, per_device(): totals = lax.all_to_all(totals, 'grp', 0, 0, tiled=True)  12 us
    all_to_all x1, starting transfers between devices, per_device(): parts = lax.all_to_all(states, 'seq', 0, 0, tiled=True)  11.5 us
    unnamed x30, local copies, waits for them, and re-layouts  8.84 us
    all_to_all x1, starting transfers between devices, per_device(): lax.all_to_all(entries, 'seq', 0, 0, tiled=True)  6.86 us
    pallas_call x1, Pallas kernels, inside_call(): pl.pallas_call(inside_kernel, grid=(STEPS,), in_specs=[columns, columns,...  6.44 us
    pallas_call x1, Pallas kernels, state_call(): pl.pallas_call(state_kernel, in_specs=[pl.BlockSpec(memory_space=pltpu.HB...  3.63 us
  transfers between devices with their start and end apart: 2, of which 1 were waited for; matrix products, arithmetic and copies ran while one was open for 0% of the time, Pallas kernels for 5%

profile of v3, /device:TPU:32, one launch (start us, length us, event | category | flops | bytes accessed | tf_op | source)
XLA Modules:
  0.0 129.3 jit_solution(13791107993350129310)
XLA Ops:
  0.0 3.6 %span_states.1 = (bf16[2,16,128,128]{3,2,1,0:T(8,128)(2,1)}, f32[1,128]{1,0:T(1,128)}) custom-call(bf16[256,2048]{1,0:T(8,128)(2,1)} %x_hbm.1, f32[32,256]{1,0:T(8,128)} %rf_hbm.1, f32[32,256]{1,0:T(8,128)} %rb_hbm.1, bf16[256,128]{1,0:T(8,128)(2,1)} %bf_hbm.1, bf16[256,128]{1,0:T(8,128)(2,1)} %bb_hbm.1), custom_call_target="tpu_custom_call" | custom-call | tf_op jit(solution)/shard_map/span_states/pallas_call | solution.py:118
  3.6 0.0 copy-start.2
  3.6 0.0 copy-start.3
  3.7 0.0 copy-start.8
  3.7 0.0 copy-start.9
  3.7 0.0 copy-start.10
  3.7 0.0 copy-start.11
  3.7 0.0 copy-start.12
  3.7 0.0 copy-start.13
  3.7 11.5 %all-to-all-start = ((bf16[32,128,128]{2,1,0:T(8,128)(2,1)}), bf16[32,128,128]{2,1,0:T(8,128)(2,1)S(1)}, u32[]{:S(2)}, u32[]{:S(2)}) async-start(bf16[32,128,128]{2,1,0:T(8,128)(2,1)} %bitcast.12), calls=%async_computation | async-start | bytes 2097152 | tf_op jit(solution)/shard_map/all_to_all | solution.py:309
  15.3 55.7 %all-gather = f32[32,1,128]{2,1,0:T(1,128)S(1)} all-gather(f32[1,1,128]{2,1,0:T(1,128)} %bitcast.13), channel_id=1, replica_groups=mesh['grp'=8,'seq'=32] {'seq'}, dimensions={0}, use_global_device_ids=true | all-gather | bytes 16896 | tf_op jit(solution)/shard_map/all_gather | solution.py:310
  71.0 0.1 pad_add_fusion.place_ref
  71.1 0.0 all-to-all-done.parts_ref
  71.1 0.9 group_totals.1
  72.0 12.0 %all_to_all.15.totals_ref = bf16[8,144,128]{2,1,0:T(8,128)(2,1)S(1)} all-to-all(bf16[8,144,128]{2,1,0:T(8,128)(2,1)S(1)} %group_totals.1), channel_id=1, replica_groups=mesh['grp'=8,'seq'=32] {'grp'}, dimensions={0} | all-to-all | bytes 589824 | tf_op jit(solution)/shard_map/all_to_all | solution.py:321
  84.0 1.9 %entry_states.1 = bf16[32,128,128]{2,1,0:T(8,128)(2,1)} custom-call(s32[3]{0:T(128)S(1)} %pad_add_fusion.place_ref, bf16[8,144,128]{2,1,0:T(8,128)(2,1)S(1)} %all_to_all.15.totals_ref, f32[32,128]{1,0:T(8,128)S(1)} %bitcast.10, bf16[32,128,128]{2,1,0:T(8,128)(2,1)S(1)} %all-to-all-done.parts_ref), custom_call_target="tpu_custom_call" | custom-call | tf_op jit(solution)/shard_map/entry_states/pallas_call | solution.py:322
  85.9 0.0 copy-start.14
  85.9 6.9 %all-to-all-start.2 = ((bf16[32,128,128]{2,1,0:T(8,128)(2,1)}), bf16[32,128,128]{2,1,0:T(8,128)(2,1)S(1)}, u32[]{:S(2)}, u32[]{:S(2)}) async-start(bf16[32,128,128]{2,1,0:T(8,128)(2,1)} %entry_states.1), calls=%async_computation.2 | async-start | bytes 2097152 | tf_op jit(solution)/shard_map/all_to_all | solution.py:331
  92.8 0.0 copy-done.2
  92.8 0.0 copy-done.3
  92.8 0.0 copy-done.8
  92.8 0.0 copy-done.9
  92.8 0.0 copy-done.10
  92.8 0.0 copy-done.11
  92.8 0.0 copy-done.12
  92.8 0.0 copy-done.13
  92.8 0.0 copy-start
  92.9 2.2 %copy-done = bf16[2048,1024]{1,0:T(8,128)(2,1)S(1)} copy-done((bf16[2048,1024]{1,0:T(8,128)(2,1)S(1)}, bf16[2048,1024]{1,0:T(8,128)(2,1)}, u32[]{:S(2)}) %copy-start) | copy-done | bytes 4194328
  95.0 6.4 %inside_spans.1 = (bf16[256,2048]{1,0:T(8,128)(2,1)S(1)}, bf16[256,2048]{1,0:T(8,128)(2,1)S(1)}, bf16[256,128]{1,0:T(8,128)(2,1)S(1)}) custom-call(bf16[256,2048]{1,0:T(8,128)(2,1)S(1)} %copy-done.2, bf16[256,2048]{1,0:T(8,128)(2,1)S(1)} %copy-done.3, f32[32,256]{1,0:T(8,128)S(1)} %copy-done.12, f32[32,256]{1,0:T(8,128)S(1)} %copy-done.13, ...), custom_call_target="tpu_custom_call" | custom-call | flops 536870912 | bytes 4194304 | tf_op jit(solution)/shard_map/inside_spans/pallas_call | solution.py:186
  101.5 0.0 copy-start.4
  101.5 1.0 copy-done.4
  102.5 0.0 copy-start.6
  102.5 1.0 copy-done.6
  103.5 18.0 %all-to-all-done.2 = bf16[32,128,128]{2,1,0:T(8,128)(2,1)S(1)} async-done(((bf16[32,128,128]{2,1,0:T(8,128)(2,1)}), bf16[32,128,128]{2,1,0:T(8,128)(2,1)S(1)}, u32[]{:S(2)}, u32[]{:S(2)}) %all-to-all-start.2) | async-done | bytes 1048608 | tf_op jit(solution)/shard_map/all_to_all | solution.py:331
  121.4 0.0 copy-done.14
  121.4 0.0 copy-start.1
  121.4 2.2 %copy-done.1 = bf16[2048,1024]{1,0:T(8,128)(2,1)S(1)} copy-done((bf16[2048,1024]{1,0:T(8,128)(2,1)S(1)}, bf16[2048,1024]{1,0:T(8,128)(2,1)}, u32[]{:S(2)}) %copy-start.1) | copy-done | bytes 4194328
  123.6 0.0 copy-start.5
  123.6 1.2 copy-done.5
  124.8 0.0 copy-start.7
  124.8 1.2 copy-done.7
  126.1 3.3 %gate_norm_project.1 = bf16[256,1024]{1,0:T(8,128)(2,1)} custom-call(bf16[256,2048]{1,0:T(8,128)(2,1)S(1)} %copy-done.5, bf16[256,2048]{1,0:T(8,128)(2,1)S(1)} %copy-done.7, bf16[256,128]{1,0:T(8,128)(2,1)S(1)} %get-tuple-element.12.scale_ref, bf16[2,16,128,128]{3,2,1,0:T(8,128)(2,1)S(1)} %bitcast.8, bf16[256,128]{1,0:T(8,128)(2,1)S(1)} %copy-done.8, ...), custom_call_target="tpu_custom_call" | custom-call | tf_op jit(solution)/shard_map/gate_norm_project/pallas_call | solution.py:287
Async XLA Ops:
  3.6 89.1 %copy-start.2 = (bf16[256,2048]{1,0:T(8,128)(2,1)S(1)}, bf16[256,2048]{1,0:T(8,128)(2,1)}, u32[]{:S(2)}) copy-start(bf16[256,2048]{1,0:T(8,128)(2,1)} %x_hbm.1) | copy-start | bytes 3145732
  3.6 89.1 %copy-start.3 = (bf16[256,2048]{1,0:T(8,128)(2,1)S(1)}, bf16[256,2048]{1,0:T(8,128)(2,1)}, u32[]{:S(2)}) copy-start(bf16[256,2048]{1,0:T(8,128)(2,1)} %gate_ref.1) | copy-start | bytes 3145732
  3.7 89.1 %copy-start.8 = (bf16[256,128]{1,0:T(8,128)(2,1)S(1)}, bf16[256,128]{1,0:T(8,128)(2,1)}, u32[]{:S(2)}) copy-start(bf16[256,128]{1,0:T(8,128)(2,1)} %cf_ref.3) | copy-start | bytes 196612
  3.7 89.1 %copy-start.9 = (bf16[256,128]{1,0:T(8,128)(2,1)S(1)}, bf16[256,128]{1,0:T(8,128)(2,1)}, u32[]{:S(2)}) copy-start(bf16[256,128]{1,0:T(8,128)(2,1)} %cb_ref.3) | copy-start | bytes 196612
  3.7 89.1 %copy-start.10 = (bf16[256,128]{1,0:T(8,128)(2,1)S(1)}, bf16[256,128]{1,0:T(8,128)(2,1)}, u32[]{:S(2)}) copy-start(bf16[256,128]{1,0:T(8,128)(2,1)} %bf_hbm.1) | copy-start | bytes 196612
  3.7 89.1 %copy-start.11 = (bf16[256,128]{1,0:T(8,128)(2,1)S(1)}, bf16[256,128]{1,0:T(8,128)(2,1)}, u32[]{:S(2)}) copy-start(bf16[256,128]{1,0:T(8,128)(2,1)} %bb_hbm.1) | copy-start | bytes 196612
  3.7 89.1 %copy-start.12 = (f32[32,256]{1,0:T(8,128)S(1)}, f32[32,256]{1,0:T(8,128)}, u32[]{:S(2)}) copy-start(f32[32,256]{1,0:T(8,128)} %rf_hbm.1) | copy-start | bytes 98308
  3.7 89.1 %copy-start.13 = (f32[32,256]{1,0:T(8,128)S(1)}, f32[32,256]{1,0:T(8,128)}, u32[]{:S(2)}) copy-start(f32[32,256]{1,0:T(8,128)} %rb_hbm.1) | copy-start | bytes 98308
  3.7 67.3 %all-to-all-start = ((bf16[32,128,128]{2,1,0:T(8,128)(2,1)}), bf16[32,128,128]{2,1,0:T(8,128)(2,1)S(1)}, u32[]{:S(2)}, u32[]{:S(2)}) async-start(bf16[32,128,128]{2,1,0:T(8,128)(2,1)} %bitcast.12), calls=%async_computation | async-start | bytes 2097152 | tf_op jit(solution)/shard_map/all_to_all | solution.py:309
  85.9 35.5 %copy-start.14 = (f32[2048]{0:T(1024)S(1)}, f32[2048]{0:T(1024)}, u32[]{:S(2)}) copy-start(f32[2048]{0:T(1024)} %param.18) | copy-start | bytes 24580
  85.9 35.5 %all-to-all-start.2 = ((bf16[32,128,128]{2,1,0:T(8,128)(2,1)}), bf16[32,128,128]{2,1,0:T(8,128)(2,1)S(1)}, u32[]{:S(2)}, u32[]{:S(2)}) async-start(bf16[32,128,128]{2,1,0:T(8,128)(2,1)} %entry_states.1), calls=%async_computation.2 | async-start | bytes 2097152 | tf_op jit(solution)/shard_map/all_to_all | solution.py:331
  92.8 2.2 %copy-start = (bf16[2048,1024]{1,0:T(8,128)(2,1)S(1)}, bf16[2048,1024]{1,0:T(8,128)(2,1)}, u32[]{:S(2)}) copy-start(bf16[2048,1024]{1,0:T(8,128)(2,1)} %w_ref.3) | copy-start | bytes 12582916
  101.5 1.0 copy-start.4
  102.5 1.0 copy-start.6
  121.4 2.2 %copy-start.1 = (bf16[2048,1024]{1,0:T(8,128)(2,1)S(1)}, bf16[2048,1024]{1,0:T(8,128)(2,1)}, u32[]{:S(2)}) copy-start(bf16[2048,1024]{1,0:T(8,128)(2,1)} %w_ref.3) | copy-start | bytes 12582916
  123.6 1.2 copy-start.5
  124.8 1.2 copy-start.7

commit v4 on v1

--- a/solution.py
+++ b/solution.py
@@ -15,6 +15,7 @@
 BLK = 256
 STEPS = E // BLK
 FW = 256
+FINAL_VMEM = 59400000
 HPB = BLK // HEAD
 ROWS = N + 16
 LOG2E = 1.4426950408889634
@@ -56,12 +57,11 @@
     return high, a - high
 
 
-def head_select(block, rows, width, first, pairs):
-    row = lax.broadcasted_iota(jnp.int32, (rows, width), 0)
+def head_select(block, rows, width, first):
+    row = lax.broadcasted_iota(jnp.int32, (rows, width), 0) - first
     column = lax.broadcasted_iota(jnp.int32, (rows, width), 1)
     head = block * (width // HEAD) + column // HEAD
-    hit = (row % H == head) & (row >= first) & (row < first + pairs * H)
-    return jnp.where(hit, 1.0, 0.0).astype(BF16)
+    return jnp.where((row == head) | (row == head + H), 1.0, 0.0).astype(BF16)
 
 
 def dot(a, b):
@@ -77,8 +77,7 @@
 
 
 def state_kernel(
-    x_hbm, rf_hbm, rb_hbm, bf_hbm, bb_hbm, out_ref,
-    x_ref, r_ref, b_ref, scale_ref, sems,
+    x_hbm, rf_hbm, rb_hbm, bf_hbm, bb_hbm, out_ref, x_ref, r_ref, b_ref, select_ref, sems
 ):
     copies = [
         pltpu.make_async_copy(rf_hbm, r_ref.at[0], sems.at[0]),
@@ -89,31 +88,31 @@
     ]
     for copy in copies:
         copy.start()
+    select_ref[...] = head_select(0, 2 * H, E, 0)
     copies[0].wait()
     copies[1].wait()
-    parts, keeps = [], []
+    scales = []
     for d, sums in enumerate((lane_sums, lane_sums_back)):
         r = r_ref[d]
         c = sums(r)
         total = c[:, Q - 1 : Q] if d == 0 else c[:, 0:1]
-        parts += two_parts(step_of(r) * jnp.exp(c - total))
-        keeps.append(jnp.broadcast_to(jnp.exp(-total), (H, E)))
-    scale_ref[...] = jnp.concatenate(parts, axis=0).T.astype(BF16)
+        parts = two_parts(step_of(r) * jnp.exp(c - total))
+        scales.append(jnp.concatenate(parts, axis=0).T.astype(BF16))
+        keep = jnp.broadcast_to(jnp.exp(-total), (H, 128))
+        lane = lax.broadcasted_iota(jnp.int32, (H, 128), 1)
+        for k in range(E // 128):
+            own = jnp.where(lane < HEAD, keep[2 * k : 2 * k + 1], keep[2 * k + 1 : 2 * k + 2])
+            out_ref[d, k, N:ROWS, :] = three_rows(own[:1], 128)
     copies[2].wait()
     copies[3].wait()
     turned = [b_ref[d].astype(F32).T.astype(BF16) for d in range(2)]
     copies[4].wait()
     x = x_ref[...].astype(F32)
-    head = lax.broadcasted_iota(jnp.int32, (H, E), 0)
-    column = lax.broadcasted_iota(jnp.int32, (H, E), 1)
     for d in range(2):
-        factor = dot(scale_ref[...], head_select(0, 4 * H, E, 2 * H * d, 2))
+        factor = dot(scales[d], select_ref[...])
         s = dot(turned[d], (x * factor).astype(BF16)).astype(BF16)
-        keep = jnp.where(head == column // HEAD, keeps[d], 0.0)
-        tail = three_rows(jnp.sum(keep, axis=0, keepdims=True), E)
         for k in range(E // 128):
             out_ref[d, k, 0:N, :] = s[:, 128 * k : 128 * (k + 1)]
-            out_ref[d, k, N:ROWS, :] = tail[:, 128 * k : 128 * (k + 1)]
 
 
 def state_call(x, rate_f, rate_b, b_f, b_b):
@@ -126,10 +125,10 @@
             pltpu.VMEM((Q, E), BF16),
             pltpu.VMEM((2, H, Q), F32),
             pltpu.VMEM((2, Q, N), BF16),
-            pltpu.VMEM((Q, 4 * H), BF16),
+            pltpu.VMEM((2 * H, E), BF16),
             pltpu.SemaphoreType.DMA((5,)),
         ],
-        compiler_params=LIMIT,
+        compiler_params=pltpu.CompilerParams(vmem_limit_bytes=60 * 1024 * 1024),
         name="span_states",
     )(x, rate_f, rate_b, b_f, b_b)
 
@@ -163,7 +162,7 @@
     gate = gate_ref[...].astype(F32)
     silu_ref[...] = (gate * jax.nn.sigmoid(gate)).astype(BF16)
     cols = cols_ref[...]
-    own = dot(cols.astype(BF16), head_select(j, 4 * H, BLK, 2 * H, 2))
+    own = dot(cols.astype(BF16), head_select(j, 4 * H, BLK, 2 * H))
     cols = pltpu.roll(cols, lax.rem(4 * H - HPB * j, 4 * H), 1)
     lane = lax.broadcasted_iota(jnp.int32, (Q, 128), 1)
     for p in range(HPB // 2):
@@ -250,16 +249,20 @@
 
 
 def final_kernel(
-    in_ref, silu_ref, scale_ref, m_ref, cf_ref, cb_ref, gain_ref, w_ref, out_ref, normed_ref
+    in_ref, silu_ref, scale_ref, m_ref, cf_ref, cb_ref, gain_ref, w_hbm,
+    out_ref, normed_ref, w_ref, sem,
 ):
+    copy = pltpu.make_async_copy(w_hbm, w_ref, sem)
+    copy.start()
+    scales = [scale_ref[:, 2 * H * d : 2 * H * (d + 1)] for d in range(2)]
     square = jnp.zeros((Q, 128), F32)
     for j in range(E // FW):
         at = pl.ds(FW * j, FW)
         y = in_ref[:, at].astype(F32)
+        select = head_select(j, 2 * H, FW, 0)
         for d, c_ref in enumerate((cf_ref, cb_ref)):
-            factor = dot(scale_ref[...], head_select(j, 4 * H, FW, 2 * H * d, 2))
             m = jnp.concatenate([m_ref[d, FW // 128 * j + k] for k in range(FW // 128)], axis=1)
-            y = y + factor * dot(c_ref[...], m)
+            y = y + dot(scales[d], select) * dot(c_ref[...], m)
         gated = y * silu_ref[:, at].astype(F32)
         for k in range(FW // 128):
             part = gated[:, 128 * k : 128 * (k + 1)]
@@ -267,6 +270,7 @@
         normed_ref[:, at] = (gated * gain_ref[:, at]).astype(BF16)
     mean = jnp.sum(square, axis=1, keepdims=True) * (1.0 / E)
     scale = lax.rsqrt(mean + 1e-05)
+    copy.wait()
     for n in range(D // 256):
         at = pl.ds(256 * n, 256)
         out_ref[:, at] = (dot(normed_ref[...], w_ref[:, at]) * scale).astype(BF16)
@@ -275,11 +279,16 @@
 def final_call(inside, silu, scale, m, c_f, c_b, gain, weight):
     return pl.pallas_call(
         final_kernel,
-        in_specs=[pl.BlockSpec(memory_space=pltpu.VMEM)] * 8,
+        in_specs=[pl.BlockSpec(memory_space=pltpu.VMEM)] * 7
+        + [pl.BlockSpec(memory_space=pltpu.HBM)],
         out_specs=pl.BlockSpec(memory_space=pltpu.VMEM),
         out_shape=jax.ShapeDtypeStruct((Q, D), BF16),
-        scratch_shapes=[pltpu.VMEM((Q, E), BF16)],
-        compiler_params=LIMIT,
+        scratch_shapes=[
+            pltpu.VMEM((Q, E), BF16),
+            pltpu.VMEM((E, D), BF16),
+            pltpu.SemaphoreType.DMA,
+        ],
+        compiler_params=pltpu.CompilerParams(vmem_limit_bytes=FINAL_VMEM),
         name="gate_norm_project",
     )(inside, silu, scale, m, c_f, c_b, gain, weight)
 

time: 105 us -> 103 us (0.981)
  local copies, waits for them, and re-layouts: 9.08 us -> 3.58 us
  Pallas kernels: 15.7 us -> 19 us
    unnamed x30 -> x24, local copies, waits for them, and re-layouts: 9.08 us -> 3.58 us
    pallas_call x1, Pallas kernels: 3.28 us -> 6.13 us  [final_call(): pl.pallas_call(final_kernel, in_specs=[pl.BlockSpec(memory_space=pltpu.VM...]
where the time goes in v4:
time: 103 us; the launch traced here: 102 us
  waiting for transfers between devices  50.6 us (49%)
  Pallas kernels  19 us (18%)
  starting transfers between devices  16.9 us (16%)
  blocking collectives  12 us (12%)
  local copies, waits for them, and re-layouts  3.58 us (3%)
    all_to_all x1, waiting for transfers between devices, per_device(): parts = lax.all_to_all(states, 'seq', 0, 0, tiled=True)  31.1 us
    all_to_all x1, waiting for transfers between devices, per_device(): lax.all_to_all(entries, 'seq', 0, 0, tiled=True)  19.4 us
    all_to_all x1, blocking collectives, per_device(): totals = lax.all_to_all(totals, 'grp', 0, 0, tiled=True)  12 us
    all_to_all x1, starting transfers between devices, per_device(): parts = lax.all_to_all(states, 'seq', 0, 0, tiled=True)  11.4 us
    pallas_call x1, Pallas kernels, inside_call(): pl.pallas_call(inside_kernel, grid=(STEPS,), in_specs=[columns, columns,...  6.49 us
    pallas_call x1, Pallas kernels, final_call(): pl.pallas_call(final_kernel, in_specs=[pl.BlockSpec(memory_space=pltpu.VM...  6.13 us
    all_to_all x1, starting transfers between devices, per_device(): lax.all_to_all(entries, 'seq', 0, 0, tiled=True)  5.56 us
    pallas_call x1, Pallas kernels, state_call(): pl.pallas_call(state_kernel, in_specs=[pl.BlockSpec(memory_space=pltpu.HB...  3.73 us
  transfers between devices with their start and end apart: 2, of which 2 were waited for; matrix products, arithmetic and copies ran while one was open for 0% of the time, Pallas kernels for 6%

profile of v4, /device:TPU:32, one launch (start us, length us, event | category | flops | bytes accessed | tf_op | source)
XLA Modules:
  0.0 102.3 jit_solution(9055903273237316518)
XLA Ops:
  0.0 3.7 %span_states.1 = bf16[2,16,144,128]{3,2,1,0:T(8,128)(2,1)} custom-call(bf16[256,2048]{1,0:T(8,128)(2,1)} %x_hbm.1, f32[32,256]{1,0:T(8,128)} %rf_hbm.1, f32[32,256]{1,0:T(8,128)} %rb_hbm.1, bf16[256,128]{1,0:T(8,128)(2,1)} %bf_hbm.1, bf16[256,128]{1,0:T(8,128)(2,1)} %bb_hbm.1), custom_call_target="tpu_custom_call" | custom-call | tf_op jit(solution)/shard_map/span_states/pallas_call | solution.py:119
  3.7 11.4 %all-to-all-start = ((bf16[32,144,128]{2,1,0:T(8,128)(2,1)}), bf16[32,144,128]{2,1,0:T(8,128)(2,1)S(1)}, u32[]{:S(2)}, u32[]{:S(2)}) async-start(bf16[32,144,128]{2,1,0:T(8,128)(2,1)} %bitcast.5), calls=%async_computation | async-start | bytes 2359296 | tf_op jit(solution)/shard_map/all_to_all | solution.py:307
  15.1 0.1 pad_add_fusion.place_ref
  15.2 31.1 %all-to-all-done.parts_ref = bf16[32,144,128]{2,1,0:T(8,128)(2,1)S(1)} async-done(((bf16[32,144,128]{2,1,0:T(8,128)(2,1)}), bf16[32,144,128]{2,1,0:T(8,128)(2,1)S(1)}, u32[]{:S(2)}, u32[]{:S(2)}) %all-to-all-start) | async-done | bytes 1179680 | tf_op jit(solution)/shard_map/all_to_all | solution.py:307
  46.3 0.9 group_totals.1
  47.2 12.0 %all_to_all.15.totals_ref = bf16[8,144,128]{2,1,0:T(8,128)(2,1)S(1)} all-to-all(bf16[8,144,128]{2,1,0:T(8,128)(2,1)S(1)} %group_totals.1), channel_id=1, replica_groups=mesh['grp'=8,'seq'=32] {'grp'}, dimensions={0} | all-to-all | bytes 589824 | tf_op jit(solution)/shard_map/all_to_all | solution.py:316
  59.2 0.0 copy-start.10
  59.2 1.8 %entry_states.1 = bf16[32,128,128]{2,1,0:T(8,128)(2,1)} custom-call(s32[2]{0:T(128)S(1)} %pad_add_fusion.place_ref, bf16[8,144,128]{2,1,0:T(8,128)(2,1)S(1)} %all_to_all.15.totals_ref, bf16[32,144,128]{2,1,0:T(8,128)(2,1)S(1)} %all-to-all-done.parts_ref), custom_call_target="tpu_custom_call" | custom-call | tf_op jit(solution)/shard_map/entry_states/pallas_call | solution.py:317
  61.0 0.0 copy-start.2
  61.0 0.0 copy-start.3
  61.0 0.0 copy-start.4
  61.0 0.0 copy-start.6
  61.0 0.0 copy-start.7
  61.0 0.0 copy-start.8
  61.0 0.0 copy-start.9
  61.1 5.6 %all-to-all-start.2 = ((bf16[32,128,128]{2,1,0:T(8,128)(2,1)}), bf16[32,128,128]{2,1,0:T(8,128)(2,1)S(1)}, u32[]{:S(2)}, u32[]{:S(2)}) async-start(bf16[32,128,128]{2,1,0:T(8,128)(2,1)} %entry_states.1), calls=%async_computation.2 | async-start | bytes 2097152 | tf_op jit(solution)/shard_map/all_to_all | solution.py:325
  66.6 0.0 copy-done.10
  66.6 0.0 copy-done.2
  66.6 0.0 copy-done.3
  66.7 0.0 copy-done.4
  66.7 0.0 copy-done.6
  66.7 0.0 copy-done.7
  66.7 0.0 copy-done.8
  66.7 0.0 copy-done.9
  66.7 6.5 %inside_spans.1 = (bf16[256,2048]{1,0:T(8,128)(2,1)S(1)}, bf16[256,2048]{1,0:T(8,128)(2,1)S(1)}, bf16[256,128]{1,0:T(8,128)(2,1)S(1)}) custom-call(bf16[256,2048]{1,0:T(8,128)(2,1)S(1)} %copy-done.2, bf16[256,2048]{1,0:T(8,128)(2,1)S(1)} %copy-done.10, f32[32,256]{1,0:T(8,128)S(1)} %copy-done.8, f32[32,256]{1,0:T(8,128)S(1)} %copy-done.9, ...), custom_call_target="tpu_custom_call" | custom-call | flops 536870912 | bytes 4194304 | tf_op jit(solution)/shard_map/inside_spans/pallas_call | solution.py:184
  73.2 0.0 copy-start
  73.2 1.0 copy-done
  74.2 0.0 copy-start.1
  74.2 1.0 copy-done.1
  75.2 0.0 copy-start.5
  75.2 0.6 copy-done.5
  75.8 19.4 %all-to-all-done.2 = bf16[32,128,128]{2,1,0:T(8,128)(2,1)S(1)} async-done(((bf16[32,128,128]{2,1,0:T(8,128)(2,1)}), bf16[32,128,128]{2,1,0:T(8,128)(2,1)S(1)}, u32[]{:S(2)}, u32[]{:S(2)}) %all-to-all-start.2) | async-done | bytes 1048608 | tf_op jit(solution)/shard_map/all_to_all | solution.py:325
  95.2 0.0 copy-start.11
  95.2 1.0 copy-done.11
  96.2 6.1 %gate_norm_project.1 = bf16[256,1024]{1,0:T(8,128)(2,1)} custom-call(bf16[256,2048]{1,0:T(8,128)(2,1)} %copy-done, bf16[256,2048]{1,0:T(8,128)(2,1)} %copy-done.1, bf16[256,128]{1,0:T(8,128)(2,1)} %copy-done.5, bf16[2,16,128,128]{3,2,1,0:T(8,128)(2,1)} %bitcast.6, bf16[256,128]{1,0:T(8,128)(2,1)} %cf_ref.3, bf16[256,128]{1,0:T(8,128)(2,1)} %cb_ref.3, ...), custom_call_target="tpu_custom_call" | custom-call | tf_op jit(solution)/shard_map/gate_norm_project/pallas_call | solution.py:280
Async XLA Ops:
  3.7 42.6 %all-to-all-start = ((bf16[32,144,128]{2,1,0:T(8,128)(2,1)}), bf16[32,144,128]{2,1,0:T(8,128)(2,1)S(1)}, u32[]{:S(2)}, u32[]{:S(2)}) async-start(bf16[32,144,128]{2,1,0:T(8,128)(2,1)} %bitcast.5), calls=%async_computation | async-start | bytes 2359296 | tf_op jit(solution)/shard_map/all_to_all | solution.py:307
  59.2 7.4 %copy-start.10 = (bf16[256,2048]{1,0:T(8,128)(2,1)S(1)}, bf16[256,2048]{1,0:T(8,128)(2,1)}, u32[]{:S(2)}) copy-start(bf16[256,2048]{1,0:T(8,128)(2,1)} %gate_ref.1) | copy-start | bytes 3145732
  61.0 5.6 %copy-start.2 = (bf16[256,2048]{1,0:T(8,128)(2,1)S(1)}, bf16[256,2048]{1,0:T(8,128)(2,1)}, u32[]{:S(2)}) copy-start(bf16[256,2048]{1,0:T(8,128)(2,1)} %x_hbm.1) | copy-start | bytes 3145732
  61.0 5.6 %copy-start.3 = (bf16[256,128]{1,0:T(8,128)(2,1)S(1)}, bf16[256,128]{1,0:T(8,128)(2,1)}, u32[]{:S(2)}) copy-start(bf16[256,128]{1,0:T(8,128)(2,1)} %cf_ref.3) | copy-start | bytes 196612
  61.0 5.6 %copy-start.4 = (bf16[256,128]{1,0:T(8,128)(2,1)S(1)}, bf16[256,128]{1,0:T(8,128)(2,1)}, u32[]{:S(2)}) copy-start(bf16[256,128]{1,0:T(8,128)(2,1)} %cb_ref.3) | copy-start | bytes 196612
  61.0 5.7 %copy-start.6 = (bf16[256,128]{1,0:T(8,128)(2,1)S(1)}, bf16[256,128]{1,0:T(8,128)(2,1)}, u32[]{:S(2)}) copy-start(bf16[256,128]{1,0:T(8,128)(2,1)} %bf_hbm.1) | copy-start | bytes 196612
  61.0 5.7 %copy-start.7 = (bf16[256,128]{1,0:T(8,128)(2,1)S(1)}, bf16[256,128]{1,0:T(8,128)(2,1)}, u32[]{:S(2)}) copy-start(bf16[256,128]{1,0:T(8,128)(2,1)} %bb_hbm.1) | copy-start | bytes 196612
  61.0 5.7 %copy-start.8 = (f32[32,256]{1,0:T(8,128)S(1)}, f32[32,256]{1,0:T(8,128)}, u32[]{:S(2)}) copy-start(f32[32,256]{1,0:T(8,128)} %rf_hbm.1) | copy-start | bytes 98308
  61.0 5.7 %copy-start.9 = (f32[32,256]{1,0:T(8,128)S(1)}, f32[32,256]{1,0:T(8,128)}, u32[]{:S(2)}) copy-start(f32[32,256]{1,0:T(8,128)} %rb_hbm.1) | copy-start | bytes 98308
  61.1 34.2 %all-to-all-start.2 = ((bf16[32,128,128]{2,1,0:T(8,128)(2,1)}), bf16[32,128,128]{2,1,0:T(8,128)(2,1)S(1)}, u32[]{:S(2)}, u32[]{:S(2)}) async-start(bf16[32,128,128]{2,1,0:T(8,128)(2,1)} %entry_states.1), calls=%async_computation.2 | async-start | bytes 2097152 | tf_op jit(solution)/shard_map/all_to_all | solution.py:325
  73.2 1.0 copy-start
  74.2 1.0 copy-start.1
  75.2 0.6 copy-start.5
  95.2 1.0 copy-start.11

commit v5 on v4

--- a/solution.py
+++ b/solution.py
@@ -15,9 +15,10 @@
 BLK = 256
 STEPS = E // BLK
 FW = 256
-FINAL_VMEM = 59400000
+FINAL_VMEM = 48 * 1024 * 1024
 HPB = BLK // HEAD
 ROWS = N + 16
+CHUNKS = 4
 LOG2E = 1.4426950408889634
 F32 = jnp.float32
 BF16 = jnp.bfloat16
@@ -77,7 +78,8 @@
 
 
 def state_kernel(
-    x_hbm, rf_hbm, rb_hbm, bf_hbm, bb_hbm, out_ref, x_ref, r_ref, b_ref, select_ref, sems
+    x_hbm, rf_hbm, rb_hbm, bf_hbm, bb_hbm, out_hbm,
+    x_ref, r_ref, b_ref, select_ref, out_ref, sems,
 ):
     copies = [
         pltpu.make_async_copy(rf_hbm, r_ref.at[0], sems.at[0]),
@@ -113,20 +115,25 @@
         s = dot(turned[d], (x * factor).astype(BF16)).astype(BF16)
         for k in range(E // 128):
             out_ref[d, k, 0:N, :] = s[:, 128 * k : 128 * (k + 1)]
+        copies.append(pltpu.make_async_copy(out_ref.at[d], out_hbm.at[d], sems.at[5 + d]))
+        copies[-1].start()
+    copies[5].wait()
+    copies[6].wait()
 
 
 def state_call(x, rate_f, rate_b, b_f, b_b):
     return pl.pallas_call(
         state_kernel,
         in_specs=[pl.BlockSpec(memory_space=pltpu.HBM)] * 5,
-        out_specs=pl.BlockSpec(memory_space=pltpu.VMEM),
+        out_specs=pl.BlockSpec(memory_space=pltpu.HBM),
         out_shape=jax.ShapeDtypeStruct((2, E // 128, ROWS, 128), BF16),
         scratch_shapes=[
             pltpu.VMEM((Q, E), BF16),
             pltpu.VMEM((2, H, Q), F32),
             pltpu.VMEM((2, Q, N), BF16),
             pltpu.VMEM((2 * H, E), BF16),
-            pltpu.SemaphoreType.DMA((5,)),
+            pltpu.VMEM((2, E // 128, ROWS, 128), BF16),
+            pltpu.SemaphoreType.DMA((7,)),
         ],
         compiler_params=pltpu.CompilerParams(vmem_limit_bytes=60 * 1024 * 1024),
         name="span_states",
@@ -225,7 +232,7 @@
         out_ref[g, N:ROWS, :] = tail
 
 
-def entry_kernel(count, groups, place_ref, totals_ref, parts_ref, out_ref):
+def entry_kernel(count, groups, place_ref, totals_ref, parts_ref, out_hbm, out_ref, sems):
     backward, mine = place_ref[0], place_ref[1]
 
     def outer(i, state):
@@ -234,14 +241,20 @@
         return keep * state + own
 
     state = lax.fori_loop(0, mine, outer, jnp.zeros((N, 128), F32))
-
-    def step(i, state):
-        index = jnp.where(backward == 1, count - 1 - i, i)
-        out_ref[index] = state.astype(BF16)
-        own, keep = read_part(parts_ref, index)
-        return keep * state + own
-
-    lax.fori_loop(0, count, step, state, unroll=4)
+    chunk = count // CHUNKS
+    copies = []
+    for q in range(CHUNKS):
+        first = jnp.where(backward == 1, count - chunk * (q + 1), chunk * q)
+        for i in range(chunk):
+            index = first + jnp.where(backward == 1, chunk - 1 - i, i)
+            out_ref[index] = state.astype(BF16)
+            own, keep = read_part(parts_ref, index)
+            state = keep * state + own
+        span = pl.ds(first, chunk)
+        copies.append(pltpu.make_async_copy(out_ref.at[span], out_hbm.at[span], sems.at[q]))
+        copies[-1].start()
+    for copy in copies:
+        copy.wait()
 
 
 def vmem_specs(n):
@@ -250,10 +263,10 @@
 
 def final_kernel(
     in_ref, silu_ref, scale_ref, m_ref, cf_ref, cb_ref, gain_ref, w_hbm,
-    out_ref, normed_ref, w_ref, sem,
+    out_hbm, normed_ref, w_ref, out_ref, sems,
 ):
-    copy = pltpu.make_async_copy(w_hbm, w_ref, sem)
-    copy.start()
+    copies = [pltpu.make_async_copy(w_hbm, w_ref, sems.at[0])]
+    copies[0].start()
     scales = [scale_ref[:, 2 * H * d : 2 * H * (d + 1)] for d in range(2)]
     square = jnp.zeros((Q, 128), F32)
     for j in range(E // FW):
@@ -270,10 +283,16 @@
         normed_ref[:, at] = (gated * gain_ref[:, at]).astype(BF16)
     mean = jnp.sum(square, axis=1, keepdims=True) * (1.0 / E)
     scale = lax.rsqrt(mean + 1e-05)
-    copy.wait()
-    for n in range(D // 256):
-        at = pl.ds(256 * n, 256)
-        out_ref[:, at] = (dot(normed_ref[...], w_ref[:, at]) * scale).astype(BF16)
+    copies[0].wait()
+    half = Q // 2
+    for n in range(2):
+        rows = pl.ds(half * n, half)
+        mixed = dot(normed_ref[rows, :], w_ref[...]) * scale[half * n : half * (n + 1)]
+        out_ref[rows, :] = mixed.astype(BF16)
+        copies.append(pltpu.make_async_copy(out_ref.at[rows], out_hbm.at[rows], sems.at[n + 1]))
+        copies[-1].start()
+    copies[1].wait()
+    copies[2].wait()
 
 
 def final_call(inside, silu, scale, m, c_f, c_b, gain, weight):
@@ -281,12 +300,13 @@
         final_kernel,
         in_specs=[pl.BlockSpec(memory_space=pltpu.VMEM)] * 7
         + [pl.BlockSpec(memory_space=pltpu.HBM)],
-        out_specs=pl.BlockSpec(memory_space=pltpu.VMEM),
+        out_specs=pl.BlockSpec(memory_space=pltpu.HBM),
         out_shape=jax.ShapeDtypeStruct((Q, D), BF16),
         scratch_shapes=[
             pltpu.VMEM((Q, E), BF16),
             pltpu.VMEM((E, D), BF16),
-            pltpu.SemaphoreType.DMA,
+            pltpu.VMEM((Q, D), BF16),
+            pltpu.SemaphoreType.DMA((3,)),
         ],
         compiler_params=pltpu.CompilerParams(vmem_limit_bytes=FINAL_VMEM),
         name="gate_norm_project",
@@ -317,8 +337,12 @@
     entries = pl.pallas_call(
         functools.partial(entry_kernel, count, groups),
         in_specs=vmem_specs(2),
-        out_specs=pl.BlockSpec(memory_space=pltpu.VMEM),
+        out_specs=pl.BlockSpec(memory_space=pltpu.HBM),
         out_shape=jax.ShapeDtypeStruct((count, N, 128), BF16),
+        scratch_shapes=[
+            pltpu.VMEM((count, N, 128), BF16),
+            pltpu.SemaphoreType.DMA((CHUNKS,)),
+        ],
         compiler_params=LIMIT,
         name="entry_states",
     )(place, totals, parts)

time: 103 us -> 101 us (0.981)
  local copies, waits for them, and re-layouts: 3.58 us -> 2.49 us
    unnamed x24 -> x18, local copies, waits for them, and re-layouts: 3.58 us -> 2.49 us
where the time goes in v5:
time: 101 us; the launch traced here: 100 us
  waiting for transfers between devices  50.7 us (50%)
  Pallas kernels  18 us (18%)
  starting transfers between devices  16.9 us (17%)
  blocking collectives  12 us (12%)
  local copies, waits for them, and re-layouts  2.49 us (2%)
    all_to_all x1, waiting for transfers between devices, per_device(): parts = lax.all_to_all(states, 'seq', 0, 0, tiled=True)  31.1 us
    all_to_all x1, waiting for transfers between devices, per_device(): lax.all_to_all(entries, 'seq', 0, 0, tiled=True)  19.6 us
    all_to_all x1, blocking collectives, per_device(): totals = lax.all_to_all(totals, 'grp', 0, 0, tiled=True)  12 us
    all_to_all x1, starting transfers between devices, per_device(): parts = lax.all_to_all(states, 'seq', 0, 0, tiled=True)  11.4 us
    pallas_call x1, Pallas kernels, inside_call(): pl.pallas_call(inside_kernel, grid=(STEPS,), in_specs=[columns, columns,...  6.47 us
    all_to_all x1, starting transfers between devices, per_device(): lax.all_to_all(entries, 'seq', 0, 0, tiled=True)  5.57 us
    pallas_call x1, Pallas kernels, final_call(): pl.pallas_call(final_kernel, in_specs=[pl.BlockSpec(memory_space=pltpu.VM...  5.5 us
    pallas_call x1, Pallas kernels, state_call(): pl.pallas_call(state_kernel, in_specs=[pl.BlockSpec(memory_space=pltpu.HB...  3.53 us
  transfers between devices with their start and end apart: 2, of which 2 were waited for; matrix products, arithmetic and copies ran while one was open for 0% of the time, Pallas kernels for 6%

profile of v5, /device:TPU:32, one launch (start us, length us, event | category | flops | bytes accessed | tf_op | source)
XLA Modules:
  0.0 100.4 jit_solution(1861676667497897832)
XLA Ops:
  0.0 3.5 %span_states.1 = bf16[2,16,144,128]{3,2,1,0:T(8,128)(2,1)} custom-call(bf16[256,2048]{1,0:T(8,128)(2,1)} %x_hbm.1, f32[32,256]{1,0:T(8,128)} %rf_hbm.1, f32[32,256]{1,0:T(8,128)} %rb_hbm.1, bf16[256,128]{1,0:T(8,128)(2,1)} %bf_hbm.1, bf16[256,128]{1,0:T(8,128)(2,1)} %bb_hbm.1), custom_call_target="tpu_custom_call" | custom-call | tf_op jit(solution)/shard_map/span_states/pallas_call | solution.py:125
  3.5 11.4 %all-to-all-start = ((bf16[32,144,128]{2,1,0:T(8,128)(2,1)}), bf16[32,144,128]{2,1,0:T(8,128)(2,1)S(1)}, u32[]{:S(2)}, u32[]{:S(2)}) async-start(bf16[32,144,128]{2,1,0:T(8,128)(2,1)} %bitcast.7), calls=%async_computation | async-start | bytes 2359296 | tf_op jit(solution)/shard_map/all_to_all | solution.py:327
  14.9 0.1 pad_add_fusion.place_ref
  15.0 31.1 %all-to-all-done.parts_ref = bf16[32,144,128]{2,1,0:T(8,128)(2,1)S(1)} async-done(((bf16[32,144,128]{2,1,0:T(8,128)(2,1)}), bf16[32,144,128]{2,1,0:T(8,128)(2,1)S(1)}, u32[]{:S(2)}, u32[]{:S(2)}) %all-to-all-start) | async-done | bytes 1179680 | tf_op jit(solution)/shard_map/all_to_all | solution.py:327
  46.1 0.9 group_totals.1
  47.0 12.0 %all_to_all.15.totals_ref = bf16[8,144,128]{2,1,0:T(8,128)(2,1)S(1)} all-to-all(bf16[8,144,128]{2,1,0:T(8,128)(2,1)S(1)} %group_totals.1), channel_id=1, replica_groups=mesh['grp'=8,'seq'=32] {'grp'}, dimensions={0} | all-to-all | bytes 589824 | tf_op jit(solution)/shard_map/all_to_all | solution.py:336
  59.0 1.6 %entry_states.1 = bf16[32,128,128]{2,1,0:T(8,128)(2,1)} custom-call(s32[2]{0:T(128)S(1)} %pad_add_fusion.place_ref, bf16[8,144,128]{2,1,0:T(8,128)(2,1)S(1)} %all_to_all.15.totals_ref, bf16[32,144,128]{2,1,0:T(8,128)(2,1)S(1)} %all-to-all-done.parts_ref), custom_call_target="tpu_custom_call" | custom-call | tf_op jit(solution)/shard_map/entry_states/pallas_call | solution.py:337
  60.6 0.0 copy-start.1
  60.6 0.0 copy-start.2
  60.6 0.0 copy-start.3
  60.6 0.0 copy-start.4
  60.7 0.0 copy-start.5
  60.7 0.0 copy-start.6
  60.7 5.6 %all-to-all-start.2 = ((bf16[32,128,128]{2,1,0:T(8,128)(2,1)}), bf16[32,128,128]{2,1,0:T(8,128)(2,1)S(1)}, u32[]{:S(2)}, u32[]{:S(2)}) async-start(bf16[32,128,128]{2,1,0:T(8,128)(2,1)} %entry_states.1), calls=%async_computation.2 | async-start | bytes 2097152 | tf_op jit(solution)/shard_map/all_to_all | solution.py:349
  66.3 0.0 copy-done.1
  66.3 0.0 copy-done.2
  66.3 0.0 copy-done.3
  66.3 0.0 copy-done.4
  66.3 0.0 copy-done.5
  66.3 0.0 copy-done.6
  66.3 0.0 copy-start
  66.3 1.2 %copy-done = bf16[256,2048]{1,0:T(8,128)(2,1)S(1)} copy-done((bf16[256,2048]{1,0:T(8,128)(2,1)S(1)}, bf16[256,2048]{1,0:T(8,128)(2,1)}, u32[]{:S(2)}) %copy-start) | copy-done | bytes 1048600
  67.5 0.0 copy-start.8
  67.6 1.2 %copy-done.8 = bf16[256,2048]{1,0:T(8,128)(2,1)S(1)} copy-done((bf16[256,2048]{1,0:T(8,128)(2,1)S(1)}, bf16[256,2048]{1,0:T(8,128)(2,1)}, u32[]{:S(2)}) %copy-start.8) | copy-done | bytes 1048600
  68.8 0.0 copy-start.7
  68.8 6.5 %inside_spans.1 = (bf16[256,2048]{1,0:T(8,128)(2,1)S(1)}, bf16[256,2048]{1,0:T(8,128)(2,1)S(1)}, bf16[256,128]{1,0:T(8,128)(2,1)S(1)}) custom-call(bf16[256,2048]{1,0:T(8,128)(2,1)S(1)} %copy-done, bf16[256,2048]{1,0:T(8,128)(2,1)S(1)} %copy-done.8, f32[32,256]{1,0:T(8,128)S(1)} %copy-done.5, f32[32,256]{1,0:T(8,128)S(1)} %copy-done.6, ...), custom_call_target="tpu_custom_call" | custom-call | flops 536870912 | bytes 4194304 | tf_op jit(solution)/shard_map/inside_spans/pallas_call | solution.py:191
  75.3 19.6 %all-to-all-done.2 = bf16[32,128,128]{2,1,0:T(8,128)(2,1)S(1)} async-done(((bf16[32,128,128]{2,1,0:T(8,128)(2,1)}), bf16[32,128,128]{2,1,0:T(8,128)(2,1)S(1)}, u32[]{:S(2)}, u32[]{:S(2)}) %all-to-all-start.2) | async-done | bytes 1048608 | tf_op jit(solution)/shard_map/all_to_all | solution.py:349
  94.9 0.0 copy-done.7
  94.9 5.5 %gate_norm_project.1 = bf16[256,1024]{1,0:T(8,128)(2,1)} custom-call(bf16[256,2048]{1,0:T(8,128)(2,1)S(1)} %get-tuple-element.8.in_ref, bf16[256,2048]{1,0:T(8,128)(2,1)S(1)} %get-tuple-element.9.silu_ref, bf16[256,128]{1,0:T(8,128)(2,1)S(1)} %get-tuple-element.10.scale_ref, bf16[2,16,128,128]{3,2,1,0:T(8,128)(2,1)S(1)} %bitcast.5, ...), custom_call_target="tpu_custom_call" | custom-call | tf_op jit(solution)/shard_map/gate_norm_project/pallas_call | solution.py:299
Async XLA Ops:
  3.5 42.6 %all-to-all-start = ((bf16[32,144,128]{2,1,0:T(8,128)(2,1)}), bf16[32,144,128]{2,1,0:T(8,128)(2,1)S(1)}, u32[]{:S(2)}, u32[]{:S(2)}) async-start(bf16[32,144,128]{2,1,0:T(8,128)(2,1)} %bitcast.7), calls=%async_computation | async-start | bytes 2359296 | tf_op jit(solution)/shard_map/all_to_all | solution.py:327
  60.6 5.7 %copy-start.1 = (bf16[256,128]{1,0:T(8,128)(2,1)S(1)}, bf16[256,128]{1,0:T(8,128)(2,1)}, u32[]{:S(2)}) copy-start(bf16[256,128]{1,0:T(8,128)(2,1)} %cf_ref.3) | copy-start | bytes 196612
  60.6 5.7 %copy-start.2 = (bf16[256,128]{1,0:T(8,128)(2,1)S(1)}, bf16[256,128]{1,0:T(8,128)(2,1)}, u32[]{:S(2)}) copy-start(bf16[256,128]{1,0:T(8,128)(2,1)} %cb_ref.3) | copy-start | bytes 196612
  60.6 5.7 %copy-start.3 = (bf16[256,128]{1,0:T(8,128)(2,1)S(1)}, bf16[256,128]{1,0:T(8,128)(2,1)}, u32[]{:S(2)}) copy-start(bf16[256,128]{1,0:T(8,128)(2,1)} %bf_hbm.1) | copy-start | bytes 196612
  60.6 5.6 %copy-start.4 = (bf16[256,128]{1,0:T(8,128)(2,1)S(1)}, bf16[256,128]{1,0:T(8,128)(2,1)}, u32[]{:S(2)}) copy-start(bf16[256,128]{1,0:T(8,128)(2,1)} %bb_hbm.1) | copy-start | bytes 196612
  60.7 5.6 %copy-start.5 = (f32[32,256]{1,0:T(8,128)S(1)}, f32[32,256]{1,0:T(8,128)}, u32[]{:S(2)}) copy-start(f32[32,256]{1,0:T(8,128)} %rf_hbm.1) | copy-start | bytes 98308
  60.7 5.6 %copy-start.6 = (f32[32,256]{1,0:T(8,128)S(1)}, f32[32,256]{1,0:T(8,128)}, u32[]{:S(2)}) copy-start(f32[32,256]{1,0:T(8,128)} %rb_hbm.1) | copy-start | bytes 98308
  60.7 34.2 %all-to-all-start.2 = ((bf16[32,128,128]{2,1,0:T(8,128)(2,1)}), bf16[32,128,128]{2,1,0:T(8,128)(2,1)S(1)}, u32[]{:S(2)}, u32[]{:S(2)}) async-start(bf16[32,128,128]{2,1,0:T(8,128)(2,1)} %entry_states.1), calls=%async_computation.2 | async-start | bytes 2097152 | tf_op jit(solution)/shard_map/all_to_all | solution.py:349
  66.3 1.2 %copy-start = (bf16[256,2048]{1,0:T(8,128)(2,1)S(1)}, bf16[256,2048]{1,0:T(8,128)(2,1)}, u32[]{:S(2)}) copy-start(bf16[256,2048]{1,0:T(8,128)(2,1)} %x_hbm.1) | copy-start | bytes 3145732
  67.5 1.2 %copy-start.8 = (bf16[256,2048]{1,0:T(8,128)(2,1)S(1)}, bf16[256,2048]{1,0:T(8,128)(2,1)}, u32[]{:S(2)}) copy-start(bf16[256,2048]{1,0:T(8,128)(2,1)} %gate_ref.1) | copy-start | bytes 3145732
  68.8 26.1 %copy-start.7 = (f32[2048]{0:T(1024)S(1)}, f32[2048]{0:T(1024)}, u32[]{:S(2)}) copy-start(f32[2048]{0:T(1024)} %param.18) | copy-start | bytes 24580

commit v6 on v5

--- a/solution.py
+++ b/solution.py
@@ -19,6 +19,8 @@
 HPB = BLK // HEAD
 ROWS = N + 16
 CHUNKS = 4
+YSIZE = 4
+ZSIZE = 8
 LOG2E = 1.4426950408889634
 F32 = jnp.float32
 BF16 = jnp.bfloat16
@@ -78,7 +80,7 @@
 
 
 def state_kernel(
-    x_hbm, rf_hbm, rb_hbm, bf_hbm, bb_hbm, out_hbm,
+    x_hbm, rf_hbm, rb_hbm, bf_hbm, bb_hbm, out_hbm, total_ref,
     x_ref, r_ref, b_ref, select_ref, out_ref, sems,
 ):
     copies = [
@@ -93,18 +95,17 @@
     select_ref[...] = head_select(0, 2 * H, E, 0)
     copies[0].wait()
     copies[1].wait()
-    scales = []
+    scales, totals = [], 0.0
     for d, sums in enumerate((lane_sums, lane_sums_back)):
         r = r_ref[d]
         c = sums(r)
         total = c[:, Q - 1 : Q] if d == 0 else c[:, 0:1]
         parts = two_parts(step_of(r) * jnp.exp(c - total))
         scales.append(jnp.concatenate(parts, axis=0).T.astype(BF16))
-        keep = jnp.broadcast_to(jnp.exp(-total), (H, 128))
+        row = lax.broadcasted_iota(jnp.int32, (H, 128), 0)
         lane = lax.broadcasted_iota(jnp.int32, (H, 128), 1)
-        for k in range(E // 128):
-            own = jnp.where(lane < HEAD, keep[2 * k : 2 * k + 1], keep[2 * k + 1 : 2 * k + 2])
-            out_ref[d, k, N:ROWS, :] = three_rows(own[:1], 128)
+        totals = totals + jnp.where(lane == row + H * d, total, 0.0)
+    total_ref[...] = jnp.sum(totals, axis=0, keepdims=True)
     copies[2].wait()
     copies[3].wait()
     turned = [b_ref[d].astype(F32).T.astype(BF16) for d in range(2)]
@@ -114,7 +115,7 @@
         factor = dot(scales[d], select_ref[...])
         s = dot(turned[d], (x * factor).astype(BF16)).astype(BF16)
         for k in range(E // 128):
-            out_ref[d, k, 0:N, :] = s[:, 128 * k : 128 * (k + 1)]
+            out_ref[d, k] = s[:, 128 * k : 128 * (k + 1)]
         copies.append(pltpu.make_async_copy(out_ref.at[d], out_hbm.at[d], sems.at[5 + d]))
         copies[-1].start()
     copies[5].wait()
@@ -125,14 +126,17 @@
     return pl.pallas_call(
         state_kernel,
         in_specs=[pl.BlockSpec(memory_space=pltpu.HBM)] * 5,
-        out_specs=pl.BlockSpec(memory_space=pltpu.HBM),
-        out_shape=jax.ShapeDtypeStruct((2, E // 128, ROWS, 128), BF16),
+        out_specs=[pl.BlockSpec(memory_space=pltpu.HBM), pl.BlockSpec(memory_space=pltpu.VMEM)],
+        out_shape=[
+            jax.ShapeDtypeStruct((2, E // 128, N, 128), BF16),
+            jax.ShapeDtypeStruct((1, 128), F32),
+        ],
         scratch_shapes=[
             pltpu.VMEM((Q, E), BF16),
             pltpu.VMEM((2, H, Q), F32),
             pltpu.VMEM((2, Q, N), BF16),
             pltpu.VMEM((2 * H, E), BF16),
-            pltpu.VMEM((2, E // 128, ROWS, 128), BF16),
+            pltpu.VMEM((2, E // 128, N, 128), BF16),
             pltpu.SemaphoreType.DMA((7,)),
         ],
         compiler_params=pltpu.CompilerParams(vmem_limit_bytes=60 * 1024 * 1024),
@@ -214,14 +218,29 @@
     return state, tail[0:1] + tail[1:2] + tail[2:3]
 
 
-def total_kernel(count, copies, place_ref, parts_ref, out_ref):
+def owned_decays(first, logs_ref, keep_ref):
+    lane = lax.broadcasted_iota(jnp.int32, logs_ref.shape, 1)
+    logs = logs_ref[...]
+    low = jnp.sum(jnp.where(lane == first, logs, 0.0), axis=1, keepdims=True)
+    high = jnp.sum(jnp.where(lane == first + 1, logs, 0.0), axis=1, keepdims=True)
+    keep_ref[...] = jnp.exp(-jnp.where(lane < HEAD, low, high))
+
+
+def decay_of(index, place_ref, keep_ref):
+    along_y = (place_ref[3] - index // ZSIZE) & (YSIZE - 1)
+    along_z = (place_ref[4] - index % ZSIZE) & (ZSIZE - 1)
+    return keep_ref[pl.ds(along_z * YSIZE + along_y, 1), :]
+
+
+def total_kernel(count, copies, place_ref, logs_ref, parts_ref, out_ref, keep_ref):
     backward = place_ref[0]
+    owned_decays(place_ref[2], logs_ref, keep_ref)
 
     def step(i, carried):
         state, kept = carried
         index = jnp.where(backward == 1, count - 1 - i, i)
-        own, keep = read_part(parts_ref, index)
-        return keep * state + own, keep * kept
+        keep = decay_of(index, place_ref, keep_ref)
+        return keep * state + parts_ref[index].astype(F32), keep * kept
 
     state, kept = lax.fori_loop(
         0, count, step, (jnp.zeros((N, 128), F32), jnp.ones((1, 128), F32)), unroll=4
@@ -232,8 +251,11 @@
         out_ref[g, N:ROWS, :] = tail
 
 
-def entry_kernel(count, groups, place_ref, totals_ref, parts_ref, out_hbm, out_ref, sems):
+def entry_kernel(
+    count, groups, place_ref, totals_ref, logs_ref, parts_ref, out_hbm, out_ref, keep_ref, sems
+):
     backward, mine = place_ref[0], place_ref[1]
+    owned_decays(place_ref[2], logs_ref, keep_ref)
 
     def outer(i, state):
         index = jnp.where(backward == 1, groups - 1 - i, i)
@@ -248,8 +270,8 @@
         for i in range(chunk):
             index = first + jnp.where(backward == 1, chunk - 1 - i, i)
             out_ref[index] = state.astype(BF16)
-            own, keep = read_part(parts_ref, index)
-            state = keep * state + own
+            keep = decay_of(index, place_ref, keep_ref)
+            state = keep * state + parts_ref[index].astype(F32)
         span = pl.ds(first, chunk)
         copies.append(pltpu.make_async_copy(out_ref.at[span], out_hbm.at[span], sems.at[q]))
         copies[-1].start()
@@ -263,10 +285,13 @@
 
 def final_kernel(
     in_ref, silu_ref, scale_ref, m_ref, cf_ref, cb_ref, gain_ref, w_hbm,
-    out_hbm, normed_ref, w_ref, out_ref, sems,
-):
-    copies = [pltpu.make_async_copy(w_hbm, w_ref, sems.at[0])]
-    copies[0].start()
+    out_ref, normed_ref, w_ref, sems,
+):
+    copies = []
+    for i in range(4):
+        rows = pl.ds(E // 4 * i, E // 4)
+        copies.append(pltpu.make_async_copy(w_hbm.at[rows], w_ref.at[rows], sems.at[i]))
+        copies[-1].start()
     scales = [scale_ref[:, 2 * H * d : 2 * H * (d + 1)] for d in range(2)]
     square = jnp.zeros((Q, 128), F32)
     for j in range(E // FW):
@@ -283,16 +308,11 @@
         normed_ref[:, at] = (gated * gain_ref[:, at]).astype(BF16)
     mean = jnp.sum(square, axis=1, keepdims=True) * (1.0 / E)
     scale = lax.rsqrt(mean + 1e-05)
-    copies[0].wait()
-    half = Q // 2
-    for n in range(2):
-        rows = pl.ds(half * n, half)
-        mixed = dot(normed_ref[rows, :], w_ref[...]) * scale[half * n : half * (n + 1)]
-        out_ref[rows, :] = mixed.astype(BF16)
-        copies.append(pltpu.make_async_copy(out_ref.at[rows], out_hbm.at[rows], sems.at[n + 1]))
-        copies[-1].start()
-    copies[1].wait()
-    copies[2].wait()
+    for copy in copies:
+        copy.wait()
+    for n in range(D // 256):
+        at = pl.ds(256 * n, 256)
+        out_ref[:, at] = (dot(normed_ref[...], w_ref[:, at]) * scale).astype(BF16)
 
 
 def final_call(inside, silu, scale, m, c_f, c_b, gain, weight):
@@ -300,13 +320,12 @@
         final_kernel,
         in_specs=[pl.BlockSpec(memory_space=pltpu.VMEM)] * 7
         + [pl.BlockSpec(memory_space=pltpu.HBM)],
-        out_specs=pl.BlockSpec(memory_space=pltpu.HBM),
+        out_specs=pl.BlockSpec(memory_space=pltpu.VMEM),
         out_shape=jax.ShapeDtypeStruct((Q, D), BF16),
         scratch_shapes=[
             pltpu.VMEM((Q, E), BF16),
             pltpu.VMEM((E, D), BF16),
-            pltpu.VMEM((Q, D), BF16),
-            pltpu.SemaphoreType.DMA((3,)),
+            pltpu.SemaphoreType.DMA((4,)),
         ],
         compiler_params=pltpu.CompilerParams(vmem_limit_bytes=FINAL_VMEM),
         name="gate_norm_project",
@@ -318,34 +337,48 @@
     rate_forward, rate_backward, norm_gain, out_weight,
 ):
     count, groups = lax.axis_size("seq"), lax.axis_size("grp")
-    states = state_call(features, rate_forward, rate_backward, b_forward, b_backward)
-    states = states.reshape(count, ROWS, 128)
-    backward = (lax.axis_index("seq") >= count // 2).astype(jnp.int32)
-    group = lax.axis_index("grp")
+    states, logs = state_call(features, rate_forward, rate_backward, b_forward, b_backward)
+    states = states.reshape(count, N, 128)
+    member, group = lax.axis_index("seq"), lax.axis_index("grp")
+    backward = (member >= count // 2).astype(jnp.int32)
     mine = jnp.where(backward == 1, groups - 1 - group, group)
-    place = jnp.stack([backward, mine]).astype(jnp.int32)
+    place = [backward, mine, 2 * member, member // ZSIZE, member % ZSIZE]
+    place = jnp.stack(place).astype(jnp.int32)
     parts = lax.all_to_all(states, "seq", 0, 0, tiled=True)
+    rows = [logs]
+    for far in range(1, YSIZE):
+        pairs = [(i, (i + far * ZSIZE) % count) for i in range(count)]
+        rows.append(lax.ppermute(logs, "seq", pairs))
+    logs = jnp.concatenate(rows, axis=0)
+    rows = [logs]
+    for far in range(1, ZSIZE):
+        pairs = [(i, i // ZSIZE * ZSIZE + (i + far) % ZSIZE) for i in range(count)]
+        rows.append(lax.ppermute(logs, "seq", pairs))
+    logs = jnp.concatenate(rows, axis=0)
+    keep = pltpu.VMEM((count, 128), F32)
     totals = pl.pallas_call(
         functools.partial(total_kernel, count, groups),
-        in_specs=vmem_specs(1),
+        in_specs=vmem_specs(2),
         out_specs=pl.BlockSpec(memory_space=pltpu.VMEM),
         out_shape=jax.ShapeDtypeStruct((groups, ROWS, 128), BF16),
+        scratch_shapes=[keep],
         compiler_params=LIMIT,
         name="group_totals",
-    )(place, parts)
+    )(place, logs, parts)
     totals = lax.all_to_all(totals, "grp", 0, 0, tiled=True)
     entries = pl.pallas_call(
         functools.partial(entry_kernel, count, groups),
-        in_specs=vmem_specs(2),
+        in_specs=vmem_specs(3),
         out_specs=pl.BlockSpec(memory_space=pltpu.HBM),
         out_shape=jax.ShapeDtypeStruct((count, N, 128), BF16),
         scratch_shapes=[
             pltpu.VMEM((count, N, 128), BF16),
+            keep,
             pltpu.SemaphoreType.DMA((CHUNKS,)),
         ],
         compiler_params=LIMIT,
         name="entry_states",
-    )(place, totals, parts)
+    )(place, totals, logs, parts)
     m = lax.all_to_all(entries, "seq", 0, 0, tiled=True).reshape(2, E // 128, N, 128)
     inside, silu, scale = inside_call(
         features, gate_input, rate_forward, rate_backward,

time: 101 us -> 104 us (1.030)
  starting transfers between devices: 16.9 us -> 40.1 us
  waiting for transfers between devices: 50.7 us -> 28.6 us
    all_to_all x1, waiting for transfers between devices: 31.1 us -> 0.01 us  [per_device(): parts = lax.all_to_all(states, 'seq', 0, 0, tiled=True)]
    ppermute x0 -> x10, starting transfers between devices: none -> 21 us  [per_device(): rows.append(lax.ppermute(logs, 'seq', pairs))]
    ppermute x0 -> x10, waiting for transfers between devices: none -> 8.95 us  [per_device(): rows.append(lax.ppermute(logs, 'seq', pairs))]
    all_to_all x1, starting transfers between devices: 5.57 us -> 7.58 us  [per_device(): lax.all_to_all(entries, 'seq', 0, 0, tiled=True)]
  transfers between devices with their start and end apart: 2 -> 12, of which waited for: 2 -> 6; matrix products, arithmetic and copies ran while one was open for 0% -> 1% of each run, Pallas kernels for 6% -> 6%
where the time goes in v6:
time: 104 us; the launch traced here: 103 us
  starting transfers between devices  40.1 us (39%)
  waiting for transfers between devices  28.6 us (28%)
  Pallas kernels  18.3 us (18%)
  blocking collectives  12 us (12%)
  local copies, waits for them, and re-layouts  3.32 us (3%)
    ppermute x10, starting transfers between devices, per_device(): rows.append(lax.ppermute(logs, 'seq', pairs))  21 us
    all_to_all x1, waiting for transfers between devices, per_device(): lax.all_to_all(entries, 'seq', 0, 0, tiled=True)  19.6 us
    all_to_all x1, blocking collectives, per_device(): totals = lax.all_to_all(totals, 'grp', 0, 0, tiled=True)  12 us
    all_to_all x1, starting transfers between devices, per_device(): parts = lax.all_to_all(states, 'seq', 0, 0, tiled=True)  11.5 us
    ppermute x10, waiting for transfers between devices, per_device(): rows.append(lax.ppermute(logs, 'seq', pairs))  8.95 us
    all_to_all x1, starting transfers between devices, per_device(): lax.all_to_all(entries, 'seq', 0, 0, tiled=True)  7.58 us
    pallas_call x1, Pallas kernels, inside_call(): pl.pallas_call(inside_kernel, grid=(STEPS,), in_specs=[columns, columns,...  6.48 us
    pallas_call x1, Pallas kernels, final_call(): pl.pallas_call(final_kernel, in_specs=[pl.BlockSpec(memory_space=pltpu.VM...  5.04 us
  transfers between devices with their start and end apart: 12, of which 6 were waited for; matrix products, arithmetic and copies ran while one was open for 1% of the time, Pallas kernels for 6%

profile of v6, /device:TPU:32, one launch (start us, length us, event | category | flops | bytes accessed | tf_op | source)
XLA Modules:
  0.0 103.3 jit_solution(7952460339319171824)
XLA Ops:
  0.0 4.1 %span_states.1 = (bf16[2,16,128,128]{3,2,1,0:T(8,128)(2,1)}, f32[1,128]{1,0:T(1,128)}) custom-call(bf16[256,2048]{1,0:T(8,128)(2,1)} %x_hbm.1, f32[32,256]{1,0:T(8,128)} %rf_hbm.1, f32[32,256]{1,0:T(8,128)} %rb_hbm.1, bf16[256,128]{1,0:T(8,128)(2,1)} %bf_hbm.1, bf16[256,128]{1,0:T(8,128)(2,1)} %bb_hbm.1), custom_call_target="tpu_custom_call" | custom-call | tf_op jit(solution)/shard_map/span_states/pallas_call | solution.py:126
  4.1 0.0 copy-start.1
  4.1 0.0 copy-start.2
  4.1 0.0 copy-start.3
  4.1 0.0 copy-start.4
  4.1 0.0 copy-start.5
  4.1 0.0 copy-start.6
  4.2 11.5 %all-to-all-start = ((bf16[32,128,128]{2,1,0:T(8,128)(2,1)}), bf16[32,128,128]{2,1,0:T(8,128)(2,1)S(1)}, u32[]{:S(2)}, u32[]{:S(2)}) async-start(bf16[32,128,128]{2,1,0:T(8,128)(2,1)} %bitcast.10), calls=%async_computation | async-start | bytes 2097152 | tf_op jit(solution)/shard_map/all_to_all | solution.py:347
  15.7 2.8 %collective-permute-start.2 = (f32[1,128]{1,0:T(1,128)}, f32[1,128]{1,0:T(1,128)S(1)}, u32[]{:S(2)}, u32[]{:S(2)}) collective-permute-start(f32[1,128]{1,0:T(1,128)} %get-tuple-element.13), channel_id=1, source_target_pairs={{0,24},{1,25},{2,26},{3,27},{4,28},{5,29},{6,30},{7,31},{8,0},{9,1... | collective-permute-start | bytes 1544 | tf_op jit(solution)/shard_map/ppermute | solution.py:351
  18.5 0.8 collective-permute-start.1
  19.3 0.9 collective-permute-start
  20.1 0.0 collective-permute-done.2
  20.1 3.4 %collective-permute-done.1 = f32[1,128]{1,0:T(1,128)S(1)} collective-permute-done((f32[1,128]{1,0:T(1,128)}, f32[1,128]{1,0:T(1,128)S(1)}, u32[]{:S(2)}, u32[]{:S(2)}) %collective-permute-start.1) | collective-permute-done | bytes 544 | tf_op jit(solution)/shard_map/ppermute | solution.py:351
  23.6 0.5 collective-permute-done
  24.1 0.7 pad_maximum_fusion
  24.8 0.6 collective-permute-start.9
  25.3 3.6 %collective-permute-start.8 = (f32[4,128]{1,0:T(4,128)S(1)}, f32[4,128]{1,0:T(4,128)S(1)}, u32[]{:S(2)}, u32[]{:S(2)}) collective-permute-start(f32[4,128]{1,0:T(4,128)S(1)} %pad_maximum_fusion), channel_id=1, source_target_pairs={{0,6},{1,7},{2,0},{3,1},{4,2},{5,3},{6,4},{7,5},{8,14},{9,15},{10,... | collective-permute-start | bytes 6152 | tf_op jit(solution)/shard_map/ppermute | solution.py:356
  28.9 2.4 %collective-permute-start.7 = (f32[4,128]{1,0:T(4,128)S(1)}, f32[4,128]{1,0:T(4,128)S(1)}, u32[]{:S(2)}, u32[]{:S(2)}) collective-permute-start(f32[4,128]{1,0:T(4,128)S(1)} %pad_maximum_fusion), channel_id=1, source_target_pairs={{0,5},{1,6},{2,7},{3,0},{4,1},{5,2},{6,3},{7,4},{8,13},{9,14},{10,... | collective-permute-start | bytes 6152 | tf_op jit(solution)/shard_map/ppermute | solution.py:356
  31.3 2.7 %collective-permute-start.6 = (f32[4,128]{1,0:T(4,128)S(1)}, f32[4,128]{1,0:T(4,128)S(1)}, u32[]{:S(2)}, u32[]{:S(2)}) collective-permute-start(f32[4,128]{1,0:T(4,128)S(1)} %pad_maximum_fusion), channel_id=1, source_target_pairs={{0,4},{1,5},{2,6},{3,7},{4,0},{5,1},{6,2},{7,3},{8,12},{9,13},{10,... | collective-permute-start | bytes 6152 | tf_op jit(solution)/shard_map/ppermute | solution.py:356
  33.9 2.4 %collective-permute-start.5 = (f32[4,128]{1,0:T(4,128)S(1)}, f32[4,128]{1,0:T(4,128)S(1)}, u32[]{:S(2)}, u32[]{:S(2)}) collective-permute-start(f32[4,128]{1,0:T(4,128)S(1)} %pad_maximum_fusion), channel_id=1, source_target_pairs={{0,3},{1,4},{2,5},{3,6},{4,7},{5,0},{6,1},{7,2},{8,11},{9,12},{10,... | collective-permute-start | bytes 6152 | tf_op jit(solution)/shard_map/ppermute | solution.py:356
  36.3 2.9 %collective-permute-done.9 = f32[4,128]{1,0:T(4,128)S(1)} collective-permute-done((f32[4,128]{1,0:T(4,128)S(1)}, f32[4,128]{1,0:T(4,128)S(1)}, u32[]{:S(2)}, u32[]{:S(2)}) %collective-permute-start.9) | collective-permute-done | bytes 2080 | tf_op jit(solution)/shard_map/ppermute | solution.py:356
  39.3 3.5 %collective-permute-start.4 = (f32[4,128]{1,0:T(4,128)S(1)}, f32[4,128]{1,0:T(4,128)S(1)}, u32[]{:S(2)}, u32[]{:S(2)}) collective-permute-start(f32[4,128]{1,0:T(4,128)S(1)} %pad_maximum_fusion), channel_id=1, source_target_pairs={{0,2},{1,3},{2,4},{3,5},{4,6},{5,7},{6,0},{7,1},{8,10},{9,11},{10,... | collective-permute-start | bytes 6152 | tf_op jit(solution)/shard_map/ppermute | solution.py:356
  42.8 0.0 collective-permute-done.8
  42.8 1.4 %collective-permute-start.3 = (f32[4,128]{1,0:T(4,128)S(1)}, f32[4,128]{1,0:T(4,128)S(1)}, u32[]{:S(2)}, u32[]{:S(2)}) collective-permute-start(f32[4,128]{1,0:T(4,128)S(1)} %pad_maximum_fusion), channel_id=1, source_target_pairs={{0,1},{1,2},{2,3},{3,4},{4,5},{5,6},{6,7},{7,0},{8,9},{9,10},{10,1... | collective-permute-start | bytes 6152 | tf_op jit(solution)/shard_map/ppermute | solution.py:356
  44.2 0.1 stack.23.place_ref
  44.3 0.0 collective-permute-done.7
  44.3 0.0 collective-permute-done.6
  44.3 0.0 collective-permute-done.5
  44.3 0.6 collective-permute-done.4
  45.0 1.4 %collective-permute-done.3 = f32[4,128]{1,0:T(4,128)S(1)} collective-permute-done((f32[4,128]{1,0:T(4,128)S(1)}, f32[4,128]{1,0:T(4,128)S(1)}, u32[]{:S(2)}, u32[]{:S(2)}) %collective-permute-start.3) | collective-permute-done | bytes 2080 | tf_op jit(solution)/shard_map/ppermute | solution.py:356
  46.4 0.7 concatenate.8.logs_ref
  47.1 0.0 all-to-all-done.parts_ref
  47.1 1.0 group_totals.1
  48.1 12.0 %all_to_all.15.totals_ref = bf16[8,144,128]{2,1,0:T(8,128)(2,1)S(1)} all-to-all(bf16[8,144,128]{2,1,0:T(8,128)(2,1)S(1)} %group_totals.1), channel_id=1, replica_groups=mesh['grp'=8,'seq'=32] {'grp'}, dimensions={0} | all-to-all | bytes 589824 | tf_op jit(solution)/shard_map/all_to_all | solution.py:368
  60.1 1.7 %entry_states.1 = bf16[32,128,128]{2,1,0:T(8,128)(2,1)} custom-call(s32[5]{0:T(128)S(1)} %stack.23.place_ref, bf16[8,144,128]{2,1,0:T(8,128)(2,1)S(1)} %all_to_all.15.totals_ref, f32[32,128]{1,0:T(8,128)S(1)} %concatenate.8.logs_ref, bf16[32,128,128]{2,1,0:T(8,128)(2,1)S(1)} %all-to-all-done.parts_ref), custom_call_target="tpu_custom_call" | custom-call | tf_op jit(solution)/shard_map/entry_states/pallas_call | solution.py:369
  61.9 7.6 %all-to-all-start.2 = ((bf16[32,128,128]{2,1,0:T(8,128)(2,1)}), bf16[32,128,128]{2,1,0:T(8,128)(2,1)S(1)}, u32[]{:S(2)}, u32[]{:S(2)}) async-start(bf16[32,128,128]{2,1,0:T(8,128)(2,1)} %entry_states.1), calls=%async_computation.2 | async-start | bytes 2097152 | tf_op jit(solution)/shard_map/all_to_all | solution.py:382
  69.4 0.0 copy-done.1
  69.5 0.0 copy-done.2
  69.5 0.0 copy-done.3
  69.5 0.0 copy-done.4
  69.5 0.0 copy-done.5
  69.5 0.0 copy-done.6
  69.5 0.0 copy-start
  69.5 1.2 %copy-done = bf16[256,2048]{1,0:T(8,128)(2,1)S(1)} copy-done((bf16[256,2048]{1,0:T(8,128)(2,1)S(1)}, bf16[256,2048]{1,0:T(8,128)(2,1)}, u32[]{:S(2)}) %copy-start) | copy-done | bytes 1048600
  70.7 1.2 %copy-done.8 = bf16[256,2048]{1,0:T(8,128)(2,1)S(1)} copy-done((bf16[256,2048]{1,0:T(8,128)(2,1)S(1)}, bf16[256,2048]{1,0:T(8,128)(2,1)}, u32[]{:S(2)}) %copy-start.8) | copy-done | bytes 1048600
  72.0 6.5 %inside_spans.1 = (bf16[256,2048]{1,0:T(8,128)(2,1)S(1)}, bf16[256,2048]{1,0:T(8,128)(2,1)S(1)}, bf16[256,128]{1,0:T(8,128)(2,1)S(1)}) custom-call(bf16[256,2048]{1,0:T(8,128)(2,1)S(1)} %copy-done, bf16[256,2048]{1,0:T(8,128)(2,1)S(1)} %copy-done.8, f32[32,256]{1,0:T(8,128)S(1)} %copy-done.5, f32[32,256]{1,0:T(8,128)S(1)} %copy-done.6, ...), custom_call_target="tpu_custom_call" | custom-call | flops 536870912 | bytes 4194304 | tf_op jit(solution)/shard_map/inside_spans/pallas_call | solution.py:195
  78.4 19.6 %all-to-all-done.2 = bf16[32,128,128]{2,1,0:T(8,128)(2,1)S(1)} async-done(((bf16[32,128,128]{2,1,0:T(8,128)(2,1)}), bf16[32,128,128]{2,1,0:T(8,128)(2,1)S(1)}, u32[]{:S(2)}, u32[]{:S(2)}) %all-to-all-start.2) | async-done | bytes 1048608 | tf_op jit(solution)/shard_map/all_to_all | solution.py:382
  98.1 5.0 %gate_norm_project.1 = bf16[256,1024]{1,0:T(8,128)(2,1)} custom-call(bf16[256,2048]{1,0:T(8,128)(2,1)S(1)} %get-tuple-element.10.in_ref, bf16[256,2048]{1,0:T(8,128)(2,1)S(1)} %get-tuple-element.11.silu_ref, bf16[256,128]{1,0:T(8,128)(2,1)S(1)} %get-tuple-element.12.scale_ref, bf16[2,16,128,128]{3,2,1,0:T(8,128)(2,1)S(1)} %bitcast.8, ...), custom_call_target="tpu_custom_call" | custom-call | tf_op jit(solution)/shard_map/gate_norm_project/pallas_call | solution.py:319
  (3 shorter events, 0.0 us)
Async XLA Ops:
  4.1 65.4 %copy-start.1 = (bf16[256,128]{1,0:T(8,128)(2,1)S(1)}, bf16[256,128]{1,0:T(8,128)(2,1)}, u32[]{:S(2)}) copy-start(bf16[256,128]{1,0:T(8,128)(2,1)} %cf_ref.3) | copy-start | bytes 196612
  4.1 65.4 %copy-start.2 = (bf16[256,128]{1,0:T(8,128)(2,1)S(1)}, bf16[256,128]{1,0:T(8,128)(2,1)}, u32[]{:S(2)}) copy-start(bf16[256,128]{1,0:T(8,128)(2,1)} %cb_ref.3) | copy-start | bytes 196612
  4.1 65.4 %copy-start.3 = (bf16[256,128]{1,0:T(8,128)(2,1)S(1)}, bf16[256,128]{1,0:T(8,128)(2,1)}, u32[]{:S(2)}) copy-start(bf16[256,128]{1,0:T(8,128)(2,1)} %bf_hbm.1) | copy-start | bytes 196612
  4.1 65.4 %copy-start.4 = (bf16[256,128]{1,0:T(8,128)(2,1)S(1)}, bf16[256,128]{1,0:T(8,128)(2,1)}, u32[]{:S(2)}) copy-start(bf16[256,128]{1,0:T(8,128)(2,1)} %bb_hbm.1) | copy-start | bytes 196612
  4.1 65.4 %copy-start.5 = (f32[32,256]{1,0:T(8,128)S(1)}, f32[32,256]{1,0:T(8,128)}, u32[]{:S(2)}) copy-start(f32[32,256]{1,0:T(8,128)} %rf_hbm.1) | copy-start | bytes 98308
  4.1 65.4 %copy-start.6 = (f32[32,256]{1,0:T(8,128)S(1)}, f32[32,256]{1,0:T(8,128)}, u32[]{:S(2)}) copy-start(f32[32,256]{1,0:T(8,128)} %rb_hbm.1) | copy-start | bytes 98308
  4.2 43.0 %all-to-all-start = ((bf16[32,128,128]{2,1,0:T(8,128)(2,1)}), bf16[32,128,128]{2,1,0:T(8,128)(2,1)S(1)}, u32[]{:S(2)}, u32[]{:S(2)}) async-start(bf16[32,128,128]{2,1,0:T(8,128)(2,1)} %bitcast.10), calls=%async_computation | async-start | bytes 2097152 | tf_op jit(solution)/shard_map/all_to_all | solution.py:347
  15.7 4.5 %collective-permute-start.2 = (f32[1,128]{1,0:T(1,128)}, f32[1,128]{1,0:T(1,128)S(1)}, u32[]{:S(2)}, u32[]{:S(2)}) collective-permute-start(f32[1,128]{1,0:T(1,128)} %get-tuple-element.13), channel_id=1, source_target_pairs={{0,24},{1,25},{2,26},{3,27},{4,28},{5,29},{6,30},{7,31},{8,0},{9,1... | collective-permute-start | bytes 1544 | tf_op jit(solution)/shard_map/ppermute | solution.py:351
  18.5 5.1 %collective-permute-start.1 = (f32[1,128]{1,0:T(1,128)}, f32[1,128]{1,0:T(1,128)S(1)}, u32[]{:S(2)}, u32[]{:S(2)}) collective-permute-start(f32[1,128]{1,0:T(1,128)} %get-tuple-element.13), channel_id=1, source_target_pairs={{0,16},{1,17},{2,18},{3,19},{4,20},{5,21},{6,22},{7,23},{8,24},{9,... | collective-permute-start | bytes 1544 | tf_op jit(solution)/shard_map/ppermute | solution.py:351
  19.3 4.8 %collective-permute-start = (f32[1,128]{1,0:T(1,128)}, f32[1,128]{1,0:T(1,128)S(1)}, u32[]{:S(2)}, u32[]{:S(2)}) collective-permute-start(f32[1,128]{1,0:T(1,128)} %get-tuple-element.13), channel_id=1, source_target_pairs={{0,8},{1,9},{2,10},{3,11},{4,12},{5,13},{6,14},{7,15},{8,16},{9,17... | collective-permute-start | bytes 1544 | tf_op jit(solution)/shard_map/ppermute | solution.py:351
  24.8 14.5 %collective-permute-start.9 = (f32[4,128]{1,0:T(4,128)S(1)}, f32[4,128]{1,0:T(4,128)S(1)}, u32[]{:S(2)}, u32[]{:S(2)}) collective-permute-start(f32[4,128]{1,0:T(4,128)S(1)} %pad_maximum_fusion), channel_id=1, source_target_pairs={{0,7},{1,0},{2,1},{3,2},{4,3},{5,4},{6,5},{7,6},{8,15},{9,8},{10,9... | collective-permute-start | bytes 6152 | tf_op jit(solution)/shard_map/ppermute | solution.py:356
  25.3 17.5 %collective-permute-start.8 = (f32[4,128]{1,0:T(4,128)S(1)}, f32[4,128]{1,0:T(4,128)S(1)}, u32[]{:S(2)}, u32[]{:S(2)}) collective-permute-start(f32[4,128]{1,0:T(4,128)S(1)} %pad_maximum_fusion), channel_id=1, source_target_pairs={{0,6},{1,7},{2,0},{3,1},{4,2},{5,3},{6,4},{7,5},{8,14},{9,15},{10,... | collective-permute-start | bytes 6152 | tf_op jit(solution)/shard_map/ppermute | solution.py:356
  28.9 15.4 %collective-permute-start.7 = (f32[4,128]{1,0:T(4,128)S(1)}, f32[4,128]{1,0:T(4,128)S(1)}, u32[]{:S(2)}, u32[]{:S(2)}) collective-permute-start(f32[4,128]{1,0:T(4,128)S(1)} %pad_maximum_fusion), channel_id=1, source_target_pairs={{0,5},{1,6},{2,7},{3,0},{4,1},{5,2},{6,3},{7,4},{8,13},{9,14},{10,... | collective-permute-start | bytes 6152 | tf_op jit(solution)/shard_map/ppermute | solution.py:356
  31.3 13.1 %collective-permute-start.6 = (f32[4,128]{1,0:T(4,128)S(1)}, f32[4,128]{1,0:T(4,128)S(1)}, u32[]{:S(2)}, u32[]{:S(2)}) collective-permute-start(f32[4,128]{1,0:T(4,128)S(1)} %pad_maximum_fusion), channel_id=1, source_target_pairs={{0,4},{1,5},{2,6},{3,7},{4,0},{5,1},{6,2},{7,3},{8,12},{9,13},{10,... | collective-permute-start | bytes 6152 | tf_op jit(solution)/shard_map/ppermute | solution.py:356
  33.9 10.4 %collective-permute-start.5 = (f32[4,128]{1,0:T(4,128)S(1)}, f32[4,128]{1,0:T(4,128)S(1)}, u32[]{:S(2)}, u32[]{:S(2)}) collective-permute-start(f32[4,128]{1,0:T(4,128)S(1)} %pad_maximum_fusion), channel_id=1, source_target_pairs={{0,3},{1,4},{2,5},{3,6},{4,7},{5,0},{6,1},{7,2},{8,11},{9,12},{10,... | collective-permute-start | bytes 6152 | tf_op jit(solution)/shard_map/ppermute | solution.py:356
  39.3 5.7 %collective-permute-start.4 = (f32[4,128]{1,0:T(4,128)S(1)}, f32[4,128]{1,0:T(4,128)S(1)}, u32[]{:S(2)}, u32[]{:S(2)}) collective-permute-start(f32[4,128]{1,0:T(4,128)S(1)} %pad_maximum_fusion), channel_id=1, source_target_pairs={{0,2},{1,3},{2,4},{3,5},{4,6},{5,7},{6,0},{7,1},{8,10},{9,11},{10,... | collective-permute-start | bytes 6152 | tf_op jit(solution)/shard_map/ppermute | solution.py:356
  42.8 3.6 %collective-permute-start.3 = (f32[4,128]{1,0:T(4,128)S(1)}, f32[4,128]{1,0:T(4,128)S(1)}, u32[]{:S(2)}, u32[]{:S(2)}) collective-permute-start(f32[4,128]{1,0:T(4,128)S(1)} %pad_maximum_fusion), channel_id=1, source_target_pairs={{0,1},{1,2},{2,3},{3,4},{4,5},{5,6},{6,7},{7,0},{8,9},{9,10},{10,1... | collective-permute-start | bytes 6152 | tf_op jit(solution)/shard_map/ppermute | solution.py:356
  60.1 37.9 %copy-start.7 = (f32[2048]{0:T(1024)S(1)}, f32[2048]{0:T(1024)}, u32[]{:S(2)}) copy-start(f32[2048]{0:T(1024)} %param.18) | copy-start | bytes 24580
  61.9 36.2 %all-to-all-start.2 = ((bf16[32,128,128]{2,1,0:T(8,128)(2,1)}), bf16[32,128,128]{2,1,0:T(8,128)(2,1)S(1)}, u32[]{:S(2)}, u32[]{:S(2)}) async-start(bf16[32,128,128]{2,1,0:T(8,128)(2,1)} %entry_states.1), calls=%async_computation.2 | async-start | bytes 2097152 | tf_op jit(solution)/shard_map/all_to_all | solution.py:382
  69.5 1.2 %copy-start = (bf16[256,2048]{1,0:T(8,128)(2,1)S(1)}, bf16[256,2048]{1,0:T(8,128)(2,1)}, u32[]{:S(2)}) copy-start(bf16[256,2048]{1,0:T(8,128)(2,1)} %x_hbm.1) | copy-start | bytes 3145732
  70.7 1.2 %copy-start.8 = (bf16[256,2048]{1,0:T(8,128)(2,1)S(1)}, bf16[256,2048]{1,0:T(8,128)(2,1)}, u32[]{:S(2)}) copy-start(bf16[256,2048]{1,0:T(8,128)(2,1)} %gate_ref.1) | copy-start | bytes 3145732

commit v7 on v4

--- a/solution.py
+++ b/solution.py
@@ -15,9 +15,12 @@
 BLK = 256
 STEPS = E // BLK
 FW = 256
-FINAL_VMEM = 59400000
+FINAL_VMEM = 48 * 1024 * 1024
 HPB = BLK // HEAD
 ROWS = N + 16
+SHARE = N // 2
+HALF = E // 2
+PART = SHARE + 16
 LOG2E = 1.4426950408889634
 F32 = jnp.float32
 BF16 = jnp.bfloat16
@@ -68,16 +71,20 @@
     return jnp.dot(a, b, preferred_element_type=F32)
 
 
-def three_rows(value, width):
-    high, rest = two_parts(value)
-    middle, low = two_parts(rest)
+def tail_rows(values, width):
     row = lax.broadcasted_iota(jnp.int32, (16, width), 0)
-    tail = jnp.where(row == 0, high, jnp.where(row == 1, middle, jnp.where(row == 2, low, 0.0)))
+    tail = jnp.zeros((16, width), F32)
+    for i, value in enumerate(values):
+        high, rest = two_parts(value)
+        middle, low = two_parts(rest)
+        for k, part in enumerate((high, middle, low)):
+            tail = jnp.where(row == 3 * i + k, part, tail)
     return tail.astype(BF16)
 
 
 def state_kernel(
-    x_hbm, rf_hbm, rb_hbm, bf_hbm, bb_hbm, out_ref, x_ref, r_ref, b_ref, select_ref, sems
+    x_hbm, rf_hbm, rb_hbm, bf_hbm, bb_hbm, out_hbm,
+    x_ref, r_ref, b_ref, select_ref, out_ref, sems,
 ):
     copies = [
         pltpu.make_async_copy(rf_hbm, r_ref.at[0], sems.at[0]),
@@ -91,42 +98,57 @@
     select_ref[...] = head_select(0, 2 * H, E, 0)
     copies[0].wait()
     copies[1].wait()
-    scales = []
+    scales, keeps = [], []
+    lane = lax.broadcasted_iota(jnp.int32, (H, 128), 1)
     for d, sums in enumerate((lane_sums, lane_sums_back)):
         r = r_ref[d]
         c = sums(r)
         total = c[:, Q - 1 : Q] if d == 0 else c[:, 0:1]
         parts = two_parts(step_of(r) * jnp.exp(c - total))
         scales.append(jnp.concatenate(parts, axis=0).T.astype(BF16))
-        keep = jnp.broadcast_to(jnp.exp(-total), (H, 128))
-        lane = lax.broadcasted_iota(jnp.int32, (H, 128), 1)
-        for k in range(E // 128):
-            own = jnp.where(lane < HEAD, keep[2 * k : 2 * k + 1], keep[2 * k + 1 : 2 * k + 2])
-            out_ref[d, k, N:ROWS, :] = three_rows(own[:1], 128)
+        keeps.append(jnp.broadcast_to(jnp.exp(-total), (H, 128)))
+    for k in range(E // 128):
+        own = [
+            jnp.where(lane[:1] < HEAD, keep[2 * k : 2 * k + 1], keep[2 * k + 1 : 2 * k + 2])
+            for keep in keeps
+        ]
+        tail = tail_rows(own, 128)
+        out_ref[2 * k, N:ROWS, :] = tail
+        out_ref[2 * k + 1, N:ROWS, :] = tail
     copies[2].wait()
     copies[3].wait()
     turned = [b_ref[d].astype(F32).T.astype(BF16) for d in range(2)]
     copies[4].wait()
-    x = x_ref[...].astype(F32)
-    for d in range(2):
-        factor = dot(scales[d], select_ref[...])
-        s = dot(turned[d], (x * factor).astype(BF16)).astype(BF16)
-        for k in range(E // 128):
-            out_ref[d, k, 0:N, :] = s[:, 128 * k : 128 * (k + 1)]
+    for part in range(2):
+        x = x_ref[:, HALF * part : HALF * (part + 1)].astype(F32)
+        for d in range(2):
+            factor = dot(scales[d], select_ref[:, HALF * part : HALF * (part + 1)])
+            s = dot(turned[d], (x * factor).astype(BF16)).astype(BF16)
+            for k in range(HALF // 128):
+                for n in range(2):
+                    out_ref[HALF // 64 * part + 2 * k + n, SHARE * d : SHARE * (d + 1), :] = s[
+                        SHARE * n : SHARE * (n + 1), 128 * k : 128 * (k + 1)
+                    ]
+        span = pl.ds(HALF // 64 * part, HALF // 64)
+        copies.append(pltpu.make_async_copy(out_ref.at[span], out_hbm.at[span], sems.at[5 + part]))
+        copies[-1].start()
+    copies[5].wait()
+    copies[6].wait()
 
 
 def state_call(x, rate_f, rate_b, b_f, b_b):
     return pl.pallas_call(
         state_kernel,
         in_specs=[pl.BlockSpec(memory_space=pltpu.HBM)] * 5,
-        out_specs=pl.BlockSpec(memory_space=pltpu.VMEM),
-        out_shape=jax.ShapeDtypeStruct((2, E // 128, ROWS, 128), BF16),
+        out_specs=pl.BlockSpec(memory_space=pltpu.HBM),
+        out_shape=jax.ShapeDtypeStruct((2 * E // 128, ROWS, 128), BF16),
         scratch_shapes=[
             pltpu.VMEM((Q, E), BF16),
             pltpu.VMEM((2, H, Q), F32),
             pltpu.VMEM((2, Q, N), BF16),
             pltpu.VMEM((2 * H, E), BF16),
-            pltpu.SemaphoreType.DMA((5,)),
+            pltpu.VMEM((2 * E // 128, ROWS, 128), BF16),
+            pltpu.SemaphoreType.DMA((7,)),
         ],
         compiler_params=pltpu.CompilerParams(vmem_limit_bytes=60 * 1024 * 1024),
         name="span_states",
@@ -201,59 +223,82 @@
     )(x, gate, rate_f, rate_b, b_f, c_f, b_b, c_b)
 
 
-def read_part(ref, index):
-    state = ref[index, 0:N, :].astype(F32)
+def read_part(ref, index, d):
+    state = ref[index, SHARE * d : SHARE * (d + 1), :].astype(F32)
     tail = ref[index, N:ROWS, :].astype(F32)
-    return state, tail[0:1] + tail[1:2] + tail[2:3]
-
-
-def total_kernel(count, copies, place_ref, parts_ref, out_ref):
-    backward = place_ref[0]
-
+    return state, tail[3 * d : 3 * d + 1] + tail[3 * d + 1 : 3 * d + 2] + tail[3 * d + 2 : 3 * d + 3]
+
+
+def total_kernel(count, groups, group_ref, parts_ref, out_ref):
     def step(i, carried):
-        state, kept = carried
-        index = jnp.where(backward == 1, count - 1 - i, i)
-        own, keep = read_part(parts_ref, index)
-        return keep * state + own, keep * kept
-
-    state, kept = lax.fori_loop(
-        0, count, step, (jnp.zeros((N, 128), F32), jnp.ones((1, 128), F32)), unroll=4
+        result = []
+        for d in range(2):
+            state, kept = carried[2 * d : 2 * d + 2]
+            own, keep = read_part(parts_ref, i if d == 0 else count - 1 - i, d)
+            result += [keep * state + own, keep * kept]
+        return tuple(result)
+
+    start = (jnp.zeros((SHARE, 128), F32), jnp.ones((1, 128), F32))
+    result = lax.fori_loop(0, count, step, start + start, unroll=4)
+    states = [result[2 * d].astype(BF16) for d in range(2)]
+    tails = [tail_rows([result[2 * d + 1]], 128) for d in range(2)]
+    for g in range(groups):
+        later = g > group_ref[0]
+
+        @pl.when(later)
+        def _():
+            out_ref[g, 0:SHARE, :] = states[0]
+            out_ref[g, SHARE:PART, :] = tails[0]
+
+        @pl.when(jnp.logical_not(later))
+        def _():
+            out_ref[g, 0:SHARE, :] = states[1]
+            out_ref[g, SHARE:PART, :] = tails[1]
+
+
+def entry_kernel(count, groups, group_ref, totals_ref, parts_ref, out_hbm, out_ref, sems):
+    group = group_ref[0]
+
+    def outer(index, state):
+        own = totals_ref[index, 0:SHARE, :].astype(F32)
+        tail = totals_ref[index, SHARE:PART, :].astype(F32)
+        return (tail[0:1] + tail[1:2] + tail[2:3]) * state + own
+
+    empty = jnp.zeros((SHARE, 128), F32)
+    forward = lax.fori_loop(0, group, outer, empty)
+    backward = lax.fori_loop(
+        0, groups - 1 - group, lambda i, state: outer(groups - 1 - i, state), empty
     )
-    tail = three_rows(kept, 128)
-    for g in range(copies):
-        out_ref[g, 0:N, :] = state.astype(BF16)
-        out_ref[g, N:ROWS, :] = tail
-
-
-def entry_kernel(count, groups, place_ref, totals_ref, parts_ref, out_ref):
-    backward, mine = place_ref[0], place_ref[1]
-
-    def outer(i, state):
-        index = jnp.where(backward == 1, groups - 1 - i, i)
-        own, keep = read_part(totals_ref, index)
-        return keep * state + own
-
-    state = lax.fori_loop(0, mine, outer, jnp.zeros((N, 128), F32))
-
-    def step(i, state):
-        index = jnp.where(backward == 1, count - 1 - i, i)
-        out_ref[index] = state.astype(BF16)
-        own, keep = read_part(parts_ref, index)
-        return keep * state + own
-
-    lax.fori_loop(0, count, step, state, unroll=4)
+    states = [forward, backward]
+    for i in range(count):
+        for d in range(2):
+            index = i if d == 0 else count - 1 - i
+            out_ref[index, SHARE * d : SHARE * (d + 1), :] = states[d].astype(BF16)
+            own, keep = read_part(parts_ref, index, d)
+            states[d] = keep * states[d] + own
+    copy = pltpu.make_async_copy(out_ref, out_hbm, sems.at[0])
+    copy.start()
+    copy.wait()
 
 
 def vmem_specs(n):
     return [pl.BlockSpec(memory_space=pltpu.SMEM)] + [pl.BlockSpec(memory_space=pltpu.VMEM)] * n
 
 
+def state_of(ref, d, block):
+    rows = pl.ds(SHARE * d, SHARE)
+    return jnp.concatenate([ref[2 * block, rows, :], ref[2 * block + 1, rows, :]], axis=0)
+
+
 def final_kernel(
     in_ref, silu_ref, scale_ref, m_ref, cf_ref, cb_ref, gain_ref, w_hbm,
-    out_ref, normed_ref, w_ref, sem,
+    out_ref, normed_ref, w_ref, sems,
 ):
-    copy = pltpu.make_async_copy(w_hbm, w_ref, sem)
-    copy.start()
+    copies = []
+    for i in range(4):
+        rows = pl.ds(E // 4 * i, E // 4)
+        copies.append(pltpu.make_async_copy(w_hbm.at[rows], w_ref.at[rows], sems.at[i]))
+        copies[-1].start()
     scales = [scale_ref[:, 2 * H * d : 2 * H * (d + 1)] for d in range(2)]
     square = jnp.zeros((Q, 128), F32)
     for j in range(E // FW):
@@ -261,7 +306,7 @@
         y = in_ref[:, at].astype(F32)
         select = head_select(j, 2 * H, FW, 0)
         for d, c_ref in enumerate((cf_ref, cb_ref)):
-            m = jnp.concatenate([m_ref[d, FW // 128 * j + k] for k in range(FW // 128)], axis=1)
+            m = jnp.concatenate([state_of(m_ref, d, FW // 128 * j + k) for k in range(FW // 128)], 1)
             y = y + dot(scales[d], select) * dot(c_ref[...], m)
         gated = y * silu_ref[:, at].astype(F32)
         for k in range(FW // 128):
@@ -270,7 +315,8 @@
         normed_ref[:, at] = (gated * gain_ref[:, at]).astype(BF16)
     mean = jnp.sum(square, axis=1, keepdims=True) * (1.0 / E)
     scale = lax.rsqrt(mean + 1e-05)
-    copy.wait()
+    for copy in copies:
+        copy.wait()
     for n in range(D // 256):
         at = pl.ds(256 * n, 256)
         out_ref[:, at] = (dot(normed_ref[...], w_ref[:, at]) * scale).astype(BF16)
@@ -286,7 +332,7 @@
         scratch_shapes=[
             pltpu.VMEM((Q, E), BF16),
             pltpu.VMEM((E, D), BF16),
-            pltpu.SemaphoreType.DMA,
+            pltpu.SemaphoreType.DMA((4,)),
         ],
         compiler_params=pltpu.CompilerParams(vmem_limit_bytes=FINAL_VMEM),
         name="gate_norm_project",
@@ -299,17 +345,13 @@
 ):
     count, groups = lax.axis_size("seq"), lax.axis_size("grp")
     states = state_call(features, rate_forward, rate_backward, b_forward, b_backward)
-    states = states.reshape(count, ROWS, 128)
-    backward = (lax.axis_index("seq") >= count // 2).astype(jnp.int32)
-    group = lax.axis_index("grp")
-    mine = jnp.where(backward == 1, groups - 1 - group, group)
-    place = jnp.stack([backward, mine]).astype(jnp.int32)
+    place = lax.axis_index("grp").astype(jnp.int32).reshape(1)
     parts = lax.all_to_all(states, "seq", 0, 0, tiled=True)
     totals = pl.pallas_call(
         functools.partial(total_kernel, count, groups),
         in_specs=vmem_specs(1),
         out_specs=pl.BlockSpec(memory_space=pltpu.VMEM),
-        out_shape=jax.ShapeDtypeStruct((groups, ROWS, 128), BF16),
+        out_shape=jax.ShapeDtypeStruct((groups, PART, 128), BF16),
         compiler_params=LIMIT,
         name="group_totals",
     )(place, parts)
@@ -317,12 +359,16 @@
     entries = pl.pallas_call(
         functools.partial(entry_kernel, count, groups),
         in_specs=vmem_specs(2),
-        out_specs=pl.BlockSpec(memory_space=pltpu.VMEM),
+        out_specs=pl.BlockSpec(memory_space=pltpu.HBM),
         out_shape=jax.ShapeDtypeStruct((count, N, 128), BF16),
+        scratch_shapes=[
+            pltpu.VMEM((count, N, 128), BF16),
+            pltpu.SemaphoreType.DMA((1,)),
+        ],
         compiler_params=LIMIT,
         name="entry_states",
     )(place, totals, parts)
-    m = lax.all_to_all(entries, "seq", 0, 0, tiled=True).reshape(2, E // 128, N, 128)
+    m = lax.all_to_all(entries, "seq", 0, 0, tiled=True)
     inside, silu, scale = inside_call(
         features, gate_input, rate_forward, rate_backward,
         b_forward, c_forward, b_backward, c_backward,

time: 103 us -> 98.2 us (0.953)
  Pallas kernels: 19 us -> 17.2 us
  blocking collectives: 12 us -> 10.6 us
  local copies, waits for them, and re-layouts: 3.58 us -> 2.49 us
    all_to_all x1, blocking collectives: 12 us -> 10.6 us  [per_device(): totals = lax.all_to_all(totals, 'grp', 0, 0, tiled=True)]
    pallas_call x1, Pallas kernels: 6.13 us -> 5.02 us  [final_call(): pl.pallas_call(final_kernel, in_specs=[pl.BlockSpec(memory_space=pltpu.VM...]
    unnamed x24 -> x18, local copies, waits for them, and re-layouts: 3.58 us -> 2.49 us
  transfers between devices with their start and end apart: 2 -> 2, of which waited for: 2 -> 2; matrix products, arithmetic and copies ran while one was open for 0% -> 0% of each run, Pallas kernels for 6% -> 7%
where the time goes in v7:
time: 98.2 us; the launch traced here: 97.8 us
  waiting for transfers between devices  50.5 us (51%)
  Pallas kernels  17.2 us (18%)
  starting transfers between devices  16.8 us (17%)
  blocking collectives  10.6 us (11%)
  local copies, waits for them, and re-layouts  2.49 us (3%)
    all_to_all x1, waiting for transfers between devices, per_device(): parts = lax.all_to_all(states, 'seq', 0, 0, tiled=True)  31.2 us
    all_to_all x1, waiting for transfers between devices, per_device(): m = lax.all_to_all(entries, 'seq', 0, 0, tiled=True)  19.3 us
    all_to_all x1, starting transfers between devices, per_device(): parts = lax.all_to_all(states, 'seq', 0, 0, tiled=True)  11.4 us
    all_to_all x1, blocking collectives, per_device(): totals = lax.all_to_all(totals, 'grp', 0, 0, tiled=True)  10.6 us
    pallas_call x1, Pallas kernels, inside_call(): pl.pallas_call(inside_kernel, grid=(STEPS,), in_specs=[columns, columns,...  6.48 us
    all_to_all x1, starting transfers between devices, per_device(): m = lax.all_to_all(entries, 'seq', 0, 0, tiled=True)  5.46 us
    pallas_call x1, Pallas kernels, final_call(): pl.pallas_call(final_kernel, in_specs=[pl.BlockSpec(memory_space=pltpu.VM...  5.02 us
    pallas_call x1, Pallas kernels, state_call(): pl.pallas_call(state_kernel, in_specs=[pl.BlockSpec(memory_space=pltpu.HB...  3.98 us
  transfers between devices with their start and end apart: 2, of which 2 were waited for; matrix products, arithmetic and copies ran while one was open for 0% of the time, Pallas kernels for 7%

profile of v7, /device:TPU:32, one launch (start us, length us, event | category | flops | bytes accessed | tf_op | source)
XLA Modules:
  0.0 97.8 jit_solution(17761857933403554652)
XLA Ops:
  0.0 4.0 %span_states.1 = bf16[32,144,128]{2,1,0:T(8,128)(2,1)} custom-call(bf16[256,2048]{1,0:T(8,128)(2,1)} %x_hbm.1, f32[32,256]{1,0:T(8,128)} %rf_hbm.1, f32[32,256]{1,0:T(8,128)} %rb_hbm.1, bf16[256,128]{1,0:T(8,128)(2,1)} %bf_hbm.1, bf16[256,128]{1,0:T(8,128)(2,1)} %bb_hbm.1), custom_call_target="tpu_custom_call" | custom-call | tf_op jit(solution)/shard_map/span_states/pallas_call | solution.py:140
  4.0 11.4 %all-to-all-start = ((bf16[32,144,128]{2,1,0:T(8,128)(2,1)}), bf16[32,144,128]{2,1,0:T(8,128)(2,1)S(1)}, u32[]{:S(2)}, u32[]{:S(2)}) async-start(bf16[32,144,128]{2,1,0:T(8,128)(2,1)} %span_states.1), calls=%async_computation | async-start | bytes 2359296 | tf_op jit(solution)/shard_map/all_to_all | solution.py:349
  15.4 31.2 %all-to-all-done.parts_ref = bf16[32,144,128]{2,1,0:T(8,128)(2,1)S(1)} async-done(((bf16[32,144,128]{2,1,0:T(8,128)(2,1)}), bf16[32,144,128]{2,1,0:T(8,128)(2,1)S(1)}, u32[]{:S(2)}, u32[]{:S(2)}) %all-to-all-start) | async-done | bytes 1179680 | tf_op jit(solution)/shard_map/all_to_all | solution.py:349
  46.6 0.4 group_totals.1
  47.0 10.6 %all_to_all.15.totals_ref = bf16[8,80,128]{2,1,0:T(8,128)(2,1)S(1)} all-to-all(bf16[8,80,128]{2,1,0:T(8,128)(2,1)S(1)} %group_totals.1), channel_id=1, replica_groups=mesh['grp'=8,'seq'=32] {'grp'}, dimensions={0} | all-to-all | bytes 327680 | tf_op jit(solution)/shard_map/all_to_all | solution.py:358
  57.6 1.3 %entry_states.1 = bf16[32,128,128]{2,1,0:T(8,128)(2,1)} custom-call(s32[1]{0:T(128)} %bitcast.group_ref, bf16[8,80,128]{2,1,0:T(8,128)(2,1)S(1)} %all_to_all.15.totals_ref, bf16[32,144,128]{2,1,0:T(8,128)(2,1)S(1)} %all-to-all-done.parts_ref), custom_call_target="tpu_custom_call" | custom-call | tf_op jit(solution)/shard_map/entry_states/pallas_call | solution.py:359
  58.9 0.0 copy-start.1
  58.9 0.0 copy-start.2
  58.9 0.0 copy-start.3
  58.9 0.0 copy-start.4
  59.0 0.0 copy-start.5
  59.0 0.0 copy-start.6
  59.0 5.5 %all-to-all-start.2 = ((bf16[32,128,128]{2,1,0:T(8,128)(2,1)}), bf16[32,128,128]{2,1,0:T(8,128)(2,1)S(1)}, u32[]{:S(2)}, u32[]{:S(2)}) async-start(bf16[32,128,128]{2,1,0:T(8,128)(2,1)} %entry_states.1), calls=%async_computation.2 | async-start | bytes 2097152 | tf_op jit(solution)/shard_map/all_to_all | solution.py:371
  64.4 0.0 copy-done.1
  64.5 0.0 copy-done.2
  64.5 0.0 copy-done.3
  64.5 0.0 copy-done.4
  64.5 0.0 copy-done.5
  64.5 0.0 copy-done.6
  64.5 0.0 copy-start
  64.5 1.2 %copy-done = bf16[256,2048]{1,0:T(8,128)(2,1)S(1)} copy-done((bf16[256,2048]{1,0:T(8,128)(2,1)S(1)}, bf16[256,2048]{1,0:T(8,128)(2,1)}, u32[]{:S(2)}) %copy-start) | copy-done | bytes 1048600
  65.7 0.0 copy-start.8
  65.7 1.2 %copy-done.8 = bf16[256,2048]{1,0:T(8,128)(2,1)S(1)} copy-done((bf16[256,2048]{1,0:T(8,128)(2,1)S(1)}, bf16[256,2048]{1,0:T(8,128)(2,1)}, u32[]{:S(2)}) %copy-start.8) | copy-done | bytes 1048600
  67.0 0.0 copy-start.7
  67.0 6.5 %inside_spans.1 = (bf16[256,2048]{1,0:T(8,128)(2,1)S(1)}, bf16[256,2048]{1,0:T(8,128)(2,1)S(1)}, bf16[256,128]{1,0:T(8,128)(2,1)S(1)}) custom-call(bf16[256,2048]{1,0:T(8,128)(2,1)S(1)} %copy-done, bf16[256,2048]{1,0:T(8,128)(2,1)S(1)} %copy-done.8, f32[32,256]{1,0:T(8,128)S(1)} %copy-done.5, f32[32,256]{1,0:T(8,128)S(1)} %copy-done.6, ...), custom_call_target="tpu_custom_call" | custom-call | flops 536870912 | bytes 4194304 | tf_op jit(solution)/shard_map/inside_spans/pallas_call | solution.py:206
  73.4 19.3 %all-to-all-done.2.m_ref = bf16[32,128,128]{2,1,0:T(8,128)(2,1)S(1)} async-done(((bf16[32,128,128]{2,1,0:T(8,128)(2,1)}), bf16[32,128,128]{2,1,0:T(8,128)(2,1)S(1)}, u32[]{:S(2)}, u32[]{:S(2)}) %all-to-all-start.2) | async-done | bytes 1048608 | tf_op jit(solution)/shard_map/all_to_all | solution.py:371
  92.7 0.0 copy-done.7
  92.7 5.0 %gate_norm_project.1 = bf16[256,1024]{1,0:T(8,128)(2,1)} custom-call(bf16[256,2048]{1,0:T(8,128)(2,1)S(1)} %get-tuple-element.8.in_ref, bf16[256,2048]{1,0:T(8,128)(2,1)S(1)} %get-tuple-element.9.silu_ref, bf16[256,128]{1,0:T(8,128)(2,1)S(1)} %get-tuple-element.10.scale_ref, bf16[32,128,128]{2,1,0:T(8,128)(2,1)S(1)} %all-to-all-done.2.m_ref, ...), custom_call_target="tpu_custom_call" | custom-call | tf_op jit(solution)/shard_map/gate_norm_project/pallas_call | solution.py:326
Async XLA Ops:
  4.0 42.6 %all-to-all-start = ((bf16[32,144,128]{2,1,0:T(8,128)(2,1)}), bf16[32,144,128]{2,1,0:T(8,128)(2,1)S(1)}, u32[]{:S(2)}, u32[]{:S(2)}) async-start(bf16[32,144,128]{2,1,0:T(8,128)(2,1)} %span_states.1), calls=%async_computation | async-start | bytes 2359296 | tf_op jit(solution)/shard_map/all_to_all | solution.py:349
  58.9 5.5 %copy-start.1 = (bf16[256,128]{1,0:T(8,128)(2,1)S(1)}, bf16[256,128]{1,0:T(8,128)(2,1)}, u32[]{:S(2)}) copy-start(bf16[256,128]{1,0:T(8,128)(2,1)} %cf_ref.3) | copy-start | bytes 196612
  58.9 5.5 %copy-start.2 = (bf16[256,128]{1,0:T(8,128)(2,1)S(1)}, bf16[256,128]{1,0:T(8,128)(2,1)}, u32[]{:S(2)}) copy-start(bf16[256,128]{1,0:T(8,128)(2,1)} %cb_ref.3) | copy-start | bytes 196612
  58.9 5.5 %copy-start.3 = (bf16[256,128]{1,0:T(8,128)(2,1)S(1)}, bf16[256,128]{1,0:T(8,128)(2,1)}, u32[]{:S(2)}) copy-start(bf16[256,128]{1,0:T(8,128)(2,1)} %bf_hbm.1) | copy-start | bytes 196612
  58.9 5.5 %copy-start.4 = (bf16[256,128]{1,0:T(8,128)(2,1)S(1)}, bf16[256,128]{1,0:T(8,128)(2,1)}, u32[]{:S(2)}) copy-start(bf16[256,128]{1,0:T(8,128)(2,1)} %bb_hbm.1) | copy-start | bytes 196612
  59.0 5.5 %copy-start.5 = (f32[32,256]{1,0:T(8,128)S(1)}, f32[32,256]{1,0:T(8,128)}, u32[]{:S(2)}) copy-start(f32[32,256]{1,0:T(8,128)} %rf_hbm.1) | copy-start | bytes 98308
  59.0 5.5 %copy-start.6 = (f32[32,256]{1,0:T(8,128)S(1)}, f32[32,256]{1,0:T(8,128)}, u32[]{:S(2)}) copy-start(f32[32,256]{1,0:T(8,128)} %rb_hbm.1) | copy-start | bytes 98308
  59.0 33.8 %all-to-all-start.2 = ((bf16[32,128,128]{2,1,0:T(8,128)(2,1)}), bf16[32,128,128]{2,1,0:T(8,128)(2,1)S(1)}, u32[]{:S(2)}, u32[]{:S(2)}) async-start(bf16[32,128,128]{2,1,0:T(8,128)(2,1)} %entry_states.1), calls=%async_computation.2 | async-start | bytes 2097152 | tf_op jit(solution)/shard_map/all_to_all | solution.py:371
  64.5 1.2 %copy-start = (bf16[256,2048]{1,0:T(8,128)(2,1)S(1)}, bf16[256,2048]{1,0:T(8,128)(2,1)}, u32[]{:S(2)}) copy-start(bf16[256,2048]{1,0:T(8,128)(2,1)} %x_hbm.1) | copy-start | bytes 3145732
  65.7 1.2 %copy-start.8 = (bf16[256,2048]{1,0:T(8,128)(2,1)S(1)}, bf16[256,2048]{1,0:T(8,128)(2,1)}, u32[]{:S(2)}) copy-start(bf16[256,2048]{1,0:T(8,128)(2,1)} %gate_ref.1) | copy-start | bytes 3145732
  67.0 25.8 %copy-start.7 = (f32[2048]{0:T(1024)S(1)}, f32[2048]{0:T(1024)}, u32[]{:S(2)}) copy-start(f32[2048]{0:T(1024)} %param.18) | copy-start | bytes 24580

commit v8 on v7

--- a/solution.py
+++ b/solution.py
@@ -119,11 +119,11 @@
     copies[3].wait()
     turned = [b_ref[d].astype(F32).T.astype(BF16) for d in range(2)]
     copies[4].wait()
+    x = x_ref[...].astype(F32)
+    scaled = [(x * dot(scales[d], select_ref[...])).astype(BF16) for d in range(2)]
     for part in range(2):
-        x = x_ref[:, HALF * part : HALF * (part + 1)].astype(F32)
         for d in range(2):
-            factor = dot(scales[d], select_ref[:, HALF * part : HALF * (part + 1)])
-            s = dot(turned[d], (x * factor).astype(BF16)).astype(BF16)
+            s = dot(turned[d], scaled[d][:, HALF * part : HALF * (part + 1)]).astype(BF16)
             for k in range(HALF // 128):
                 for n in range(2):
                     out_ref[HALF // 64 * part + 2 * k + n, SHARE * d : SHARE * (d + 1), :] = s[
@@ -295,8 +295,8 @@
     out_ref, normed_ref, w_ref, sems,
 ):
     copies = []
-    for i in range(4):
-        rows = pl.ds(E // 4 * i, E // 4)
+    for i in range(2):
+        rows = pl.ds(E // 2 * i, E // 2)
         copies.append(pltpu.make_async_copy(w_hbm.at[rows], w_ref.at[rows], sems.at[i]))
         copies[-1].start()
     scales = [scale_ref[:, 2 * H * d : 2 * H * (d + 1)] for d in range(2)]
@@ -332,7 +332,7 @@
         scratch_shapes=[
             pltpu.VMEM((Q, E), BF16),
             pltpu.VMEM((E, D), BF16),
-            pltpu.SemaphoreType.DMA((4,)),
+            pltpu.SemaphoreType.DMA((2,)),
         ],
         compiler_params=pltpu.CompilerParams(vmem_limit_bytes=FINAL_VMEM),
         name="gate_norm_project",

time: 98.2 us -> 97.4 us (level)
  no operation moved by 1% of the time
where the time goes in v8:
time: 97.4 us; the launch traced here: 97 us
  waiting for transfers between devices  50.5 us (52%)
  starting transfers between devices  16.8 us (17%)
  Pallas kernels  16.4 us (17%)
  blocking collectives  10.6 us (11%)
  local copies, waits for them, and re-layouts  2.49 us (3%)
    all_to_all x1, waiting for transfers between devices, per_device(): parts = lax.all_to_all(states, 'seq', 0, 0, tiled=True)  31.2 us
    all_to_all x1, waiting for transfers between devices, per_device(): m = lax.all_to_all(entries, 'seq', 0, 0, tiled=True)  19.3 us
    all_to_all x1, starting transfers between devices, per_device(): parts = lax.all_to_all(states, 'seq', 0, 0, tiled=True)  11.4 us
    all_to_all x1, blocking collectives, per_device(): totals = lax.all_to_all(totals, 'grp', 0, 0, tiled=True)  10.6 us
    pallas_call x1, Pallas kernels, inside_call(): pl.pallas_call(inside_kernel, grid=(STEPS,), in_specs=[columns, columns,...  6.48 us
    all_to_all x1, starting transfers between devices, per_device(): m = lax.all_to_all(entries, 'seq', 0, 0, tiled=True)  5.46 us
    pallas_call x1, Pallas kernels, final_call(): pl.pallas_call(final_kernel, in_specs=[pl.BlockSpec(memory_space=pltpu.VM...  4.58 us
    pallas_call x1, Pallas kernels, state_call(): pl.pallas_call(state_kernel, in_specs=[pl.BlockSpec(memory_space=pltpu.HB...  3.6 us
  transfers between devices with their start and end apart: 2, of which 2 were waited for; matrix products, arithmetic and copies ran while one was open for 0% of the time, Pallas kernels for 7%

profile of v8, /device:TPU:32, one launch (start us, length us, event | category | flops | bytes accessed | tf_op | source)
XLA Modules:
  0.0 97.0 jit_solution(3393682453752556961)
XLA Ops:
  0.0 3.6 %span_states.1 = bf16[32,144,128]{2,1,0:T(8,128)(2,1)} custom-call(bf16[256,2048]{1,0:T(8,128)(2,1)} %x_hbm.1, f32[32,256]{1,0:T(8,128)} %rf_hbm.1, f32[32,256]{1,0:T(8,128)} %rb_hbm.1, bf16[256,128]{1,0:T(8,128)(2,1)} %bf_hbm.1, bf16[256,128]{1,0:T(8,128)(2,1)} %bb_hbm.1), custom_call_target="tpu_custom_call" | custom-call | tf_op jit(solution)/shard_map/span_states/pallas_call | solution.py:140
  3.6 11.4 %all-to-all-start = ((bf16[32,144,128]{2,1,0:T(8,128)(2,1)}), bf16[32,144,128]{2,1,0:T(8,128)(2,1)S(1)}, u32[]{:S(2)}, u32[]{:S(2)}) async-start(bf16[32,144,128]{2,1,0:T(8,128)(2,1)} %span_states.1), calls=%async_computation | async-start | bytes 2359296 | tf_op jit(solution)/shard_map/all_to_all | solution.py:349
  15.0 31.2 %all-to-all-done.parts_ref = bf16[32,144,128]{2,1,0:T(8,128)(2,1)S(1)} async-done(((bf16[32,144,128]{2,1,0:T(8,128)(2,1)}), bf16[32,144,128]{2,1,0:T(8,128)(2,1)S(1)}, u32[]{:S(2)}, u32[]{:S(2)}) %all-to-all-start) | async-done | bytes 1179680 | tf_op jit(solution)/shard_map/all_to_all | solution.py:349
  46.2 0.4 group_totals.1
  46.6 10.6 %all_to_all.15.totals_ref = bf16[8,80,128]{2,1,0:T(8,128)(2,1)S(1)} all-to-all(bf16[8,80,128]{2,1,0:T(8,128)(2,1)S(1)} %group_totals.1), channel_id=1, replica_groups=mesh['grp'=8,'seq'=32] {'grp'}, dimensions={0} | all-to-all | bytes 327680 | tf_op jit(solution)/shard_map/all_to_all | solution.py:358
  57.2 1.3 %entry_states.1 = bf16[32,128,128]{2,1,0:T(8,128)(2,1)} custom-call(s32[1]{0:T(128)} %bitcast.group_ref, bf16[8,80,128]{2,1,0:T(8,128)(2,1)S(1)} %all_to_all.15.totals_ref, bf16[32,144,128]{2,1,0:T(8,128)(2,1)S(1)} %all-to-all-done.parts_ref), custom_call_target="tpu_custom_call" | custom-call | tf_op jit(solution)/shard_map/entry_states/pallas_call | solution.py:359
  58.5 0.0 copy-start.1
  58.5 0.0 copy-start.2
  58.5 0.0 copy-start.3
  58.6 0.0 copy-start.4
  58.6 0.0 copy-start.5
  58.6 0.0 copy-start.6
  58.6 5.5 %all-to-all-start.2 = ((bf16[32,128,128]{2,1,0:T(8,128)(2,1)}), bf16[32,128,128]{2,1,0:T(8,128)(2,1)S(1)}, u32[]{:S(2)}, u32[]{:S(2)}) async-start(bf16[32,128,128]{2,1,0:T(8,128)(2,1)} %entry_states.1), calls=%async_computation.2 | async-start | bytes 2097152 | tf_op jit(solution)/shard_map/all_to_all | solution.py:371
  64.1 0.0 copy-done.1
  64.1 0.0 copy-done.2
  64.1 0.0 copy-done.3
  64.1 0.0 copy-done.4
  64.1 0.0 copy-done.5
  64.1 0.0 copy-done.6
  64.1 0.0 copy-start
  64.1 1.2 %copy-done = bf16[256,2048]{1,0:T(8,128)(2,1)S(1)} copy-done((bf16[256,2048]{1,0:T(8,128)(2,1)S(1)}, bf16[256,2048]{1,0:T(8,128)(2,1)}, u32[]{:S(2)}) %copy-start) | copy-done | bytes 1048600
  65.4 0.0 copy-start.8
  65.4 1.2 %copy-done.8 = bf16[256,2048]{1,0:T(8,128)(2,1)S(1)} copy-done((bf16[256,2048]{1,0:T(8,128)(2,1)S(1)}, bf16[256,2048]{1,0:T(8,128)(2,1)}, u32[]{:S(2)}) %copy-start.8) | copy-done | bytes 1048600
  66.6 0.0 copy-start.7
  66.6 6.5 %inside_spans.1 = (bf16[256,2048]{1,0:T(8,128)(2,1)S(1)}, bf16[256,2048]{1,0:T(8,128)(2,1)S(1)}, bf16[256,128]{1,0:T(8,128)(2,1)S(1)}) custom-call(bf16[256,2048]{1,0:T(8,128)(2,1)S(1)} %copy-done, bf16[256,2048]{1,0:T(8,128)(2,1)S(1)} %copy-done.8, f32[32,256]{1,0:T(8,128)S(1)} %copy-done.5, f32[32,256]{1,0:T(8,128)S(1)} %copy-done.6, ...), custom_call_target="tpu_custom_call" | custom-call | flops 536870912 | bytes 4194304 | tf_op jit(solution)/shard_map/inside_spans/pallas_call | solution.py:206
  73.1 19.3 %all-to-all-done.2.m_ref = bf16[32,128,128]{2,1,0:T(8,128)(2,1)S(1)} async-done(((bf16[32,128,128]{2,1,0:T(8,128)(2,1)}), bf16[32,128,128]{2,1,0:T(8,128)(2,1)S(1)}, u32[]{:S(2)}, u32[]{:S(2)}) %all-to-all-start.2) | async-done | bytes 1048608 | tf_op jit(solution)/shard_map/all_to_all | solution.py:371
  92.4 0.0 copy-done.7
  92.4 4.6 %gate_norm_project.1 = bf16[256,1024]{1,0:T(8,128)(2,1)} custom-call(bf16[256,2048]{1,0:T(8,128)(2,1)S(1)} %get-tuple-element.8.in_ref, bf16[256,2048]{1,0:T(8,128)(2,1)S(1)} %get-tuple-element.9.silu_ref, bf16[256,128]{1,0:T(8,128)(2,1)S(1)} %get-tuple-element.10.scale_ref, bf16[32,128,128]{2,1,0:T(8,128)(2,1)S(1)} %all-to-all-done.2.m_ref, ...), custom_call_target="tpu_custom_call" | custom-call | tf_op jit(solution)/shard_map/gate_norm_project/pallas_call | solution.py:326
Async XLA Ops:
  3.6 42.6 %all-to-all-start = ((bf16[32,144,128]{2,1,0:T(8,128)(2,1)}), bf16[32,144,128]{2,1,0:T(8,128)(2,1)S(1)}, u32[]{:S(2)}, u32[]{:S(2)}) async-start(bf16[32,144,128]{2,1,0:T(8,128)(2,1)} %span_states.1), calls=%async_computation | async-start | bytes 2359296 | tf_op jit(solution)/shard_map/all_to_all | solution.py:349
  58.5 5.5 %copy-start.1 = (bf16[256,128]{1,0:T(8,128)(2,1)S(1)}, bf16[256,128]{1,0:T(8,128)(2,1)}, u32[]{:S(2)}) copy-start(bf16[256,128]{1,0:T(8,128)(2,1)} %cf_ref.3) | copy-start | bytes 196612
  58.5 5.5 %copy-start.2 = (bf16[256,128]{1,0:T(8,128)(2,1)S(1)}, bf16[256,128]{1,0:T(8,128)(2,1)}, u32[]{:S(2)}) copy-start(bf16[256,128]{1,0:T(8,128)(2,1)} %cb_ref.3) | copy-start | bytes 196612
  58.5 5.5 %copy-start.3 = (bf16[256,128]{1,0:T(8,128)(2,1)S(1)}, bf16[256,128]{1,0:T(8,128)(2,1)}, u32[]{:S(2)}) copy-start(bf16[256,128]{1,0:T(8,128)(2,1)} %bf_hbm.1) | copy-start | bytes 196612
  58.6 5.5 %copy-start.4 = (bf16[256,128]{1,0:T(8,128)(2,1)S(1)}, bf16[256,128]{1,0:T(8,128)(2,1)}, u32[]{:S(2)}) copy-start(bf16[256,128]{1,0:T(8,128)(2,1)} %bb_hbm.1) | copy-start | bytes 196612
  58.6 5.5 %copy-start.5 = (f32[32,256]{1,0:T(8,128)S(1)}, f32[32,256]{1,0:T(8,128)}, u32[]{:S(2)}) copy-start(f32[32,256]{1,0:T(8,128)} %rf_hbm.1) | copy-start | bytes 98308
  58.6 5.5 %copy-start.6 = (f32[32,256]{1,0:T(8,128)S(1)}, f32[32,256]{1,0:T(8,128)}, u32[]{:S(2)}) copy-start(f32[32,256]{1,0:T(8,128)} %rb_hbm.1) | copy-start | bytes 98308
  58.6 33.8 %all-to-all-start.2 = ((bf16[32,128,128]{2,1,0:T(8,128)(2,1)}), bf16[32,128,128]{2,1,0:T(8,128)(2,1)S(1)}, u32[]{:S(2)}, u32[]{:S(2)}) async-start(bf16[32,128,128]{2,1,0:T(8,128)(2,1)} %entry_states.1), calls=%async_computation.2 | async-start | bytes 2097152 | tf_op jit(solution)/shard_map/all_to_all | solution.py:371
  64.1 1.2 %copy-start = (bf16[256,2048]{1,0:T(8,128)(2,1)S(1)}, bf16[256,2048]{1,0:T(8,128)(2,1)}, u32[]{:S(2)}) copy-start(bf16[256,2048]{1,0:T(8,128)(2,1)} %x_hbm.1) | copy-start | bytes 3145732
  65.4 1.2 %copy-start.8 = (bf16[256,2048]{1,0:T(8,128)(2,1)S(1)}, bf16[256,2048]{1,0:T(8,128)(2,1)}, u32[]{:S(2)}) copy-start(bf16[256,2048]{1,0:T(8,128)(2,1)} %gate_ref.1) | copy-start | bytes 3145732
  66.6 25.8 %copy-start.7 = (f32[2048]{0:T(1024)S(1)}, f32[2048]{0:T(1024)}, u32[]{:S(2)}) copy-start(f32[2048]{0:T(1024)} %param.18) | copy-start | bytes 24580
